TPU v7x, 32 devices: a whole 2x2x4 slice. The times are simulated.
32 devices in a mesh: path: 2 (over core), lon: 8 (over z, x), lat: 2 (over y).
Axes of the slice: x: 2, y: 2, z: 4, core: 2. Of those that a mesh axis runs over, the one named last changes fastest.
Arguments:
- observed: bfloat16 [128, 32, 384], P('lon', 'lat'), may hold values from -6 to 6
- baseline: bfloat16 [128, 32, 384], P('lon', 'lat'), may hold values from -6 to 6
- cotangent: bfloat16 [128, 32, 384], P('lon', 'lat'), may hold values from -6 to 6
- first_weight: bfloat16 [9, 384, 384], P(None, 'path'), may hold values from -0.109375 to 0.109375
- first_bias: float32 [384], replicated, may hold values from -3 to 3
- second_weight: bfloat16 [9, 384, 384], P(None, 'path'), may hold values from -0.109375 to 0.109375
- second_bias: float32 [384], replicated, may hold values from -3 to 3
Outputs:
- attribution: bfloat16 [128, 32, 384], P(('lon', 'path'), 'lat')
All inputs are finite; a program needn't handle non-finite values.
Results may differ from a plain program's by a relative error of at most 0.0038.
Values may be sent and summed in bfloat16 or wider, within the bound.
No kernel may reach another device: no remote copies, remote signals or barrier semaphores. Data moves between devices by JAX's collectives and lax.ppermute only.
A program may use at most 64 MiB of HBM per device.

v0:
```python
import jax
import jax.numpy as jnp
from jax import lax
from jax.sharding import PartitionSpec as P

NEAR = 4
FAR = 16


def padded_2(cells, sides, width):
    for axis, dim in sides:
        count = lax.axis_size(axis)
        ends = count - 1
        head = lax.slice_in_dim(cells, 0, width, axis=dim)
        tail = lax.slice_in_dim(cells, cells.shape[dim] - width, cells.shape[dim], axis=dim)
        cells = jnp.concatenate(
            [
                lax.ppermute(tail, axis, [(i, (i + 1) % count) for i in range(ends)]),
                cells,
                lax.ppermute(head, axis, [((i + 1) % count, i) for i in range(ends)]),
            ],
            axis=dim,
        )
    return cells


def smooth_act(value):
    return jax.nn.gelu(value, approximate=True)


def act_adjoint(pre_value, upstream):
    unused, pullback = jax.vjp(smooth_act, pre_value)
    return pullback(upstream)[0]


def stencil(padded, weights, dilation, rows, cols, forward):
    accumulated = jnp.zeros((rows, cols, weights.shape[1]), jnp.float32)
    for offset_row in (-1, 0, 1):
        for offset_col in (-1, 0, 1):
            tap_index = (offset_row + 1) * 3 + offset_col + 1
            sign = 1 if forward else -1
            start_row = dilation + sign * offset_row * dilation
            start_col = dilation + sign * offset_col * dilation
            window = padded[start_row : start_row + rows, start_col : start_col + cols, :]
            if forward:
                accumulated = accumulated + jnp.dot(
                    window, weights[tap_index], preferred_element_type=jnp.float32
                )
            else:
                accumulated = accumulated + lax.dot_general(
                    window,
                    weights[tap_index],
                    (((2,), (1,)), ((), ())),
                    preferred_element_type=jnp.float32,
                )
    return accumulated


def shards(observed, baseline, cotangent, first_weight, first_bias, second_weight, second_bias):
    rows, cols = (observed.shape[0], observed.shape[1])
    first_full, second_full = (
        lax.all_gather(first_weight, "path", axis=1, tiled=True),
        lax.all_gather(second_weight, "path", axis=1, tiled=True),
    )
    diff = observed.astype(jnp.float32) - baseline.astype(jnp.float32)
    upstream = cotangent.astype(jnp.float32)
    points = lax.axis_size("path")
    mix_weight = (lax.axis_index("path").astype(jnp.float32) + 0.5) / points
    point_field = (baseline.astype(jnp.float32) + mix_weight * diff).astype(jnp.bfloat16)
    point_padded = padded_2(point_field, (("lon", 0), ("lat", 1)), NEAR)
    first_pre = stencil(point_padded, first_full, NEAR, rows, cols, True) + first_bias
    hidden = (point_field.astype(jnp.float32) + smooth_act(first_pre)).astype(jnp.bfloat16)
    hidden_padded = padded_2(hidden, (("lon", 0), ("lat", 1)), FAR)
    second_pre = stencil(hidden_padded, second_full, FAR, rows, cols, True) + second_bias
    second_adj = act_adjoint(second_pre, upstream).astype(jnp.bfloat16)
    second_padded = padded_2(second_adj, (("lon", 0), ("lat", 1)), FAR)
    hidden_adj = upstream + stencil(second_padded, second_full, FAR, rows, cols, False)
    first_adj = act_adjoint(first_pre, hidden_adj).astype(jnp.bfloat16)
    first_padded = padded_2(first_adj, (("lon", 0), ("lat", 1)), NEAR)
    point_grad = hidden_adj + stencil(first_padded, first_full, NEAR, rows, cols, False)
    half_rows = rows // points
    row_start = lax.axis_index("path") * half_rows
    diff_rows = lax.dynamic_slice_in_dim(diff, row_start, half_rows, 0)
    grad_rows = lax.psum_scatter(point_grad, "path", scatter_dimension=0, tiled=True)
    return (diff_rows * grad_rows / points).astype(jnp.bfloat16)


def solution(mesh):
    placed = (
        P("lon", "lat", None),
        P("lon", "lat", None),
        P("lon", "lat", None),
        P(None, "path", None),
        P(),
        P(None, "path", None),
        P(),
    )
    return jax.shard_map(
        shards,
        mesh=mesh,
        in_specs=placed,
        out_specs=P(("lon", "path"), "lat", None),
        check_vma=False,
    )
```

profile of v0, /device:TPU:0, one launch (start us, length us, event | category | flops | bytes accessed | tf_op | source)
XLA Modules:
  0.0 137.8 jit_solution(867327399766113813)
XLA Ops:
  7.3 1.8 %convert_subtract_fusion = (f32[16,16,384]{2,1,0:T(8,128)}, bf16[16,16,384]{2,1,0:T(8,128)(2,1)S(1)}) fusion(bf16[16,16,384]{2,1,0:T(8,128)(2,1)} %param.8, bf16[16,16,384]{2,1,0:T(8,128)(2,1)} %param.7, f32[]{:T(128)S(6)} %div.9), kind=kLoop, calls=%fused_computation.45 | loop fusion | flops 589824 | bytes 983044 | tf_op jit(solution)/shard_map/sub | solution.py:65
  9.2 4.8 %collective-permute-start = (bf16[4,16,384]{2,1,0:T(8,128)(2,1)S(1)}, bf16[4,16,384]{2,1,0:T(8,128)(2,1)S(1)}, u32[]{:S(2)}, u32[]{:S(2)}) collective-permute-start(bf16[4,16,384]{2,1,0:T(8,128)(2,1)S(1)} %get-tuple-element.17), channel_id=1, source_target_pairs={{0,2},{2,4},{4,6},{6,8},{8,10},{10,12},{12,14},{1,3},{3,5},{5,7},{... | collective-permute-start | bytes 147464 | tf_op jit(solution)/shard_map/ppermute | solution.py:18
  14.0 1.3 collective-permute-start.1
  15.7 4.3 %collective-permute-done.1 = bf16[4,16,384]{2,1,0:T(8,128)(2,1)S(1)} collective-permute-done((bf16[4,16,384]{2,1,0:T(8,128)(2,1)S(1)}, bf16[4,16,384]{2,1,0:T(8,128)(2,1)S(1)}, u32[]{:S(2)}, u32[]{:S(2)}) %collective-permute-start.1) | collective-permute-done | bytes 49184 | tf_op jit(solution)/shard_map/ppermute | solution.py:20
  20.1 3.4 %collective-permute-start.2 = (bf16[24,4,384]{2,1,0:T(4,128)(2,1)S(1)}, bf16[24,4,384]{2,1,0:T(4,128)(2,1)S(1)}, u32[]{:S(2)}, u32[]{:S(2)}) collective-permute-start(bf16[24,4,384]{2,1,0:T(4,128)(2,1)S(1)} %get-tuple-element.13), channel_id=1, source_target_pairs={{0,1},{2,3},{4,5},{6,7},{8,9},{10,11},{12,13},{14,15},{16,17},{18,... | collective-permute-start | bytes 221192 | tf_op jit(solution)/shard_map/ppermute | solution.py:18
  25.5 4.3 %collective-permute-done.3 = bf16[24,4,384]{2,1,0:T(4,128)(2,1)S(1)} collective-permute-done((bf16[24,4,384]{2,1,0:T(4,128)(2,1)S(1)}, bf16[24,4,384]{2,1,0:T(4,128)(2,1)S(1)}, u32[]{:S(2)}, u32[]{:S(2)}) %collective-permute-start.3) | collective-permute-done | bytes 73760 | tf_op jit(solution)/shard_map/ppermute | solution.py:20
  30.7 1.4 fusion.47
  36.5 4.4 %collective-permute-start.4 = (bf16[16,16,384]{2,1,0:T(8,128)(2,1)S(1)}, bf16[16,16,384]{2,1,0:T(8,128)(2,1)S(1)}, u32[]{:S(2)}, u32[]{:S(2)}) collective-permute-start(bf16[16,16,384]{2,1,0:T(8,128)(2,1)S(1)} %get-tuple-element.19), channel_id=1, source_target_pairs={{0,2},{2,4},{4,6},{6,8},{8,10},{10,12},{12,14},{1,3},{3,5},{5,7},{... | collective-permute-start | bytes 589832 | tf_op jit(solution)/shard_map/ppermute | solution.py:18
  42.2 3.0 %collective-permute-done.4 = bf16[16,16,384]{2,1,0:T(8,128)(2,1)S(1)} collective-permute-done((bf16[16,16,384]{2,1,0:T(8,128)(2,1)S(1)}, bf16[16,16,384]{2,1,0:T(8,128)(2,1)S(1)}, u32[]{:S(2)}, u32[]{:S(2)}) %collective-permute-start.4) | collective-permute-done | bytes 196640 | tf_op jit(solution)/shard_map/ppermute | solution.py:18
  45.3 3.3 %collective-permute-done.5 = bf16[16,16,384]{2,1,0:T(8,128)(2,1)} collective-permute-done((bf16[16,16,384]{2,1,0:T(8,128)(2,1)S(1)}, bf16[16,16,384]{2,1,0:T(8,128)(2,1)}, u32[]{:S(2)}, u32[]{:S(2)}) %collective-permute-start.5) | collective-permute-done | bytes 196640 | tf_op jit(solution)/shard_map/ppermute | solution.py:20
  48.6 1.8 %pad_maximum_fusion = bf16[48,16,384]{2,1,0:T(8,128)(2,1)} fusion(bf16[16,16,384]{2,1,0:T(8,128)(2,1)} %collective-permute-done.5, bf16[16,16,384]{2,1,0:T(8,128)(2,1)S(1)} %get-tuple-element.19, bf16[16,16,384]{2,1,0:T(8,128)(2,1)S(1)} %collective-permute-done.4), kind=kLoop, calls=%fused_computation.38 | loop fusion | flops 589824 | bytes 1179648 | tf_op jit(solution)/shard_map/concatenate | solution.py:16
  50.4 2.4 %collective-permute-start.6 = (bf16[48,16,384]{2,1,0:T(8,128)(2,1)}, bf16[48,16,384]{2,1,0:T(8,128)(2,1)}, u32[]{:S(2)}, u32[]{:S(2)}) collective-permute-start(bf16[48,16,384]{2,1,0:T(8,128)(2,1)} %pad_maximum_fusion), channel_id=1, source_target_pairs={{0,1},{2,3},{4,5},{6,7},{8,9},{10,11},{12,13},{14,15},{16,17},{18,... | collective-permute-start | bytes 1769480 | tf_op jit(solution)/shard_map/ppermute | solution.py:18
  52.8 1.4 fusion.67
  54.2 1.3 collective-permute-start.7
  56.7 1.3 fusion.71
  58.0 2.8 %collective-permute-done.6 = bf16[48,16,384]{2,1,0:T(8,128)(2,1)} collective-permute-done((bf16[48,16,384]{2,1,0:T(8,128)(2,1)}, bf16[48,16,384]{2,1,0:T(8,128)(2,1)}, u32[]{:S(2)}, u32[]{:S(2)}) %collective-permute-start.6) | collective-permute-done | bytes 589856 | tf_op jit(solution)/shard_map/ppermute | solution.py:18
  60.8 1.3 fusion.65
  63.4 3.6 %collective-permute-done.7 = bf16[48,16,384]{2,1,0:T(8,128)(2,1)S(1)} collective-permute-done((bf16[48,16,384]{2,1,0:T(8,128)(2,1)}, bf16[48,16,384]{2,1,0:T(8,128)(2,1)S(1)}, u32[]{:S(2)}, u32[]{:S(2)}) %collective-permute-start.7) | collective-permute-done | bytes 589856 | tf_op jit(solution)/shard_map/ppermute | solution.py:20
  69.4 3.5 %collective-permute-start.8 = (bf16[16,16,384]{2,1,0:T(8,128)(2,1)S(1)}, bf16[16,16,384]{2,1,0:T(8,128)(2,1)S(1)}, u32[]{:S(2)}, u32[]{:S(2)}) collective-permute-start(bf16[16,16,384]{2,1,0:T(8,128)(2,1)S(1)} %fusion.42), channel_id=1, source_target_pairs={{0,2},{2,4},{4,6},{6,8},{8,10},{10,12},{12,14},{1,3},{3,5},{5,7},{... | collective-permute-start | bytes 589832 | tf_op jit(solution)/shard_map/ppermute | solution.py:18
  74.2 1.9 %collective-permute-done.8 = bf16[16,16,384]{2,1,0:T(8,128)(2,1)S(1)} collective-permute-done((bf16[16,16,384]{2,1,0:T(8,128)(2,1)S(1)}, bf16[16,16,384]{2,1,0:T(8,128)(2,1)S(1)}, u32[]{:S(2)}, u32[]{:S(2)}) %collective-permute-start.8) | collective-permute-done | bytes 196640 | tf_op jit(solution)/shard_map/ppermute | solution.py:18
  76.1 6.4 %collective-permute-done.9 = bf16[16,16,384]{2,1,0:T(8,128)(2,1)S(1)} collective-permute-done((bf16[16,16,384]{2,1,0:T(8,128)(2,1)S(1)}, bf16[16,16,384]{2,1,0:T(8,128)(2,1)S(1)}, u32[]{:S(2)}, u32[]{:S(2)}) %collective-permute-start.9) | collective-permute-done | bytes 196640 | tf_op jit(solution)/shard_map/ppermute | solution.py:20
  82.5 1.3 collective-permute-start.10
  84.1 4.6 %collective-permute-start.11 = (bf16[48,16,384]{2,1,0:T(8,128)(2,1)S(1)}, bf16[48,16,384]{2,1,0:T(8,128)(2,1)S(1)}, u32[]{:S(2)}, u32[]{:S(2)}) collective-permute-start(bf16[48,16,384]{2,1,0:T(8,128)(2,1)S(1)} %pad_maximum_fusion.1), channel_id=1, source_target_pairs={{0,1},{2,3},{4,5},{6,7},{8,9},{10,11},{12,13},{14,15},{16,17},{18,... | collective-permute-start | bytes 1769480 | tf_op jit(solution)/shard_map/ppermute | solution.py:18
  89.3 6.1 %collective-permute-done.10 = bf16[48,16,384]{2,1,0:T(8,128)(2,1)S(1)} collective-permute-done((bf16[48,16,384]{2,1,0:T(8,128)(2,1)S(1)}, bf16[48,16,384]{2,1,0:T(8,128)(2,1)S(1)}, u32[]{:S(2)}, u32[]{:S(2)}) %collective-permute-start.10) | collective-permute-done | bytes 589856 | tf_op jit(solution)/shard_map/ppermute | solution.py:20
  98.4 1.3 collective-permute-start.13
  99.7 5.2 %collective-permute-start.12 = (bf16[4,16,384]{2,1,0:T(8,128)(2,1)S(1)}, bf16[4,16,384]{2,1,0:T(8,128)(2,1)S(1)}, u32[]{:S(2)}, u32[]{:S(2)}) collective-permute-start(bf16[4,16,384]{2,1,0:T(8,128)(2,1)S(1)} %get-tuple-element.15), channel_id=1, source_target_pairs={{0,2},{2,4},{4,6},{6,8},{8,10},{10,12},{12,14},{1,3},{3,5},{5,7},{... | collective-permute-start | bytes 147464 | tf_op jit(solution)/shard_map/ppermute | solution.py:18
  105.2 1.4 %collective-permute-done.12 = bf16[4,16,384]{2,1,0:T(8,128)(2,1)S(1)} collective-permute-done((bf16[4,16,384]{2,1,0:T(8,128)(2,1)S(1)}, bf16[4,16,384]{2,1,0:T(8,128)(2,1)S(1)}, u32[]{:S(2)}, u32[]{:S(2)}) %collective-permute-start.12) | collective-permute-done | bytes 49184 | tf_op jit(solution)/shard_map/ppermute | solution.py:18
  106.7 1.3 collective-permute-start.14
  108.0 4.5 %collective-permute-start.15 = (bf16[24,4,384]{2,1,0:T(4,128)(2,1)S(1)}, bf16[24,4,384]{2,1,0:T(4,128)(2,1)S(1)}, u32[]{:S(2)}, u32[]{:S(2)}) collective-permute-start(bf16[24,4,384]{2,1,0:T(4,128)(2,1)S(1)} %get-tuple-element.10), channel_id=1, source_target_pairs={{0,1},{2,3},{4,5},{6,7},{8,9},{10,11},{12,13},{14,15},{16,17},{18,... | collective-permute-start | bytes 221192 | tf_op jit(solution)/shard_map/ppermute | solution.py:18
  113.1 1.4 collective-permute-done.15
  117.4 12.3 %reduce-scatter.2.cloned.1.call-done = f32[8,16,384]{2,1,0:T(8,128)} async-done(((f32[16,16,384]{2,1,0:T(8,128)}), f32[8,16,384]{2,1,0:T(8,128)}) %reduce-scatter.2.cloned.1.call-update) | async-done | bytes 196624 | tf_op jit(solution)/shard_map/reduce_scatter | solution.py:84
  129.6 1.6 %multiply_convert_fusion = bf16[8,16,384]{2,1,0:T(8,128)(2,1)} fusion(f32[8,16,384]{2,1,0:T(8,128)} %reduce-scatter.2.cloned.1.call-done, f32[16,16,384]{2,1,0:T(8,128)S(1)} %copy-done.3, s32[]{:T(128)S(6)} %select_n.3), kind=kLoop, calls=%fused_computation.139 | loop fusion | flops 147456 | bytes 491524 | tf_op jit(solution)/shard_map/convert_element_type | solution.py:85
  (69 shorter events, 23.5 us)
Async XLA Ops:
  6.5 24.2 %all-gather.3.cloned.1.call-start = ((), (), s32[]{:S(2)}) async-start(), calls=%async_computation.1 | async-start | bytes 3981312 | tf_op jit(solution)/shard_map/all_gather | solution.py:62
  7.3 45.5 %all-gather.5.cloned.1.call-start = ((), (), s32[]{:S(2)}) async-start(), calls=%async_computation.2 | async-start | bytes 3981312 | tf_op jit(solution)/shard_map/all_gather | solution.py:63
  9.2 6.6 %collective-permute-start = (bf16[4,16,384]{2,1,0:T(8,128)(2,1)S(1)}, bf16[4,16,384]{2,1,0:T(8,128)(2,1)S(1)}, u32[]{:S(2)}, u32[]{:S(2)}) collective-permute-start(bf16[4,16,384]{2,1,0:T(8,128)(2,1)S(1)} %get-tuple-element.17), channel_id=1, source_target_pairs={{0,2},{2,4},{4,6},{6,8},{8,10},{10,12},{12,14},{1,3},{3,5},{5,7},{... | collective-permute-start | bytes 147464 | tf_op jit(solution)/shard_map/ppermute | solution.py:18
  14.0 6.0 %collective-permute-start.1 = (bf16[4,16,384]{2,1,0:T(8,128)(2,1)S(1)}, bf16[4,16,384]{2,1,0:T(8,128)(2,1)S(1)}, u32[]{:S(2)}, u32[]{:S(2)}) collective-permute-start(bf16[4,16,384]{2,1,0:T(8,128)(2,1)S(1)} %get-tuple-element.18), channel_id=1, source_target_pairs={{2,0},{4,2},{6,4},{8,6},{10,8},{12,10},{14,12},{3,1},{5,3},{7,5},{... | collective-permute-start | bytes 147464 | tf_op jit(solution)/shard_map/ppermute | solution.py:20
  20.1 5.4 %collective-permute-start.2 = (bf16[24,4,384]{2,1,0:T(4,128)(2,1)S(1)}, bf16[24,4,384]{2,1,0:T(4,128)(2,1)S(1)}, u32[]{:S(2)}, u32[]{:S(2)}) collective-permute-start(bf16[24,4,384]{2,1,0:T(4,128)(2,1)S(1)} %get-tuple-element.13), channel_id=1, source_target_pairs={{0,1},{2,3},{4,5},{6,7},{8,9},{10,11},{12,13},{14,15},{16,17},{18,... | collective-permute-start | bytes 221192 | tf_op jit(solution)/shard_map/ppermute | solution.py:18
  23.5 6.2 %collective-permute-start.3 = (bf16[24,4,384]{2,1,0:T(4,128)(2,1)S(1)}, bf16[24,4,384]{2,1,0:T(4,128)(2,1)S(1)}, u32[]{:S(2)}, u32[]{:S(2)}) collective-permute-start(bf16[24,4,384]{2,1,0:T(4,128)(2,1)S(1)} %get-tuple-element.14), channel_id=1, source_target_pairs={{1,0},{3,2},{5,4},{7,6},{9,8},{11,10},{13,12},{15,14},{17,16},{19,... | collective-permute-start | bytes 221192 | tf_op jit(solution)/shard_map/ppermute | solution.py:20
  24.8 104.8 %reduce-scatter.2.cloned.1.call-start = ((), (), s32[]{:S(2)}) async-start(), calls=%async_computation.3 | async-start | bytes 589824 | tf_op jit(solution)/shard_map/reduce_scatter | solution.py:84
  30.7 3.9 %copy-start.1 = (bf16[9,384,384]{2,1,0:T(8,128)(2,1)S(1)}, bf16[9,384,384]{2,1,0:T(8,128)(2,1)}, u32[]{:S(2)}) copy-start(bf16[9,384,384]{2,1,0:T(8,128)(2,1)} %all-gather.3.cloned.1.call-done) | copy-start | bytes 7962628
  30.7 4.5 %copy-start.2 = (bf16[24,20,384]{2,1,0:T(8,128)(2,1)S(1)}, bf16[24,20,384]{2,1,0:T(8,128)(2,1)}, u32[]{:S(2)}) copy-start(bf16[24,20,384]{2,1,0:T(8,128)(2,1)} %get-tuple-element.12) | copy-start | bytes 1105924
  34.9 1.2 copy-start.5
  36.5 8.7 %collective-permute-start.4 = (bf16[16,16,384]{2,1,0:T(8,128)(2,1)S(1)}, bf16[16,16,384]{2,1,0:T(8,128)(2,1)S(1)}, u32[]{:S(2)}, u32[]{:S(2)}) collective-permute-start(bf16[16,16,384]{2,1,0:T(8,128)(2,1)S(1)} %get-tuple-element.19), channel_id=1, source_target_pairs={{0,2},{2,4},{4,6},{6,8},{8,10},{10,12},{12,14},{1,3},{3,5},{5,7},{... | collective-permute-start | bytes 589832 | tf_op jit(solution)/shard_map/ppermute | solution.py:18
  40.9 7.7 %collective-permute-start.5 = (bf16[16,16,384]{2,1,0:T(8,128)(2,1)S(1)}, bf16[16,16,384]{2,1,0:T(8,128)(2,1)}, u32[]{:S(2)}, u32[]{:S(2)}) collective-permute-start(bf16[16,16,384]{2,1,0:T(8,128)(2,1)S(1)} %get-tuple-element.19), channel_id=1, source_target_pairs={{2,0},{4,2},{6,4},{8,6},{10,8},{12,10},{14,12},{3,1},{5,3},{7,5},{... | collective-permute-start | bytes 589832 | tf_op jit(solution)/shard_map/ppermute | solution.py:20
  50.4 10.4 %collective-permute-start.6 = (bf16[48,16,384]{2,1,0:T(8,128)(2,1)}, bf16[48,16,384]{2,1,0:T(8,128)(2,1)}, u32[]{:S(2)}, u32[]{:S(2)}) collective-permute-start(bf16[48,16,384]{2,1,0:T(8,128)(2,1)} %pad_maximum_fusion), channel_id=1, source_target_pairs={{0,1},{2,3},{4,5},{6,7},{8,9},{10,11},{12,13},{14,15},{16,17},{18,... | collective-permute-start | bytes 1769480 | tf_op jit(solution)/shard_map/ppermute | solution.py:18
  52.8 9.4 %copy-start = (bf16[9,384,384]{2,1,0:T(8,128)(2,1)S(1)}, bf16[9,384,384]{2,1,0:T(8,128)(2,1)}, u32[]{:S(2)}) copy-start(bf16[9,384,384]{2,1,0:T(8,128)(2,1)} %all-gather.5.cloned.1.call-done) | copy-start | bytes 7962628
  54.2 12.9 %collective-permute-start.7 = (bf16[48,16,384]{2,1,0:T(8,128)(2,1)}, bf16[48,16,384]{2,1,0:T(8,128)(2,1)S(1)}, u32[]{:S(2)}, u32[]{:S(2)}) collective-permute-start(bf16[48,16,384]{2,1,0:T(8,128)(2,1)} %pad_maximum_fusion), channel_id=1, source_target_pairs={{1,0},{3,2},{5,4},{7,6},{9,8},{11,10},{13,12},{15,14},{17,16},{19,... | collective-permute-start | bytes 1769480 | tf_op jit(solution)/shard_map/ppermute | solution.py:20
  62.2 6.6 %copy-start.4 = (bf16[16,16,384]{2,1,0:T(8,128)(2,1)S(1)}, bf16[16,16,384]{2,1,0:T(8,128)(2,1)}, u32[]{:S(2)}) copy-start(bf16[16,16,384]{2,1,0:T(8,128)(2,1)} %param.9) | copy-start | bytes 589828
  62.2 6.6 %copy-start.6 = (f32[384]{0:T(512)S(1)}, f32[384]{0:T(512)}, u32[]{:S(2)}) copy-start(f32[384]{0:T(512)} %param.13) | copy-start | bytes 4612
  69.4 6.7 %collective-permute-start.8 = (bf16[16,16,384]{2,1,0:T(8,128)(2,1)S(1)}, bf16[16,16,384]{2,1,0:T(8,128)(2,1)S(1)}, u32[]{:S(2)}, u32[]{:S(2)}) collective-permute-start(bf16[16,16,384]{2,1,0:T(8,128)(2,1)S(1)} %fusion.42), channel_id=1, source_target_pairs={{0,2},{2,4},{4,6},{6,8},{8,10},{10,12},{12,14},{1,3},{3,5},{5,7},{... | collective-permute-start | bytes 589832 | tf_op jit(solution)/shard_map/ppermute | solution.py:18
  72.9 9.5 %collective-permute-start.9 = (bf16[16,16,384]{2,1,0:T(8,128)(2,1)S(1)}, bf16[16,16,384]{2,1,0:T(8,128)(2,1)S(1)}, u32[]{:S(2)}, u32[]{:S(2)}) collective-permute-start(bf16[16,16,384]{2,1,0:T(8,128)(2,1)S(1)} %fusion.42), channel_id=1, source_target_pairs={{2,0},{4,2},{6,4},{8,6},{10,8},{12,10},{14,12},{3,1},{5,3},{7,5},{... | collective-permute-start | bytes 589832 | tf_op jit(solution)/shard_map/ppermute | solution.py:20
  82.5 12.9 %collective-permute-start.10 = (bf16[48,16,384]{2,1,0:T(8,128)(2,1)S(1)}, bf16[48,16,384]{2,1,0:T(8,128)(2,1)S(1)}, u32[]{:S(2)}, u32[]{:S(2)}) collective-permute-start(bf16[48,16,384]{2,1,0:T(8,128)(2,1)S(1)} %pad_maximum_fusion.1), channel_id=1, source_target_pairs={{1,0},{3,2},{5,4},{7,6},{9,8},{11,10},{13,12},{15,14},{17,16},{19,... | collective-permute-start | bytes 1769480 | tf_op jit(solution)/shard_map/ppermute | solution.py:20
  84.1 12.8 %collective-permute-start.11 = (bf16[48,16,384]{2,1,0:T(8,128)(2,1)S(1)}, bf16[48,16,384]{2,1,0:T(8,128)(2,1)S(1)}, u32[]{:S(2)}, u32[]{:S(2)}) collective-permute-start(bf16[48,16,384]{2,1,0:T(8,128)(2,1)S(1)} %pad_maximum_fusion.1), channel_id=1, source_target_pairs={{0,1},{2,3},{4,5},{6,7},{8,9},{10,11},{12,13},{14,15},{16,17},{18,... | collective-permute-start | bytes 1769480 | tf_op jit(solution)/shard_map/ppermute | solution.py:18
  98.4 6.8 %collective-permute-start.13 = (bf16[4,16,384]{2,1,0:T(8,128)(2,1)S(1)}, bf16[4,16,384]{2,1,0:T(8,128)(2,1)S(1)}, u32[]{:S(2)}, u32[]{:S(2)}) collective-permute-start(bf16[4,16,384]{2,1,0:T(8,128)(2,1)S(1)} %get-tuple-element.16), channel_id=1, source_target_pairs={{2,0},{4,2},{6,4},{8,6},{10,8},{12,10},{14,12},{3,1},{5,3},{7,5},{... | collective-permute-start | bytes 147464 | tf_op jit(solution)/shard_map/ppermute | solution.py:20
  99.7 6.9 %collective-permute-start.12 = (bf16[4,16,384]{2,1,0:T(8,128)(2,1)S(1)}, bf16[4,16,384]{2,1,0:T(8,128)(2,1)S(1)}, u32[]{:S(2)}, u32[]{:S(2)}) collective-permute-start(bf16[4,16,384]{2,1,0:T(8,128)(2,1)S(1)} %get-tuple-element.15), channel_id=1, source_target_pairs={{0,2},{2,4},{4,6},{6,8},{8,10},{10,12},{12,14},{1,3},{3,5},{5,7},{... | collective-permute-start | bytes 147464 | tf_op jit(solution)/shard_map/ppermute | solution.py:18
  106.7 6.4 %collective-permute-start.14 = (bf16[24,4,384]{2,1,0:T(4,128)(2,1)S(1)}, bf16[24,4,384]{2,1,0:T(4,128)(2,1)S(1)}, u32[]{:S(2)}, u32[]{:S(2)}) collective-permute-start(bf16[24,4,384]{2,1,0:T(4,128)(2,1)S(1)} %get-tuple-element.9), channel_id=1, source_target_pairs={{1,0},{3,2},{5,4},{7,6},{9,8},{11,10},{13,12},{15,14},{17,16},{19,... | collective-permute-start | bytes 221192 | tf_op jit(solution)/shard_map/ppermute | solution.py:20
  108.0 6.5 %collective-permute-start.15 = (bf16[24,4,384]{2,1,0:T(4,128)(2,1)S(1)}, bf16[24,4,384]{2,1,0:T(4,128)(2,1)S(1)}, u32[]{:S(2)}, u32[]{:S(2)}) collective-permute-start(bf16[24,4,384]{2,1,0:T(4,128)(2,1)S(1)} %get-tuple-element.10), channel_id=1, source_target_pairs={{0,1},{2,3},{4,5},{6,7},{8,9},{10,11},{12,13},{14,15},{16,17},{18,... | collective-permute-start | bytes 221192 | tf_op jit(solution)/shard_map/ppermute | solution.py:18
  115.9 13.7 %copy-start.3 = (f32[16,16,384]{2,1,0:T(8,128)S(1)}, f32[16,16,384]{2,1,0:T(8,128)}, u32[]{:S(2)}) copy-start(f32[16,16,384]{2,1,0:T(8,128)} %get-tuple-element.5) | copy-start | bytes 1179652
Sparse Core Ops, SparseCore 0:
  8.9 14.0 all-gather.2
  24.9 13.7 all-gather.4
  117.5 12.1 reduce-scatter.1
where the time goes:
time: 138 us
  waiting for transfers between devices  53.4 us (39%)
  starting transfers between devices  43.3 us (31%)
  matrix products  20.8 us (15%)
  between operations  13.6 us (10%)
  other arithmetic  6.68 us (5%)
    ppermute x8, starting transfers between devices, padded_2(): lax.ppermute(tail, axis, [(i, (i + 1) % count) for i in range(ends)])  32.9 us
    ppermute x8, waiting for transfers between devices, padded_2(): lax.ppermute(head, axis, [((i + 1) % count, i) for i in range(ends)])  28 us
    dot_general x18, matrix products, stencil(): jnp.dot(window, weights[tap_index], preferred_element_type=jnp.float32)  14.5 us
    ppermute x8, waiting for transfers between devices, padded_2(): lax.ppermute(tail, axis, [(i, (i + 1) % count) for i in range(ends)])  12.4 us
    reduce_scatter x1, waiting for transfers between devices, shards(): lax.psum_scatter(point_grad, 'path', scatter_dimension=0, tiled=True)  12.3 us
    ppermute x8, starting transfers between devices, padded_2(): lax.ppermute(head, axis, [((i + 1) % count, i) for i in range(ends)])  10.3 us
    dot_general x18, matrix products, stencil(): lax.dot_general(window, weights[tap_index], (((2,), (1,)), ((), ())), pre...  6.26 us
    concatenate x4, other arithmetic, padded_2(): jnp.concatenate([lax.ppermute(tail, axis, [(i, (i + 1) % count) for i in...  3.13 us
  transfers between devices with their start and end apart: 19, of which 15 were waited for; matrix products, arithmetic and copies ran while one was open for 14% of the time, Pallas kernels for 0%

commit v1 on v0

v1 whole, which is shorter than its diff:
```python
import math

import jax
import jax.numpy as jnp
from jax import lax
from jax.sharding import PartitionSpec as P

NEAR = 4
FAR = 16


def smooth_act(value):
    return jax.nn.gelu(value, approximate=True)


def act_adjoint(pre_value, upstream):
    unused, pullback = jax.vjp(smooth_act, pre_value)
    return pullback(upstream)[0]


def group_sizes():
    lat = math.gcd(lax.axis_size("lat"), NEAR * NEAR)
    return NEAR * NEAR // lat, lat


def swap(chunks):
    group_lon, group_lat = group_sizes()
    lon, lat = lax.axis_size("lon"), lax.axis_size("lat")
    if (lon, lat) == (group_lon, group_lat):
        return lax.all_to_all(chunks, ("lon", "lat"), 0, 0, tiled=True)
    chunks = chunks.reshape((group_lon, group_lat) + chunks.shape[1:])
    for axis, dim, size in (("lon", 0, group_lon), ("lat", 1, group_lat)):
        count = lax.axis_size(axis)
        groups = [list(range(i, i + size)) for i in range(0, count, size)]
        chunks = lax.all_to_all(chunks, axis, dim, dim, tiled=True, axis_index_groups=groups)
    return chunks.reshape((group_lon * group_lat,) + chunks.shape[2:])


def to_classes(cells):
    rows, cols, depth = cells.shape
    cells = cells.reshape(rows // NEAR, NEAR, cols // NEAR, NEAR, depth).transpose(1, 3, 0, 2, 4)
    return cells.reshape(NEAR * NEAR, rows // NEAR, cols // NEAR, depth)


def padded(cells, width):
    for axis, dim, step in zip(("lon", "lat"), (0, 1), group_sizes()):
        count = lax.axis_size(axis)
        head = lax.slice_in_dim(cells, 0, width, axis=dim)
        tail = lax.slice_in_dim(cells, cells.shape[dim] - width, cells.shape[dim], axis=dim)
        if count == step:
            before, after = jnp.zeros_like(tail), jnp.zeros_like(head)
        else:
            before = lax.ppermute(tail, axis, [(i, i + step) for i in range(count - step)])
            after = lax.ppermute(head, axis, [(i + step, i) for i in range(count - step)])
        cells = jnp.concatenate([before, cells, after], axis=dim)
    return cells


def stencil(cells, weights, step, forward):
    rows, cols, depth = cells.shape
    around = padded(cells, step)
    total = jnp.zeros((rows, cols, depth), jnp.float32)
    for tap in range(9):
        sign = step if forward else -step
        row, col = step + (tap // 3 - 1) * sign, step + (tap % 3 - 1) * sign
        window = around[row : row + rows, col : col + cols]
        dims = (((2,), (0 if forward else 1,)), ((), ()))
        total = total + lax.dot_general(window, weights[tap], dims, preferred_element_type=jnp.float32)
    return total


def shards(observed, baseline, cotangent, first_weight, first_bias, second_weight, second_bias):
    rows, cols, depth = observed.shape
    points, point = lax.axis_size("path"), lax.axis_index("path")
    group_lon, group_lat = group_sizes()
    row_part, col_part = rows // NEAR, cols // NEAR
    ring = [(i, (i + 1) % points) for i in range(points)]

    def whole_weight(part):
        held = jnp.zeros((part.shape[0], points) + part.shape[1:], part.dtype)
        for step in range(points):
            held = lax.dynamic_update_slice_in_dim(held, part[:, None], (point - step) % points, 1)
            if step < points - 1:
                part = lax.ppermute(part, "path", ring)
        return held.reshape(held.shape[0], -1, held.shape[3])

    first_full, second_full = whole_weight(first_weight), whole_weight(second_weight)
    diff = observed.astype(jnp.float32) - baseline.astype(jnp.float32)
    mix = (point.astype(jnp.float32) + 0.5) / points
    field = (baseline.astype(jnp.float32) + mix * diff).astype(jnp.bfloat16)
    sent = jnp.stack([to_classes(field), to_classes(cotangent)], axis=1)
    got = swap(sent).reshape(group_lon, group_lat, 2, row_part, col_part, depth)
    got = got.transpose(2, 0, 3, 1, 4, 5).reshape(2, group_lon * row_part, group_lat * col_part, depth)
    field, upstream = got[0], got[1].astype(jnp.float32)

    first_pre = stencil(field, first_full, 1, True) + first_bias
    hidden = (field.astype(jnp.float32) + smooth_act(first_pre)).astype(jnp.bfloat16)
    second_pre = stencil(hidden, second_full, FAR // NEAR, True) + second_bias
    second_adj = act_adjoint(second_pre, upstream).astype(jnp.bfloat16)
    hidden_adj = upstream + stencil(second_adj, second_full, FAR // NEAR, False)
    first_adj = act_adjoint(first_pre, hidden_adj).astype(jnp.bfloat16)
    grad = hidden_adj + stencil(first_adj, first_full, 1, False)

    part = row_part // points
    grad = grad.reshape(group_lon, points, part, group_lat, col_part, depth).transpose(1, 0, 3, 2, 4, 5)
    grad = grad.reshape(points, group_lon * group_lat, part, col_part, depth)
    total = lax.dynamic_index_in_dim(grad, point, 0, keepdims=False)
    for step in range(1, points):
        other = lax.dynamic_index_in_dim(grad, (point + step) % points, 0, keepdims=False)
        total = total + lax.ppermute(other, "path", [(i, (i + step) % points) for i in range(points)])
    home = swap(total.astype(jnp.bfloat16)).reshape(NEAR, NEAR, part, col_part, depth)
    home = home.transpose(2, 0, 3, 1, 4).reshape(rows // points, cols, depth).astype(jnp.float32)
    diff_rows = lax.dynamic_slice_in_dim(diff, point * (rows // points), rows // points, 0)
    return (diff_rows * home / points).astype(jnp.bfloat16)


def solution(mesh):
    placed = (
        P("lon", "lat", None),
        P("lon", "lat", None),
        P("lon", "lat", None),
        P(None, "path", None),
        P(),
        P(None, "path", None),
        P(),
    )
    return jax.shard_map(
        shards,
        mesh=mesh,
        in_specs=placed,
        out_specs=P(("lon", "path"), "lat", None),
        check_vma=False,
    )
```

time: 138 us -> 59.5 us (0.43)
  waiting for transfers between devices: 53.4 us -> 19 us
  starting transfers between devices: 43.3 us -> 12.5 us
  between operations: 13.6 us -> 0.61 us
  local copies, waits for them, and re-layouts: 0.06 us -> 11.6 us
  matrix products: 20.8 us -> 11.7 us
  other arithmetic: 6.68 us -> 3.72 us
    ppermute x16 -> x3, starting transfers between devices: 43.2 us -> 0.58 us  [the longest x2 0.51 us: whole_weight(): part = lax.ppermute(part, 'path', ring)]
    ppermute x16 -> x3, waiting for transfers between devices: 40.4 us -> 1.43 us  [the longest x1 1.43 us: shards(): lax.ppermute(other, 'path', [(i, (i + step) % points) for i in range(poin...]
    all_to_all x0 -> x2, waiting for transfers between devices: none -> 17.6 us  [swap(): return lax.all_to_all(chunks, ('lon', 'lat'), 0, 0, tiled=True)]
    reduce_scatter x1 -> x0, waiting for transfers between devices: 12.3 us -> none  [shards(): lax.psum_scatter(point_grad, 'path', scatter_dimension=0, tiled=True)]
    all_to_all x0 -> x2, starting transfers between devices: none -> 11.9 us  [swap(): return lax.all_to_all(chunks, ('lon', 'lat'), 0, 0, tiled=True)]
    dot_general x36, matrix products: 20.8 us -> 11.7 us  [stencil(): lax.dot_general(window, weights[tap], dims, preferred_element_type=jnp.fl...]
    dynamic_update_slice x0 -> x3, local copies, waits for them, and re-layouts: none -> 3.67 us  [whole_weight(): lax.dynamic_update_slice_in_dim(held, part[:, None], (point - step) % poi...]
    concatenate x4, other arithmetic: 3.13 us -> 0.16 us  [padded(): cells = jnp.concatenate([before, cells, after], axis=dim)]
  transfers between devices with their start and end apart: 19 -> 5, of which waited for: 15 -> 3; matrix products, arithmetic and copies ran while one was open for 14% -> 13% of each run, Pallas kernels for 0% -> 0%
where the time goes in v1:
time: 59.5 us; the launch traced here: 59.1 us
  waiting for transfers between devices  19 us (32%)
  starting transfers between devices  12.5 us (21%)
  matrix products  11.7 us (20%)
  local copies, waits for them, and re-layouts  11.6 us (19%)
  other arithmetic  3.72 us (6%)
  between operations  0.61 us (1%)
    all_to_all x2, waiting for transfers between devices, swap(): return lax.all_to_all(chunks, ('lon', 'lat'), 0, 0, tiled=True)  17.6 us
    all_to_all x2, starting transfers between devices, swap(): return lax.all_to_all(chunks, ('lon', 'lat'), 0, 0, tiled=True)  11.9 us
    dot_general x36, matrix products, stencil(): lax.dot_general(window, weights[tap], dims, preferred_element_type=jnp.fl...  11.7 us
    dynamic_update_slice x3, local copies, waits for them, and re-layouts, whole_weight(): lax.dynamic_update_slice_in_dim(held, part[:, None], (point - step) % poi...  3.67 us
    convert_element_type x2, local copies, waits for them, and re-layouts, shards(): field, upstream = (got[0], got[1].astype(jnp.float32))  1.97 us
    unnamed x14, local copies, waits for them, and re-layouts  1.87 us
    sub x1, other arithmetic, shards(): diff = observed.astype(jnp.float32) - baseline.astype(jnp.float32)  1.86 us
    ppermute x1, waiting for transfers between devices, shards(): lax.ppermute(other, 'path', [(i, (i + step) % points) for i in range(poin...  1.43 us
  transfers between devices with their start and end apart: 5, of which 3 were waited for; matrix products, arithmetic and copies ran while one was open for 13% of the time, Pallas kernels for 0%

profile of v1, /device:TPU:0, one launch (start us, length us, event | category | flops | bytes accessed | tf_op | source)
XLA Modules:
  0.0 59.1 jit_solution(8823813503805112703)
XLA Ops:
  0.0 0.5 collective-permute-start
  0.5 1.9 %convert_subtract_fusion = (f32[16,16,384]{2,1,0:T(8,128)}, bf16[16,16,384]{2,1,0:T(8,128)(2,1)S(1)}) fusion(bf16[16,16,384]{2,1,0:T(8,128)(2,1)} %param.8, bf16[16,16,384]{2,1,0:T(8,128)(2,1)} %param.7, f32[]{:T(128)S(6)} %div.9), kind=kLoop, calls=%fused_computation.69 | loop fusion | flops 589824 | bytes 983044 | tf_op jit(solution)/shard_map/sub | solution.py:88
  2.5 1.0 %reshape.69 = bf16[4,4,4,4,384]{4,3,2,1,0:T(4,128)(2,1)S(1)} reshape(bf16[16,16,384]{2,1,0:T(8,128)(2,1)} %param.9) | data formatting | bytes 393216 | tf_op jit(solution)/shard_map/reshape | solution.py:41
  3.9 0.9 %copy.56 = bf16[16,2,4,4,384]{4,3,2,1,0:T(4,128)(2,1)} copy(bf16[16,2,4,4,384]{4,3,2,0,1:T(4,128)(2,1)S(1)} %pad_maximum_fusion) | data formatting | bytes 786432 | tf_op jit(solution)/shard_map/stack | solution.py:91
  4.8 8.3 %all-to-all-start = ((bf16[16,2,4,4,384]{4,3,2,1,0:T(4,128)(2,1)}), bf16[16,2,4,4,384]{4,3,2,1,0:T(4,128)(2,1)S(1)}, u32[]{:S(2)}, u32[]{:S(2)}) async-start(bf16[16,2,4,4,384]{4,3,2,1,0:T(4,128)(2,1)} %copy.56), calls=%async_computation | async-start | bytes 786432 | tf_op jit(solution)/shard_map/all_to_all | solution.py:30
  13.1 0.3 broadcast.68.clone
  13.8 1.5 %copy-done = bf16[9,2,192,384]{3,2,1,0:T(8,128)(2,1)} copy-done((bf16[9,2,192,384]{3,2,1,0:T(8,128)(2,1)}, bf16[9,2,192,384]{3,2,1,0:T(8,128)(2,1)S(1)}, u32[]{:S(2)}) %copy-start) | copy-done | bytes 2654232
  15.3 0.3 broadcast.68.clone.1
  15.9 9.9 %all-to-all-done = bf16[16,2,4,4,384]{4,3,2,1,0:T(4,128)(2,1)S(1)} async-done(((bf16[16,2,4,4,384]{4,3,2,1,0:T(4,128)(2,1)}), bf16[16,2,4,4,384]{4,3,2,1,0:T(4,128)(2,1)S(1)}, u32[]{:S(2)}, u32[]{:S(2)}) %all-to-all-start) | async-done | bytes 393248 | tf_op jit(solution)/shard_map/all_to_all | solution.py:30
  26.3 0.8 %copy.58 = f32[1,8,4,2,4,384]{5,4,3,2,1,0:T(4,128)} copy(f32[1,8,4,2,4,384]{5,1,4,3,2,0:T(8,128)S(1)} %get-tuple-element.26) | data formatting | bytes 786432 | tf_op jit(solution)/shard_map/convert_element_type | solution.py:94
  27.1 1.1 %reshape.73 = f32[32,8,384]{2,1,0:T(8,128)S(1)} reshape(f32[1,8,4,2,4,384]{5,4,3,2,1,0:T(4,128)} %copy.58) | data formatting | bytes 786432 | tf_op jit(solution)/shard_map/convert_element_type | solution.py:94
  28.3 3.1 %bitcast_dynamic-update-slice_fusion = (bf16[9,2,192,384]{3,2,1,0:T(8,128)(2,1)}, bf16[9,2,192,384]{3,2,1,0:T(8,128)(2,1)S(1)}) fusion(bf16[9,2,192,384]{3,2,1,0:T(8,128)(2,1)} %copy-done, s32[]{:T(128)S(6)} %select_n.41, bf16[9,192,384]{2,1,0:T(8,128)(2,1)} %collective-permute-done.1, bf16[9,2,192,384]{3,2,1,0:T(8,128)(2,1)S(1)} %bitcast_dynamic-update-slice_fusion.3, ...), kind=kLoop, calls=%fused_computation | loop fusion | bytes 5308420 | tf_op jit(solution)/shard_map/dynamic_update_slice | solution.py:82
  31.4 0.3 fusion.93
  32.1 0.3 fusion.48
  33.3 0.3 fusion.99
  33.7 0.3 fusion.100
  34.0 0.3 fusion.51
  34.3 0.3 fusion.92
  34.6 0.3 copy-done.5
  35.0 0.5 add_convert_fusion
  35.9 0.3 fusion.59
  36.2 0.3 fusion.57
  36.8 0.3 fusion.60
  37.8 0.3 fusion.61
  38.1 0.6 %fusion.46 = bf16[32,8,384]{2,1,0:T(8,128)(2,1)S(1)} fusion(f32[32,8,384]{2,1,0:T(8,128)S(1)} %reshape.73, f32[32,8,384]{2,1,0:T(8,128)S(1)} %fusion.61, f32[32,8,384]{2,1,0:T(8,128)S(1)} %fusion.102, f32[32,8,384]{2,1,0:T(8,128)S(1)} %fusion.58, f32[32,8,384]{2,1,0:T(8,128)S(1)} %fusion.60, f32[32,8,384]{2,1,0:T(8,128)S(1)} %fusion.96, ...), kind=kOutput, calls=%fused_computation.84 | convolution fusion | flops 78348288 | bytes 4277760 | tf_op jit(solution)/shard_map/dot_general | solution.py:68
  41.1 0.6 fusion.39
  44.1 0.4 fusion.31
  44.9 1.4 %collective-permute-done.2 = f32[16,2,4,384]{3,2,1,0:T(4,128)S(1)} collective-permute-done((f32[16,2,4,384]{3,2,1,0:T(4,128)S(1)}, f32[16,2,4,384]{3,2,1,0:T(4,128)S(1)}, u32[]{:S(2)}, u32[]{:S(2)}) %collective-permute-start.2) | collective-permute-done | bytes 196640 | tf_op jit(solution)/shard_map/ppermute | solution.py:110
  46.3 0.7 %fusion.67 = bf16[16,2,4,384]{3,2,1,0:T(4,128)(2,1)} fusion(f32[16,2,4,384]{3,2,1,0:T(4,128)S(1)} %collective-permute-done.2, f32[2,16,2,4,384]{4,3,2,1,0:T(4,128)S(1)} %bitcast.179, s32[]{:T(128)S(6)} %select_n.42), kind=kLoop, calls=%fused_computation.119 | loop fusion | flops 98304 | bytes 491524 | tf_op jit(solution)/shard_map/convert_element_type | solution.py:111
  47.0 3.6 %all-to-all-start.1 = ((bf16[16,2,4,384]{3,2,1,0:T(4,128)(2,1)}), bf16[16,2,4,384]{3,2,1,0:T(4,128)(2,1)S(1)}, u32[]{:S(2)}, u32[]{:S(2)}) async-start(bf16[16,2,4,384]{3,2,1,0:T(4,128)(2,1)} %fusion.67), calls=%async_computation.1 | async-start | bytes 196608 | tf_op jit(solution)/shard_map/all_to_all | solution.py:30
  50.6 7.7 %all-to-all-done.1 = bf16[16,2,4,384]{3,2,1,0:T(4,128)(2,1)S(1)} async-done(((bf16[16,2,4,384]{3,2,1,0:T(4,128)(2,1)}), bf16[16,2,4,384]{3,2,1,0:T(4,128)(2,1)S(1)}, u32[]{:S(2)}, u32[]{:S(2)}) %all-to-all-start.1) | async-done | bytes 98336 | tf_op jit(solution)/shard_map/all_to_all | solution.py:30
  58.5 0.7 %multiply_convert_fusion = bf16[8,16,384]{2,1,0:T(8,128)(2,1)} fusion(f32[8,16,384]{2,1,0:T(8,128)S(1)} %reshape.74, f32[16,16,384]{2,1,0:T(8,128)S(1)} %copy-done.4, s32[]{:T(128)S(6)} %select_n.37), kind=kLoop, calls=%fused_computation.120 | loop fusion | flops 147456 | bytes 491524 | tf_op jit(solution)/shard_map/convert_element_type | solution.py:114
  (62 shorter events, 9.1 us)
Async XLA Ops:
  0.0 28.3 %collective-permute-start = (bf16[9,192,384]{2,1,0:T(8,128)(2,1)}, bf16[9,192,384]{2,1,0:T(8,128)(2,1)}, u32[]{:S(2)}, u32[]{:S(2)}) collective-permute-start(bf16[9,192,384]{2,1,0:T(8,128)(2,1)} %param.10), channel_id=1, source_target_pairs={{0,16},{16,0},{1,17},{17,1},{2,18},{18,2},{3,19},{19,3},{4,20},{20... | collective-permute-start | bytes 3981320 | tf_op jit(solution)/shard_map/ppermute | solution.py:84
  0.5 27.9 %collective-permute-start.1 = (bf16[9,192,384]{2,1,0:T(8,128)(2,1)}, bf16[9,192,384]{2,1,0:T(8,128)(2,1)}, u32[]{:S(2)}, u32[]{:S(2)}) collective-permute-start(bf16[9,192,384]{2,1,0:T(8,128)(2,1)} %param.12), channel_id=1, source_target_pairs={{0,16},{16,0},{1,17},{17,1},{2,18},{18,2},{3,19},{19,3},{4,20},{20... | collective-permute-start | bytes 3981320 | tf_op jit(solution)/shard_map/ppermute | solution.py:84
  3.5 10.0 %copy-start.3 = (bf16[9,192,384]{2,1,0:T(8,128)(2,1)S(1)}, bf16[9,192,384]{2,1,0:T(8,128)(2,1)}, u32[]{:S(2)}) copy-start(bf16[9,192,384]{2,1,0:T(8,128)(2,1)} %param.12) | copy-start | bytes 3981316
  4.8 21.1 %all-to-all-start = ((bf16[16,2,4,4,384]{4,3,2,1,0:T(4,128)(2,1)}), bf16[16,2,4,4,384]{4,3,2,1,0:T(4,128)(2,1)S(1)}, u32[]{:S(2)}, u32[]{:S(2)}) async-start(bf16[16,2,4,4,384]{4,3,2,1,0:T(4,128)(2,1)} %copy.56), calls=%async_computation | async-start | bytes 786432 | tf_op jit(solution)/shard_map/all_to_all | solution.py:30
  13.5 2.2 %copy-start.2 = (bf16[9,192,384]{2,1,0:T(8,128)(2,1)S(1)}, bf16[9,192,384]{2,1,0:T(8,128)(2,1)}, u32[]{:S(2)}) copy-start(bf16[9,192,384]{2,1,0:T(8,128)(2,1)} %param.10) | copy-start | bytes 3981316
  13.8 1.5 %copy-start = (bf16[9,2,192,384]{3,2,1,0:T(8,128)(2,1)}, bf16[9,2,192,384]{3,2,1,0:T(8,128)(2,1)S(1)}, u32[]{:S(2)}) copy-start(bf16[9,2,192,384]{3,2,1,0:T(8,128)(2,1)S(1)} %bitcast_dynamic-update-slice_fusion.1) | copy-start | bytes 7962628
  32.4 1.9 %copy-start.1 = (bf16[9,2,192,384]{3,2,1,0:T(8,128)(2,1)S(1)}, bf16[9,2,192,384]{3,2,1,0:T(8,128)(2,1)}, u32[]{:S(2)}) copy-start(bf16[9,2,192,384]{3,2,1,0:T(8,128)(2,1)} %get-tuple-element.31) | copy-start | bytes 7962628
  34.3 0.7 %copy-start.5 = (f32[384]{0:T(512)S(1)}, f32[384]{0:T(512)}, u32[]{:S(2)}) copy-start(f32[384]{0:T(512)} %param.11) | copy-start | bytes 4612
  36.2 1.9 %copy-start.6 = (f32[384]{0:T(512)S(1)}, f32[384]{0:T(512)}, u32[]{:S(2)}) copy-start(f32[384]{0:T(512)} %param.13) | copy-start | bytes 4612
  44.6 13.9 %copy-start.4 = (f32[16,16,384]{2,1,0:T(8,128)S(1)}, f32[16,16,384]{2,1,0:T(8,128)}, u32[]{:S(2)}) copy-start(f32[16,16,384]{2,1,0:T(8,128)} %get-tuple-element.23) | copy-start | bytes 1179652
  44.8 1.5 %collective-permute-start.2 = (f32[16,2,4,384]{3,2,1,0:T(4,128)S(1)}, f32[16,2,4,384]{3,2,1,0:T(4,128)S(1)}, u32[]{:S(2)}, u32[]{:S(2)}) collective-permute-start(f32[16,2,4,384]{3,2,1,0:T(4,128)S(1)} %dynamic-slice_bitcast_fusion), channel_id=1, source_target_pairs={{0,16},{16,0},{1,17},{17,1},{2,18},{18,2},{3,19},{19,3},{4,20},{20... | collective-permute-start | bytes 589832 | tf_op jit(solution)/shard_map/ppermute | solution.py:110
  47.0 11.3 %all-to-all-start.1 = ((bf16[16,2,4,384]{3,2,1,0:T(4,128)(2,1)}), bf16[16,2,4,384]{3,2,1,0:T(4,128)(2,1)S(1)}, u32[]{:S(2)}, u32[]{:S(2)}) async-start(bf16[16,2,4,384]{3,2,1,0:T(4,128)(2,1)} %fusion.67), calls=%async_computation.1 | async-start | bytes 196608 | tf_op jit(solution)/shard_map/all_to_all | solution.py:30

commit v2 on v1

--- a/solution.py
+++ b/solution.py
@@ -2,12 +2,19 @@
 
 import jax
 import jax.numpy as jnp
+import numpy as np
 from jax import lax
+from jax.experimental import pallas as pl
+from jax.experimental.pallas import tpu as pltpu
 from jax.sharding import PartitionSpec as P
 
 NEAR = 4
 FAR = 16
-
+EDGE = 8
+LANES = 128
+F32, BF16 = jnp.float32, jnp.bfloat16
+VMEM = pl.BlockSpec(memory_space=pltpu.VMEM)
+ANY = pl.BlockSpec(memory_space=pl.ANY)
 
 def smooth_act(value):
     return jax.nn.gelu(value, approximate=True)
@@ -69,7 +76,257 @@
     return total
 
 
-def shards(observed, baseline, cotangent, first_weight, first_bias, second_weight, second_bias):
+def one_hot(source):
+    return jnp.asarray(np.eye(source.size, dtype=np.float32)[source.reshape(-1)], BF16)
+
+
+def gelu_and_slope(value):
+    scale, cubic = math.sqrt(2 / math.pi), 0.044715
+    square = value * value
+    bent = jnp.tanh(scale * value * (1 + cubic * square))
+    half = 0.5 * (1 + bent)
+    return value * half, half + 0.5 * value * (1 - bent * bent) * (scale * (1 + 3 * cubic * square))
+
+
+def call(kernel, outs, scratch, name, megabytes, *args, specs=None):
+    shapes = [jax.ShapeDtypeStruct(shape, dtype) for shape, dtype in outs]
+    return pl.pallas_call(
+        kernel,
+        out_shape=shapes,
+        in_specs=specs or [VMEM] * len(args),
+        out_specs=[VMEM] * len(outs),
+        scratch_shapes=scratch,
+        compiler_params=pltpu.CompilerParams(vmem_limit_bytes=megabytes << 20),
+        name=name,
+    )(*args)
+
+
+def pack_classes(observed, baseline, cotangent):
+    rows, cols, depth = observed.shape
+    points, point = lax.axis_size("path"), lax.axis_index("path")
+    cells, part = rows * cols, rows * cols // (NEAR * NEAR)
+    index = np.arange(cells).reshape(rows // NEAR, NEAR, cols // NEAR, NEAR).transpose(1, 3, 0, 2)
+    order = one_hot(index)
+
+    def kernel(order, observed, baseline, cotangent, sent, diff_rows, held, sems):
+        copies = [
+            pltpu.make_async_copy(ref, held.at[i], sems.at[i])
+            for i, ref in enumerate((observed, baseline, cotangent))
+        ]
+        for copy in copies:
+            copy.start()
+        for copy in copies:
+            copy.wait()
+        mine = lax.axis_index("path")
+        mix = (mine.astype(F32) + 0.5) / points
+        base = held[1].astype(F32)
+        diff = held[0].astype(F32) - base
+        field = (base + mix * diff).astype(BF16)
+        for i, values in enumerate((field, held[2])):
+            moved = jnp.dot(order[...], values, preferred_element_type=F32)
+            sent[:, i * part : (i + 1) * part, :] = moved.reshape(NEAR * NEAR, part, depth).astype(BF16)
+        half = pl.ds(pl.multiple_of(mine * (cells // points), cells // points), cells // points)
+        own = held[1, half, :].astype(F32)
+        diff_rows[...] = (held[0, half, :].astype(F32) - own) * (1 / points)
+
+    return call(
+        kernel,
+        [((NEAR * NEAR, 2 * part, depth), BF16), ((cells // points, depth), F32)],
+        [pltpu.VMEM((3, cells, depth), BF16), pltpu.SemaphoreType.DMA((3,))],
+        "pack_classes",
+        8,
+        order,
+        *(x.reshape(cells, depth) for x in (observed, baseline, cotangent)),
+        specs=[VMEM, ANY, ANY, ANY],
+    )
+
+
+def join_weights(halves):
+    points = len(halves[0])
+    taps, width, depth = halves[0][0].shape
+    side = math.isqrt(taps)
+
+    def kernel(*refs):
+        parts, wholes, sems = refs[: 2 * points], refs[2 * points : 2 * points + 2], refs[-1]
+        mine = lax.axis_index("path")
+        copies = []
+        for k in range(2 * points):
+            owner = lax.rem(mine + points - k % points, points)
+            span = pl.ds(pl.multiple_of(owner * width, width), width)
+            for col in range(side):
+                copies.append(
+                    pltpu.make_async_copy(
+                        parts[k].at[:, col], wholes[k // points].at[col, :, span, :], sems.at[k, col]
+                    )
+                )
+        for copy in copies:
+            copy.start()
+        for copy in copies:
+            copy.wait()
+
+    shape = (side, side, width * points, depth)
+    args = [x.reshape(side, side, width, depth) for parts in halves for x in parts]
+    return call(
+        kernel,
+        [(shape, BF16)] * 2,
+        [pltpu.SemaphoreType.DMA((2 * points, side))],
+        "join_weights",
+        16,
+        *args,
+        specs=[ANY] * len(args),
+    )
+
+
+def adjoint_of_class(got, first, first_bias, second, second_bias, sizes):
+    group_lon, group_lat, row_part, col_part = sizes
+    points = lax.axis_size("path")
+    depth = got.shape[-1]
+    rows, cols = group_lon * row_part, group_lat * col_part
+    cells, part = rows * cols, row_part * col_part
+    span = row_part // points
+    index = np.arange(cells).reshape(group_lon, group_lat, row_part, col_part).transpose(1, 3, 0, 2)
+    order = one_hot(index)
+
+    def kernel(order, got, first, first_bias, second, second_bias, kept, sent, edged, taps, slope, grad, laned):
+        def spread(values, step):
+            edged[:, EDGE : EDGE + rows, :] = values.reshape(cols, rows, depth)
+            for i in range(3):
+                start = EDGE + (i - 1) * step
+                taps[:, i * depth : (i + 1) * depth] = (
+                    edged[:, start : start + rows, :].reshape(cells, depth).astype(BF16)
+                )
+
+        def both_sides(weigh, step):
+            shift = step * rows
+            fill = jnp.zeros((shift, depth), F32)
+            after = weigh(taps[shift:, :], 2)
+            before = weigh(taps[: cells - shift, :], 0)
+            return (
+                weigh(taps[...], 1)
+                + jnp.concatenate([after, fill], axis=0)
+                + jnp.concatenate([fill, before], axis=0)
+            )
+
+        def forward(weights, step):
+            def weigh(values, col):
+                return jnp.dot(values, weights[col].reshape(3 * depth, depth), preferred_element_type=F32)
+
+            return both_sides(weigh, step)
+
+        def backward(weights, step):
+            def weigh(values, col):
+                total = None
+                for i in range(3):
+                    term = lax.dot_general(
+                        values[:, i * depth : (i + 1) * depth],
+                        weights[2 - col, 2 - i],
+                        (((1,), (1,)), ((), ())),
+                        preferred_element_type=F32,
+                    )
+                    total = term if total is None else total + term
+                return total
+
+            return both_sides(weigh, step)
+
+        edged[:, :EDGE, :] = jnp.zeros((cols, EDGE, depth), F32)
+        edged[:, EDGE + rows :, :] = jnp.zeros((cols, EDGE, depth), F32)
+        field, upstream = (
+            jnp.dot(order[...], got[:, i * part : (i + 1) * part, :].reshape(cells, depth), preferred_element_type=F32)
+            for i in range(2)
+        )
+        spread(field, 1)
+        act, slope[...] = gelu_and_slope(forward(first, 1) + first_bias[...])
+        spread(field + act, FAR // NEAR)
+        second_pre = forward(second, FAR // NEAR) + second_bias[...]
+        spread(gelu_and_slope(second_pre)[1] * upstream, FAR // NEAR)
+        hidden_adj = upstream + backward(second, FAR // NEAR)
+        grad[...] = hidden_adj
+        spread(slope[...] * hidden_adj, 1)
+        grad[...] += backward(first, 1)
+        for b in range(depth // LANES):
+            laned[b] = grad[:, b * LANES : (b + 1) * LANES].reshape(cols, rows, LANES)
+        mine = lax.axis_index("path")
+        for k in range(points):
+            owner = lax.rem(mine + k, points)
+            for i in range(span):
+                target = kept if k == 0 else sent.at[k - 1]
+                place = slice(i * (cells // row_part), (i + 1) * (cells // row_part))
+                for b in range(depth // LANES):
+                    rows_of = laned[b, :, pl.ds(owner * span + i, group_lon, stride=row_part), :]
+                    target[place, b * LANES : (b + 1) * LANES] = rows_of.reshape(-1, LANES)
+
+    share = cells // points
+    return call(
+        kernel,
+        [((share, depth), F32), ((points - 1, share, depth), F32)],
+        [
+            pltpu.VMEM((cols, rows + 2 * EDGE, depth), F32),
+            pltpu.VMEM((cells, 3 * depth), BF16),
+            pltpu.VMEM((cells, depth), F32),
+            pltpu.VMEM((cells, depth), F32),
+            pltpu.VMEM((depth // LANES, cols, rows, LANES), F32),
+        ],
+        "adjoint_of_class",
+        24,
+        order,
+        got,
+        first,
+        first_bias.reshape(1, depth),
+        second,
+        second_bias.reshape(1, depth),
+    )
+
+
+def total_for_homes(kept, others, sizes):
+    group_lon, group_lat, row_part, col_part = sizes
+    share, depth = kept.shape
+    span = row_part // lax.axis_size("path")
+    part = span * col_part
+    index = np.arange(share).reshape(span, group_lat, col_part, group_lon).transpose(3, 1, 0, 2)
+
+    def kernel(order, kept, *refs):
+        others, sent = refs[:-1], refs[-1]
+        total = kept[...]
+        for other in others:
+            total = total + other[...]
+        moved = jnp.dot(order[...], total.astype(BF16), preferred_element_type=F32)
+        sent[...] = moved.reshape(share // part, part, depth).astype(BF16)
+
+    return call(kernel, [((share // part, part, depth), BF16)], [], "total_for_homes", 4, one_hot(index), kept, *others)[0]
+
+
+def attribution_rows(home, diff_rows, rows, cols):
+    depth = home.shape[-1]
+    cells = rows * cols
+    index = np.arange(cells).reshape(NEAR, NEAR, rows // NEAR, cols // NEAR).transpose(2, 0, 3, 1)
+
+    def kernel(order, home, diff_rows, out):
+        values = home[...].astype(F32).reshape(cells, depth).astype(BF16)
+        moved = jnp.dot(order[...], values, preferred_element_type=F32)
+        out[...] = (diff_rows[...] * moved).reshape(rows, cols, depth).astype(BF16)
+
+    return call(kernel, [((rows, cols, depth), BF16)], [], "attribution_rows", 4, one_hot(index), home, diff_rows)[0]
+
+
+def one_group(observed, baseline, cotangent, first_weight, first_bias, second_weight, second_bias):
+    rows, cols, depth = observed.shape
+    points = lax.axis_size("path")
+    sizes = group_sizes() + (rows // NEAR, cols // NEAR)
+
+    def turned(values, step):
+        return lax.ppermute(values, "path", [(i, (i + step) % points) for i in range(points)])
+
+    halves = [[part] + [turned(part, step) for step in range(1, points)] for part in (first_weight, second_weight)]
+    sent, diff_rows = pack_classes(observed, baseline, cotangent)
+    got = swap(sent)
+    first, second = join_weights(halves)
+    kept, others = adjoint_of_class(got, first, first_bias, second, second_bias, sizes)
+    others = [turned(others[step - 1], step) for step in range(1, points)]
+    home = swap(total_for_homes(kept, others, sizes))
+    return attribution_rows(home, diff_rows, rows // points, cols)
+
+
+def several_groups(observed, baseline, cotangent, first_weight, first_bias, second_weight, second_bias):
     rows, cols, depth = observed.shape
     points, point = lax.axis_size("path"), lax.axis_index("path")
     group_lon, group_lat = group_sizes()
@@ -114,6 +371,12 @@
     return (diff_rows * home / points).astype(jnp.bfloat16)
 
 
+def shards(*args):
+    if group_sizes() == (lax.axis_size("lon"), lax.axis_size("lat")):
+        return one_group(*args)
+    return several_groups(*args)
+
+
 def solution(mesh):
     placed = (
         P("lon", "lat", None),

time: 59.5 us -> 48.6 us (0.82)
  waiting for transfers between devices: 19 us -> 4.15 us
  matrix products: 11.7 us -> 0 us
  blocking collectives: 0 us -> 11.6 us
  Pallas kernels: 0 us -> 8.9 us
  other arithmetic: 3.72 us -> 0 us
  starting transfers between devices: 12.5 us -> 8.9 us
  local copies, waits for them, and re-layouts: 11.6 us -> 14.4 us
    all_to_all x2 -> x1, waiting for transfers between devices: 17.6 us -> 2.72 us  [swap(): return lax.all_to_all(chunks, ('lon', 'lat'), 0, 0, tiled=True)]
    unnamed x14 -> x34, local copies, waits for them, and re-layouts: 1.87 us -> 14.4 us
    dot_general x36 -> x0, matrix products: 11.7 us -> none  [stencil(): lax.dot_general(window, weights[tap], dims, preferred_element_type=jnp.fl...]
    all_to_all x0 -> x1, blocking collectives: none -> 11.6 us  [swap(): return lax.all_to_all(chunks, ('lon', 'lat'), 0, 0, tiled=True)]
    pallas_call x0 -> x5, Pallas kernels: none -> 8.9 us  [call(): pl.pallas_call(kernel, out_shape=shapes, in_specs=specs or [VMEM] * len(a...]
    dynamic_update_slice x3 -> x0, local copies, waits for them, and re-layouts: 3.67 us -> none  [whole_weight(): lax.dynamic_update_slice_in_dim(held, part[:, None], (point - step) % poi...]
    all_to_all x2 -> x1, starting transfers between devices: 11.9 us -> 8.3 us  [swap(): return lax.all_to_all(chunks, ('lon', 'lat'), 0, 0, tiled=True)]
    convert_element_type x4 -> x0, local copies, waits for them, and re-layouts: 2.1 us -> none  [the longest x2 1.97 us: shards(): field, upstream = (got[0], got[1].astype(jnp.float32))]
  transfers between devices with their start and end apart: 5 -> 4, of which waited for: 3 -> 2; matrix products, arithmetic and copies ran while one was open for 13% -> 0% of each run, Pallas kernels for 0% -> 6%
where the time goes in v2:
time: 48.6 us; the launch traced here: 48.1 us
  local copies, waits for them, and re-layouts  14.4 us (30%)
  blocking collectives  11.6 us (24%)
  starting transfers between devices  8.9 us (18%)
  Pallas kernels  8.9 us (18%)
  waiting for transfers between devices  4.15 us (9%)
    unnamed x34, local copies, waits for them, and re-layouts  14.4 us
    all_to_all x1, blocking collectives, swap(): return lax.all_to_all(chunks, ('lon', 'lat'), 0, 0, tiled=True)  11.6 us
    pallas_call x5, Pallas kernels, call(): pl.pallas_call(kernel, out_shape=shapes, in_specs=specs or [VMEM] * len(a...  8.9 us
    all_to_all x1, starting transfers between devices, swap(): return lax.all_to_all(chunks, ('lon', 'lat'), 0, 0, tiled=True)  8.3 us
    all_to_all x1, waiting for transfers between devices, swap(): return lax.all_to_all(chunks, ('lon', 'lat'), 0, 0, tiled=True)  2.72 us
    ppermute x3, waiting for transfers between devices, turned(): lax.ppermute(values, 'path', [(i, (i + step) % points) for i in range(poi...  1.43 us
  transfers between devices with their start and end apart: 4, of which 2 were waited for; matrix products, arithmetic and copies ran while one was open for 0% of the time, Pallas kernels for 6%

profile of v2, /device:TPU:0, one launch (start us, length us, event | category | flops | bytes accessed | tf_op | source)
XLA Modules:
  0.0 48.1 jit_solution(4211758635448212512)
XLA Ops:
  0.0 0.5 collective-permute-start
  0.5 0.1 collective-permute-start.1
  0.5 0.9 %copy-done.8 = bf16[16,16,384]{2,1,0:T(8,128)(2,1)S(1)} copy-done((bf16[16,16,384]{2,1,0:T(8,128)(2,1)S(1)}, bf16[16,16,384]{2,1,0:T(8,128)(2,1)}, u32[]{:S(2)}) %copy-start.8) | copy-done | bytes 196632
  1.5 0.9 %copy-done.9 = bf16[16,16,384]{2,1,0:T(8,128)(2,1)S(1)} copy-done((bf16[16,16,384]{2,1,0:T(8,128)(2,1)S(1)}, bf16[16,16,384]{2,1,0:T(8,128)(2,1)}, u32[]{:S(2)}) %copy-start.9) | copy-done | bytes 196632
  2.4 0.9 %copy-done.10 = bf16[16,16,384]{2,1,0:T(8,128)(2,1)S(1)} copy-done((bf16[16,16,384]{2,1,0:T(8,128)(2,1)S(1)}, bf16[16,16,384]{2,1,0:T(8,128)(2,1)}, u32[]{:S(2)}) %copy-start.10) | copy-done | bytes 196632
  3.3 0.9 %copy-done.12 = bf16[256,256]{1,0:T(8,128)(2,1)S(1)} copy-done((bf16[256,256]{1,0:T(8,128)(2,1)S(1)}, bf16[256,256]{1,0:T(8,128)(2,1)}, u32[]{:S(2)}) %copy-start.12) | copy-done | bytes 131096
  4.2 1.9 %pack_classes.1 = (bf16[16,32,384]{2,1,0:T(8,128)(2,1)}, f32[128,384]{1,0:T(8,128)S(1)}) custom-call(bf16[256,256]{1,0:T(8,128)(2,1)S(1)} %copy-done.12, bf16[256,384]{1,0:T(8,128)(2,1)S(1)} %bitcast.12, bf16[256,384]{1,0:T(8,128)(2,1)S(1)} %bitcast.13, bf16[256,384]{1,0:T(8,128)(2,1)S(1)} %bitcast.14), custom_call_target="tpu_custom_call" | custom-call | tf_op jit(solution)/shard_map/pack_classes/pallas_call | solution.py:93
  6.1 8.3 %all-to-all-start = ((bf16[16,32,384]{2,1,0:T(8,128)(2,1)}), bf16[16,32,384]{2,1,0:T(8,128)(2,1)S(1)}, u32[]{:S(2)}, u32[]{:S(2)}) async-start(bf16[16,32,384]{2,1,0:T(8,128)(2,1)} %get-tuple-element.11), calls=%async_computation | async-start | bytes 786432 | tf_op jit(solution)/shard_map/all_to_all | solution.py:37
  14.4 0.0 copy-done.15
  14.4 0.0 copy-done.16
  14.5 0.0 collective-permute-done
  14.5 0.0 copy-start.4
  14.5 1.1 %copy-done.4 = bf16[9,192,384]{2,1,0:T(8,128)(2,1)} copy-done((bf16[9,192,384]{2,1,0:T(8,128)(2,1)}, bf16[9,192,384]{2,1,0:T(8,128)(2,1)S(1)}, u32[]{:S(2)}) %copy-start.4) | copy-done | bytes 1327128
  15.5 0.0 collective-permute-done.1
  15.6 1.1 %copy-done.6 = bf16[9,192,384]{2,1,0:T(8,128)(2,1)} copy-done((bf16[9,192,384]{2,1,0:T(8,128)(2,1)}, bf16[9,192,384]{2,1,0:T(8,128)(2,1)S(1)}, u32[]{:S(2)}) %copy-start.6) | copy-done | bytes 1327128
  16.6 1.3 %copy-done.2 = bf16[9,192,384]{2,1,0:T(8,128)(2,1)S(1)} copy-done((bf16[9,192,384]{2,1,0:T(8,128)(2,1)S(1)}, bf16[9,192,384]{2,1,0:T(8,128)(2,1)}, u32[]{:S(2)}) %copy-start.2) | copy-done | bytes 1327128
  17.9 1.3 %copy-done.3 = bf16[9,192,384]{2,1,0:T(8,128)(2,1)S(1)} copy-done((bf16[9,192,384]{2,1,0:T(8,128)(2,1)S(1)}, bf16[9,192,384]{2,1,0:T(8,128)(2,1)}, u32[]{:S(2)}) %copy-start.3) | copy-done | bytes 1327128
  19.3 1.3 %copy-done.5 = bf16[9,192,384]{2,1,0:T(8,128)(2,1)S(1)} copy-done((bf16[9,192,384]{2,1,0:T(8,128)(2,1)S(1)}, bf16[9,192,384]{2,1,0:T(8,128)(2,1)}, u32[]{:S(2)}) %copy-start.5) | copy-done | bytes 1327128
  20.6 1.3 %copy-done.7 = bf16[9,192,384]{2,1,0:T(8,128)(2,1)S(1)} copy-done((bf16[9,192,384]{2,1,0:T(8,128)(2,1)S(1)}, bf16[9,192,384]{2,1,0:T(8,128)(2,1)}, u32[]{:S(2)}) %copy-start.7) | copy-done | bytes 1327128
  21.9 1.1 %join_weights.1 = (bf16[3,3,384,384]{3,2,1,0:T(8,128)(2,1)S(1)}, bf16[3,3,384,384]{3,2,1,0:T(8,128)(2,1)S(1)}) custom-call(bf16[3,3,192,384]{3,2,1,0:T(8,128)(2,1)S(1)} %bitcast.8, bf16[3,3,192,384]{3,2,1,0:T(8,128)(2,1)S(1)} %bitcast.10, bf16[3,3,192,384]{3,2,1,0:T(8,128)(2,1)S(1)} %bitcast.9, bf16[3,3,192,384]{3,2,1,0:T(8,128)(2,1)S(1)} %bitcast.11), custom_call_target="tpu_custom_call" | custom-call | tf_op jit(solution)/shard_map/join_weights/pallas_call | solution.py:93
  23.0 0.0 copy-start
  23.0 1.5 %copy-done = bf16[3,3,384,384]{3,2,1,0:T(8,128)(2,1)} copy-done((bf16[3,3,384,384]{3,2,1,0:T(8,128)(2,1)}, bf16[3,3,384,384]{3,2,1,0:T(8,128)(2,1)S(1)}, u32[]{:S(2)}) %copy-start) | copy-done | bytes 2654232
  24.5 2.7 %all-to-all-done.got = bf16[16,32,384]{2,1,0:T(8,128)(2,1)S(1)} async-done(((bf16[16,32,384]{2,1,0:T(8,128)(2,1)}), bf16[16,32,384]{2,1,0:T(8,128)(2,1)S(1)}, u32[]{:S(2)}, u32[]{:S(2)}) %all-to-all-start) | async-done | bytes 393248 | tf_op jit(solution)/shard_map/all_to_all | solution.py:37
  27.3 0.0 copy-done.11
  27.3 1.7 %copy-done.1 = bf16[3,3,384,384]{3,2,1,0:T(8,128)(2,1)S(1)} copy-done((bf16[3,3,384,384]{3,2,1,0:T(8,128)(2,1)S(1)}, bf16[3,3,384,384]{3,2,1,0:T(8,128)(2,1)}, u32[]{:S(2)}) %copy-start.1) | copy-done | bytes 2654232
  29.0 4.9 %adjoint_of_class.1 = (f32[128,384]{1,0:T(8,128)S(1)}, f32[1,128,384]{2,1,0:T(8,128)S(1)}) custom-call(bf16[256,256]{1,0:T(8,128)(2,1)S(1)} %copy-done.11, bf16[16,32,384]{2,1,0:T(8,128)(2,1)S(1)} %all-to-all-done.got, bf16[3,3,384,384]{3,2,1,0:T(8,128)(2,1)S(1)} %get-tuple-element.12.first, f32[1,384]{1,0:T(1,128)S(1)} %reshape.34.first_bias, ...), custom_call_target="tpu_custom_call" | custom-call | tf_op jit(solution)/shard_map/adjoint_of_class/pallas_call | solution.py:93
  33.9 0.1 collective-permute-start.2
  34.0 1.4 %collective-permute-done.2.refs_0_ = f32[128,384]{1,0:T(8,128)S(1)} collective-permute-done((f32[128,384]{1,0:T(8,128)S(1)}, f32[128,384]{1,0:T(8,128)S(1)}, u32[]{:S(2)}, u32[]{:S(2)}) %collective-permute-start.2) | collective-permute-done | bytes 196640 | tf_op jit(solution)/shard_map/ppermute | solution.py:317
  35.4 0.0 copy-done.13
  35.4 0.2 total_for_homes.1
  35.6 11.6 %all_to_all.10.home = bf16[16,8,384]{2,1,0:T(8,128)(2,1)S(1)} all-to-all(bf16[16,8,384]{2,1,0:T(8,128)(2,1)S(1)} %total_for_homes.1), channel_id=1, replica_groups=mesh['path'=2,'lon'=8,'lat'=2] {'lon','lat'}, dimensions={0} | all-to-all | bytes 196608 | tf_op jit(solution)/shard_map/all_to_all | solution.py:37
  47.3 0.8 %attribution_rows.1 = bf16[8,16,384]{2,1,0:T(8,128)(2,1)} custom-call(bf16[128,128]{1,0:T(8,128)(2,1)S(1)} %copy-done.14, bf16[16,8,384]{2,1,0:T(8,128)(2,1)S(1)} %all_to_all.10.home, f32[128,384]{1,0:T(8,128)S(1)} %get-tuple-element.16.diff_rows), custom_call_target="tpu_custom_call" | custom-call | tf_op jit(solution)/shard_map/attribution_rows/pallas_call | solution.py:93
  (18 shorter events, 0.0 us)
Async XLA Ops:
  0.0 14.4 %copy-start.15 = (f32[384]{0:T(512)S(1)}, f32[384]{0:T(512)}, u32[]{:S(2)}) copy-start(f32[384]{0:T(512)} %param.15) | copy-start | bytes 4612
  0.0 14.4 %copy-start.16 = (f32[384]{0:T(512)S(1)}, f32[384]{0:T(512)}, u32[]{:S(2)}) copy-start(f32[384]{0:T(512)} %param.17) | copy-start | bytes 4612
  0.0 14.5 %collective-permute-start = (bf16[9,192,384]{2,1,0:T(8,128)(2,1)}, bf16[9,192,384]{2,1,0:T(8,128)(2,1)S(1)}, u32[]{:S(2)}, u32[]{:S(2)}) collective-permute-start(bf16[9,192,384]{2,1,0:T(8,128)(2,1)} %param.14), channel_id=1, source_target_pairs={{0,16},{16,0},{1,17},{17,1},{2,18},{18,2},{3,19},{19,3},{4,20},{20... | collective-permute-start | bytes 3981320 | tf_op jit(solution)/shard_map/ppermute | solution.py:317
  0.5 15.1 %collective-permute-start.1 = (bf16[9,192,384]{2,1,0:T(8,128)(2,1)}, bf16[9,192,384]{2,1,0:T(8,128)(2,1)S(1)}, u32[]{:S(2)}, u32[]{:S(2)}) collective-permute-start(bf16[9,192,384]{2,1,0:T(8,128)(2,1)} %param.16), channel_id=1, source_target_pairs={{0,16},{16,0},{1,17},{17,1},{2,18},{18,2},{3,19},{19,3},{4,20},{20... | collective-permute-start | bytes 3981320 | tf_op jit(solution)/shard_map/ppermute | solution.py:317
  0.5 0.9 %copy-start.8 = (bf16[16,16,384]{2,1,0:T(8,128)(2,1)S(1)}, bf16[16,16,384]{2,1,0:T(8,128)(2,1)}, u32[]{:S(2)}) copy-start(bf16[16,16,384]{2,1,0:T(8,128)(2,1)} %param.11) | copy-start | bytes 589828
  1.5 0.9 %copy-start.9 = (bf16[16,16,384]{2,1,0:T(8,128)(2,1)S(1)}, bf16[16,16,384]{2,1,0:T(8,128)(2,1)}, u32[]{:S(2)}) copy-start(bf16[16,16,384]{2,1,0:T(8,128)(2,1)} %param.12) | copy-start | bytes 589828
  2.4 0.9 %copy-start.10 = (bf16[16,16,384]{2,1,0:T(8,128)(2,1)S(1)}, bf16[16,16,384]{2,1,0:T(8,128)(2,1)}, u32[]{:S(2)}) copy-start(bf16[16,16,384]{2,1,0:T(8,128)(2,1)} %param.13) | copy-start | bytes 589828
  3.3 0.9 %copy-start.12 = (bf16[256,256]{1,0:T(8,128)(2,1)S(1)}, bf16[256,256]{1,0:T(8,128)(2,1)}, u32[]{:S(2)}) copy-start(bf16[256,256]{1,0:T(8,128)(2,1)} %constant.8.clone.order) | copy-start | bytes 393220
  6.1 21.1 %all-to-all-start = ((bf16[16,32,384]{2,1,0:T(8,128)(2,1)}), bf16[16,32,384]{2,1,0:T(8,128)(2,1)S(1)}, u32[]{:S(2)}, u32[]{:S(2)}) async-start(bf16[16,32,384]{2,1,0:T(8,128)(2,1)} %get-tuple-element.11), calls=%async_computation | async-start | bytes 786432 | tf_op jit(solution)/shard_map/all_to_all | solution.py:37
  14.5 1.1 %copy-start.4 = (bf16[9,192,384]{2,1,0:T(8,128)(2,1)}, bf16[9,192,384]{2,1,0:T(8,128)(2,1)S(1)}, u32[]{:S(2)}) copy-start(bf16[9,192,384]{2,1,0:T(8,128)(2,1)S(1)} %collective-permute-done) | copy-start | bytes 3981316
  15.6 1.1 %copy-start.6 = (bf16[9,192,384]{2,1,0:T(8,128)(2,1)}, bf16[9,192,384]{2,1,0:T(8,128)(2,1)S(1)}, u32[]{:S(2)}) copy-start(bf16[9,192,384]{2,1,0:T(8,128)(2,1)S(1)} %collective-permute-done.1) | copy-start | bytes 3981316
  16.6 1.3 %copy-start.2 = (bf16[9,192,384]{2,1,0:T(8,128)(2,1)S(1)}, bf16[9,192,384]{2,1,0:T(8,128)(2,1)}, u32[]{:S(2)}) copy-start(bf16[9,192,384]{2,1,0:T(8,128)(2,1)} %param.14) | copy-start | bytes 3981316
  17.9 1.3 %copy-start.3 = (bf16[9,192,384]{2,1,0:T(8,128)(2,1)S(1)}, bf16[9,192,384]{2,1,0:T(8,128)(2,1)}, u32[]{:S(2)}) copy-start(bf16[9,192,384]{2,1,0:T(8,128)(2,1)} %param.16) | copy-start | bytes 3981316
  19.3 1.3 %copy-start.5 = (bf16[9,192,384]{2,1,0:T(8,128)(2,1)S(1)}, bf16[9,192,384]{2,1,0:T(8,128)(2,1)}, u32[]{:S(2)}) copy-start(bf16[9,192,384]{2,1,0:T(8,128)(2,1)} %copy-done.4) | copy-start | bytes 3981316
  20.6 1.3 %copy-start.7 = (bf16[9,192,384]{2,1,0:T(8,128)(2,1)S(1)}, bf16[9,192,384]{2,1,0:T(8,128)(2,1)}, u32[]{:S(2)}) copy-start(bf16[9,192,384]{2,1,0:T(8,128)(2,1)} %copy-done.6) | copy-start | bytes 3981316
  21.9 5.4 %copy-start.11 = (bf16[256,256]{1,0:T(8,128)(2,1)S(1)}, bf16[256,256]{1,0:T(8,128)(2,1)}, u32[]{:S(2)}) copy-start(bf16[256,256]{1,0:T(8,128)(2,1)} %constant.9.clone.order) | copy-start | bytes 393220
  23.0 1.5 %copy-start = (bf16[3,3,384,384]{3,2,1,0:T(8,128)(2,1)}, bf16[3,3,384,384]{3,2,1,0:T(8,128)(2,1)S(1)}, u32[]{:S(2)}) copy-start(bf16[3,3,384,384]{3,2,1,0:T(8,128)(2,1)S(1)} %get-tuple-element.13.second) | copy-start | bytes 7962628
  27.3 1.8 %copy-start.1 = (bf16[3,3,384,384]{3,2,1,0:T(8,128)(2,1)S(1)}, bf16[3,3,384,384]{3,2,1,0:T(8,128)(2,1)}, u32[]{:S(2)}) copy-start(bf16[3,3,384,384]{3,2,1,0:T(8,128)(2,1)} %copy-done) | copy-start | bytes 7962628
  29.0 6.4 %copy-start.13 = (bf16[128,128]{1,0:T(8,128)(2,1)S(1)}, bf16[128,128]{1,0:T(8,128)(2,1)}, u32[]{:S(2)}) copy-start(bf16[128,128]{1,0:T(8,128)(2,1)} %constant.10.clone.order) | copy-start | bytes 98308
  29.0 18.3 %copy-start.14 = (bf16[128,128]{1,0:T(8,128)(2,1)S(1)}, bf16[128,128]{1,0:T(8,128)(2,1)}, u32[]{:S(2)}) copy-start(bf16[128,128]{1,0:T(8,128)(2,1)} %constant.11.clone.order) | copy-start | bytes 98308
  33.9 1.5 %collective-permute-start.2 = (f32[128,384]{1,0:T(8,128)S(1)}, f32[128,384]{1,0:T(8,128)S(1)}, u32[]{:S(2)}, u32[]{:S(2)}) collective-permute-start(f32[128,384]{1,0:T(8,128)S(1)} %bitcast.15), channel_id=1, source_target_pairs={{0,16},{16,0},{1,17},{17,1},{2,18},{18,2},{3,19},{19,3},{4,20},{20... | collective-permute-start | bytes 589832 | tf_op jit(solution)/shard_map/ppermute | solution.py:317

commit v3 on v2

--- a/solution.py
+++ b/solution.py
@@ -2,7 +2,6 @@
 
 import jax
 import jax.numpy as jnp
-import numpy as np
 from jax import lax
 from jax.experimental import pallas as pl
 from jax.experimental.pallas import tpu as pltpu
@@ -14,7 +13,7 @@
 LANES = 128
 F32, BF16 = jnp.float32, jnp.bfloat16
 VMEM = pl.BlockSpec(memory_space=pltpu.VMEM)
-ANY = pl.BlockSpec(memory_space=pl.ANY)
+HBM = pl.BlockSpec(memory_space=pltpu.HBM)
 
 def smooth_act(value):
     return jax.nn.gelu(value, approximate=True)
@@ -76,8 +75,14 @@
     return total
 
 
-def one_hot(source):
-    return jnp.asarray(np.eye(source.size, dtype=np.float32)[source.reshape(-1)], BF16)
+def ordering(dims, axes):
+    cells = math.prod(dims)
+    place = lax.broadcasted_iota(jnp.int32, (cells, 1), 0)
+    source, stride = jnp.zeros((cells, 1), jnp.int32), 1
+    for axis in reversed(axes):
+        source += lax.rem(lax.div(place, jnp.int32(stride)), jnp.int32(dims[axis])) * math.prod(dims[axis + 1 :])
+        stride *= dims[axis]
+    return (lax.broadcasted_iota(jnp.int32, (cells, cells), 1) == source).astype(F32).astype(BF16)
 
 
 def gelu_and_slope(value):
@@ -88,15 +93,17 @@
     return value * half, half + 0.5 * value * (1 - bent * bent) * (scale * (1 + 3 * cubic * square))
 
 
-def call(kernel, outs, scratch, name, megabytes, *args, specs=None):
-    shapes = [jax.ShapeDtypeStruct(shape, dtype) for shape, dtype in outs]
+def call(kernel, outs, scratch, name, megabytes, *args, specs=None, flops=0):
+    specs = specs or [VMEM] * len(args)
+    args = [pltpu.with_memory_space_constraint(x, spec.memory_space) for x, spec in zip(args, specs)]
     return pl.pallas_call(
         kernel,
-        out_shape=shapes,
-        in_specs=specs or [VMEM] * len(args),
+        out_shape=[pltpu.VMEM(shape, dtype) for shape, dtype in outs],
+        in_specs=specs,
         out_specs=[VMEM] * len(outs),
         scratch_shapes=scratch,
         compiler_params=pltpu.CompilerParams(vmem_limit_bytes=megabytes << 20),
+        cost_estimate=pl.CostEstimate(flops=flops, bytes_accessed=sum(x.size * x.dtype.itemsize for x in args), transcendentals=0),
         name=name,
     )(*args)
 
@@ -105,16 +112,15 @@
     rows, cols, depth = observed.shape
     points, point = lax.axis_size("path"), lax.axis_index("path")
     cells, part = rows * cols, rows * cols // (NEAR * NEAR)
-    index = np.arange(cells).reshape(rows // NEAR, NEAR, cols // NEAR, NEAR).transpose(1, 3, 0, 2)
-    order = one_hot(index)
-
-    def kernel(order, observed, baseline, cotangent, sent, diff_rows, held, sems):
+
+    def kernel(observed, baseline, cotangent, sent, diff_rows, held, sems):
         copies = [
             pltpu.make_async_copy(ref, held.at[i], sems.at[i])
             for i, ref in enumerate((observed, baseline, cotangent))
         ]
         for copy in copies:
             copy.start()
+        order = ordering((rows // NEAR, NEAR, cols // NEAR, NEAR), (1, 3, 0, 2))
         for copy in copies:
             copy.wait()
         mine = lax.axis_index("path")
@@ -123,7 +129,7 @@
         diff = held[0].astype(F32) - base
         field = (base + mix * diff).astype(BF16)
         for i, values in enumerate((field, held[2])):
-            moved = jnp.dot(order[...], values, preferred_element_type=F32)
+            moved = jnp.dot(order, values, preferred_element_type=F32)
             sent[:, i * part : (i + 1) * part, :] = moved.reshape(NEAR * NEAR, part, depth).astype(BF16)
         half = pl.ds(pl.multiple_of(mine * (cells // points), cells // points), cells // points)
         own = held[1, half, :].astype(F32)
@@ -135,59 +141,33 @@
         [pltpu.VMEM((3, cells, depth), BF16), pltpu.SemaphoreType.DMA((3,))],
         "pack_classes",
         8,
-        order,
         *(x.reshape(cells, depth) for x in (observed, baseline, cotangent)),
-        specs=[VMEM, ANY, ANY, ANY],
+        specs=[HBM] * 3,
+        flops=4 * 10**9,
     )
 
 
-def join_weights(halves):
-    points = len(halves[0])
-    taps, width, depth = halves[0][0].shape
-    side = math.isqrt(taps)
-
-    def kernel(*refs):
-        parts, wholes, sems = refs[: 2 * points], refs[2 * points : 2 * points + 2], refs[-1]
-        mine = lax.axis_index("path")
-        copies = []
-        for k in range(2 * points):
-            owner = lax.rem(mine + points - k % points, points)
-            span = pl.ds(pl.multiple_of(owner * width, width), width)
-            for col in range(side):
-                copies.append(
-                    pltpu.make_async_copy(
-                        parts[k].at[:, col], wholes[k // points].at[col, :, span, :], sems.at[k, col]
-                    )
-                )
-        for copy in copies:
-            copy.start()
-        for copy in copies:
-            copy.wait()
-
-    shape = (side, side, width * points, depth)
-    args = [x.reshape(side, side, width, depth) for parts in halves for x in parts]
-    return call(
-        kernel,
-        [(shape, BF16)] * 2,
-        [pltpu.SemaphoreType.DMA((2 * points, side))],
-        "join_weights",
-        16,
-        *args,
-        specs=[ANY] * len(args),
-    )
-
-
-def adjoint_of_class(got, first, first_bias, second, second_bias, sizes):
+def adjoint_of_class(got, first_halves, first_bias, second_halves, second_bias, sizes):
     group_lon, group_lat, row_part, col_part = sizes
     points = lax.axis_size("path")
     depth = got.shape[-1]
     rows, cols = group_lon * row_part, group_lat * col_part
     cells, part = rows * cols, row_part * col_part
     span = row_part // points
-    index = np.arange(cells).reshape(group_lon, group_lat, row_part, col_part).transpose(1, 3, 0, 2)
-    order = one_hot(index)
-
-    def kernel(order, got, first, first_bias, second, second_bias, kept, sent, edged, taps, slope, grad, laned):
+
+    def kernel(got, first_bias, second_bias, *refs):
+        mine = lax.axis_index("path")
+        for owner in range(points):
+            inputs = [(owner - k) % points for k in range(points)]
+            first, second = ([refs[j * points + k] for k in inputs] for j in range(2))
+            pl.when(mine == owner)(lambda: run(owner, got, first, first_bias, second, second_bias, *refs[2 * points :]))
+
+    def run(mine, got, first, first_bias, second, second_bias, kept, sent, edged, taps, slope, grad, laned):
+        order = ordering((group_lon, group_lat, row_part, col_part), (1, 3, 0, 2))
+
+        def tap_weight(parts, row, col):
+            return jnp.concatenate([part[row, col] for part in parts], axis=0)
+
         def spread(values, step):
             edged[:, EDGE : EDGE + rows, :] = values.reshape(cols, rows, depth)
             for i in range(3):
@@ -199,17 +179,15 @@
         def both_sides(weigh, step):
             shift = step * rows
             fill = jnp.zeros((shift, depth), F32)
+            same = weigh(taps[...], 1)
             after = weigh(taps[shift:, :], 2)
             before = weigh(taps[: cells - shift, :], 0)
-            return (
-                weigh(taps[...], 1)
-                + jnp.concatenate([after, fill], axis=0)
-                + jnp.concatenate([fill, before], axis=0)
-            )
+            return same + jnp.concatenate([after, fill], axis=0) + jnp.concatenate([fill, before], axis=0)
 
         def forward(weights, step):
             def weigh(values, col):
-                return jnp.dot(values, weights[col].reshape(3 * depth, depth), preferred_element_type=F32)
+                column = jnp.concatenate([tap_weight(weights, i, col) for i in range(3)], axis=0)
+                return jnp.dot(values, column, preferred_element_type=F32)
 
             return both_sides(weigh, step)
 
@@ -219,7 +197,7 @@
                 for i in range(3):
                     term = lax.dot_general(
                         values[:, i * depth : (i + 1) * depth],
-                        weights[2 - col, 2 - i],
+                        tap_weight(weights, 2 - i, 2 - col),
                         (((1,), (1,)), ((), ())),
                         preferred_element_type=F32,
                     )
@@ -231,13 +209,13 @@
         edged[:, :EDGE, :] = jnp.zeros((cols, EDGE, depth), F32)
         edged[:, EDGE + rows :, :] = jnp.zeros((cols, EDGE, depth), F32)
         field, upstream = (
-            jnp.dot(order[...], got[:, i * part : (i + 1) * part, :].reshape(cells, depth), preferred_element_type=F32)
+            jnp.dot(order, got[:, i * part : (i + 1) * part, :].reshape(cells, depth), preferred_element_type=F32)
             for i in range(2)
         )
         spread(field, 1)
-        act, slope[...] = gelu_and_slope(forward(first, 1) + first_bias[...])
+        act, slope[...] = gelu_and_slope(forward(first, 1) + first_bias[...].reshape(1, depth))
         spread(field + act, FAR // NEAR)
-        second_pre = forward(second, FAR // NEAR) + second_bias[...]
+        second_pre = forward(second, FAR // NEAR) + second_bias[...].reshape(1, depth)
         spread(gelu_and_slope(second_pre)[1] * upstream, FAR // NEAR)
         hidden_adj = upstream + backward(second, FAR // NEAR)
         grad[...] = hidden_adj
@@ -245,9 +223,8 @@
         grad[...] += backward(first, 1)
         for b in range(depth // LANES):
             laned[b] = grad[:, b * LANES : (b + 1) * LANES].reshape(cols, rows, LANES)
-        mine = lax.axis_index("path")
         for k in range(points):
-            owner = lax.rem(mine + k, points)
+            owner = (mine + k) % points
             for i in range(span):
                 target = kept if k == 0 else sent.at[k - 1]
                 place = slice(i * (cells // row_part), (i + 1) * (cells // row_part))
@@ -268,12 +245,11 @@
         ],
         "adjoint_of_class",
         24,
-        order,
         got,
-        first,
-        first_bias.reshape(1, depth),
-        second,
-        second_bias.reshape(1, depth),
+        first_bias,
+        second_bias,
+        *first_halves,
+        *second_halves,
     )
 
 
@@ -282,30 +258,30 @@
     share, depth = kept.shape
     span = row_part // lax.axis_size("path")
     part = span * col_part
-    index = np.arange(share).reshape(span, group_lat, col_part, group_lon).transpose(3, 1, 0, 2)
-
-    def kernel(order, kept, *refs):
+
+    def kernel(kept, *refs):
+        order = ordering((span, group_lat, col_part, group_lon), (3, 1, 0, 2))
         others, sent = refs[:-1], refs[-1]
         total = kept[...]
         for other in others:
             total = total + other[...]
-        moved = jnp.dot(order[...], total.astype(BF16), preferred_element_type=F32)
+        moved = jnp.dot(order, total.astype(BF16), preferred_element_type=F32)
         sent[...] = moved.reshape(share // part, part, depth).astype(BF16)
 
-    return call(kernel, [((share // part, part, depth), BF16)], [], "total_for_homes", 4, one_hot(index), kept, *others)[0]
+    return call(kernel, [((share // part, part, depth), BF16)], [], "total_for_homes", 4, kept, *others)[0]
 
 
 def attribution_rows(home, diff_rows, rows, cols):
     depth = home.shape[-1]
     cells = rows * cols
-    index = np.arange(cells).reshape(NEAR, NEAR, rows // NEAR, cols // NEAR).transpose(2, 0, 3, 1)
-
-    def kernel(order, home, diff_rows, out):
+
+    def kernel(home, diff_rows, out):
+        order = ordering((NEAR, NEAR, rows // NEAR, cols // NEAR), (2, 0, 3, 1))
         values = home[...].astype(F32).reshape(cells, depth).astype(BF16)
-        moved = jnp.dot(order[...], values, preferred_element_type=F32)
+        moved = jnp.dot(order, values, preferred_element_type=F32)
         out[...] = (diff_rows[...] * moved).reshape(rows, cols, depth).astype(BF16)
 
-    return call(kernel, [((rows, cols, depth), BF16)], [], "attribution_rows", 4, one_hot(index), home, diff_rows)[0]
+    return call(kernel, [((rows, cols, depth), BF16)], [], "attribution_rows", 4, home, diff_rows)[0]
 
 
 def one_group(observed, baseline, cotangent, first_weight, first_bias, second_weight, second_bias):
@@ -316,11 +292,14 @@
     def turned(values, step):
         return lax.ppermute(values, "path", [(i, (i + step) % points) for i in range(points)])
 
-    halves = [[part] + [turned(part, step) for step in range(1, points)] for part in (first_weight, second_weight)]
+    side = math.isqrt(first_weight.shape[0])
+    halves = [
+        [x.reshape((side, side) + x.shape[1:]) for x in [part] + [turned(part, step) for step in range(1, points)]]
+        for part in (first_weight, second_weight)
+    ]
     sent, diff_rows = pack_classes(observed, baseline, cotangent)
     got = swap(sent)
-    first, second = join_weights(halves)
-    kept, others = adjoint_of_class(got, first, first_bias, second, second_bias, sizes)
+    kept, others = adjoint_of_class(got, halves[0], first_bias, halves[1], second_bias, sizes)
     others = [turned(others[step - 1], step) for step in range(1, points)]
     home = swap(total_for_homes(kept, others, sizes))
     return attribution_rows(home, diff_rows, rows // points, cols)

time: 48.6 us -> 41.9 us (0.86)
  blocking collectives: 11.6 us -> 32 us
  local copies, waits for them, and re-layouts: 14.4 us -> 0.66 us
  starting transfers between devices: 8.9 us -> 0.58 us
  waiting for transfers between devices: 4.15 us -> 1.43 us
  Pallas kernels: 8.9 us -> 6.99 us
    all_to_all x1 -> x2, blocking collectives: 11.6 us -> 32 us  [swap(): return lax.all_to_all(chunks, ('lon', 'lat'), 0, 0, tiled=True)]
    unnamed x34 -> x9, local copies, waits for them, and re-layouts: 14.4 us -> 0.66 us
    all_to_all x1 -> x0, starting transfers between devices: 8.3 us -> none  [swap(): return lax.all_to_all(chunks, ('lon', 'lat'), 0, 0, tiled=True)]
    all_to_all x1 -> x0, waiting for transfers between devices: 2.72 us -> none  [swap(): return lax.all_to_all(chunks, ('lon', 'lat'), 0, 0, tiled=True)]
    pallas_call x5 -> x4, Pallas kernels: 8.9 us -> 6.99 us  [call(): pl.pallas_call(kernel, out_shape=[pltpu.VMEM(shape, dtype) for shape, dty...]
  transfers between devices with their start and end apart: 4 -> 3, of which waited for: 2 -> 1; matrix products, arithmetic and copies ran while one was open for 0% -> 0% of each run, Pallas kernels for 6% -> 4%
where the time goes in v3:
time: 41.9 us; the launch traced here: 41.7 us
  blocking collectives  32 us (76%)
  Pallas kernels  6.99 us (17%)
  waiting for transfers between devices  1.43 us (3%)
  local copies, waits for them, and re-layouts  0.66 us (2%)
  starting transfers between devices  0.58 us (1%)
    all_to_all x2, blocking collectives, swap(): return lax.all_to_all(chunks, ('lon', 'lat'), 0, 0, tiled=True)  32 us
    pallas_call x4, Pallas kernels, call(): pl.pallas_call(kernel, out_shape=[pltpu.VMEM(shape, dtype) for shape, dty...  6.99 us
    ppermute x3, waiting for transfers between devices, turned(): lax.ppermute(values, 'path', [(i, (i + step) % points) for i in range(poi...  1.43 us
  transfers between devices with their start and end apart: 3, of which 1 were waited for; matrix products, arithmetic and copies ran while one was open for 0% of the time, Pallas kernels for 4%

profile of v3, /device:TPU:0, one launch (start us, length us, event | category | flops | bytes accessed | tf_op | source)
XLA Modules:
  0.0 41.7 jit_solution(15723954815749664312)
XLA Ops:
  0.0 0.5 %collective-permute-start = (bf16[9,192,384]{2,1,0:T(8,128)(2,1)}, bf16[9,192,384]{2,1,0:T(8,128)(2,1)S(1)}, u32[]{:S(2)}, u32[]{:S(2)}) collective-permute-start(bf16[9,192,384]{2,1,0:T(8,128)(2,1)} %param.10), channel_id=1, source_target_pairs={{0,16},{16,0},{1,17},{17,1},{2,18},{18,2},{3,19},{19,3},{4,20},{20... | collective-permute-start | bytes 3981320 | tf_op jit(solution)/shard_map/ppermute | solution.py:293
  0.5 0.1 collective-permute-start.1
  0.5 0.0 copy-start
  0.5 0.0 copy-start.1
  0.5 0.0 copy-start.2
  0.5 0.0 copy-start.3
  0.5 1.7 %pack_classes.1 = (bf16[16,32,384]{2,1,0:T(8,128)(2,1)S(1)}, f32[128,384]{1,0:T(8,128)S(1)}) custom-call(bf16[256,384]{1,0:T(8,128)(2,1)} %bitcast.13, bf16[256,384]{1,0:T(8,128)(2,1)} %bitcast.14, bf16[256,384]{1,0:T(8,128)(2,1)} %bitcast.15), custom_call_target="tpu_custom_call" | custom-call | flops 4000000000 | bytes 589824 | tf_op jit(solution)/shard_map/pack_classes/pallas_call | solution.py:99
  2.2 20.9 %all_to_all.10.got = bf16[16,32,384]{2,1,0:T(8,128)(2,1)S(1)} all-to-all(bf16[16,32,384]{2,1,0:T(8,128)(2,1)S(1)} %get-tuple-element.9), channel_id=1, replica_groups=mesh['path'=2,'lon'=8,'lat'=2] {'lon','lat'}, dimensions={0} | all-to-all | bytes 786432 | tf_op jit(solution)/shard_map/all_to_all | solution.py:36
  23.1 0.0 collective-permute-done
  23.1 0.0 collective-permute-done.1
  23.1 0.0 copy-done
  23.1 0.0 copy-done.1
  23.1 0.0 copy-done.2
  23.1 0.0 copy-done.3
  23.1 5.0 %adjoint_of_class.1 = (f32[128,384]{1,0:T(8,128)S(1)}, f32[1,128,384]{2,1,0:T(8,128)S(1)}) custom-call(bf16[16,32,384]{2,1,0:T(8,128)(2,1)S(1)} %all_to_all.10.got, f32[384]{0:T(512)S(1)} %copy-done.2, f32[384]{0:T(512)S(1)} %copy-done.3, bf16[3,3,192,384]{3,2,1,0:T(8,128)(2,1)S(1)} %bitcast.8, bf16[3,3,192,384]{3,2,1,0:T(8,128)(2,1)S(1)} %bitcast.10, ...), custom_call_target="tpu_custom_call" | custom-call | bytes 5704704 | tf_op jit(solution)/shard_map/adjoint_of_class/pallas_call | solution.py:99
  28.1 0.1 collective-permute-start.2
  28.2 1.4 %collective-permute-done.2.refs_0_ = f32[128,384]{1,0:T(8,128)S(1)} collective-permute-done((f32[128,384]{1,0:T(8,128)S(1)}, f32[128,384]{1,0:T(8,128)S(1)}, u32[]{:S(2)}, u32[]{:S(2)}) %collective-permute-start.2) | collective-permute-done | bytes 196640 | tf_op jit(solution)/shard_map/ppermute | solution.py:293
  29.6 0.2 total_for_homes.1
  29.8 11.1 %all_to_all.11.home = bf16[16,8,384]{2,1,0:T(8,128)(2,1)S(1)} all-to-all(bf16[16,8,384]{2,1,0:T(8,128)(2,1)S(1)} %total_for_homes.1), channel_id=1, replica_groups=mesh['path'=2,'lon'=8,'lat'=2] {'lon','lat'}, dimensions={0} | all-to-all | bytes 196608 | tf_op jit(solution)/shard_map/all_to_all | solution.py:36
  40.9 0.2 attribution_rows.1
  41.1 0.6 %copy.8 = bf16[8,16,384]{2,1,0:T(8,128)(2,1)} copy(bf16[8,16,384]{2,1,0:T(8,128)(2,1)S(1)} %attribution_rows.1) | data formatting | bytes 196608
Async XLA Ops:
  0.0 23.1 %collective-permute-start = (bf16[9,192,384]{2,1,0:T(8,128)(2,1)}, bf16[9,192,384]{2,1,0:T(8,128)(2,1)S(1)}, u32[]{:S(2)}, u32[]{:S(2)}) collective-permute-start(bf16[9,192,384]{2,1,0:T(8,128)(2,1)} %param.10), channel_id=1, source_target_pairs={{0,16},{16,0},{1,17},{17,1},{2,18},{18,2},{3,19},{19,3},{4,20},{20... | collective-permute-start | bytes 3981320 | tf_op jit(solution)/shard_map/ppermute | solution.py:293
  0.5 22.6 %collective-permute-start.1 = (bf16[9,192,384]{2,1,0:T(8,128)(2,1)}, bf16[9,192,384]{2,1,0:T(8,128)(2,1)S(1)}, u32[]{:S(2)}, u32[]{:S(2)}) collective-permute-start(bf16[9,192,384]{2,1,0:T(8,128)(2,1)} %param.12), channel_id=1, source_target_pairs={{0,16},{16,0},{1,17},{17,1},{2,18},{18,2},{3,19},{19,3},{4,20},{20... | collective-permute-start | bytes 3981320 | tf_op jit(solution)/shard_map/ppermute | solution.py:293
  0.5 22.6 %copy-start = (bf16[9,192,384]{2,1,0:T(8,128)(2,1)S(1)}, bf16[9,192,384]{2,1,0:T(8,128)(2,1)}, u32[]{:S(2)}) copy-start(bf16[9,192,384]{2,1,0:T(8,128)(2,1)} %param.10) | copy-start | bytes 3981316
  0.5 22.6 %copy-start.1 = (bf16[9,192,384]{2,1,0:T(8,128)(2,1)S(1)}, bf16[9,192,384]{2,1,0:T(8,128)(2,1)}, u32[]{:S(2)}) copy-start(bf16[9,192,384]{2,1,0:T(8,128)(2,1)} %param.12) | copy-start | bytes 3981316
  0.5 22.6 %copy-start.2 = (f32[384]{0:T(512)S(1)}, f32[384]{0:T(512)}, u32[]{:S(2)}) copy-start(f32[384]{0:T(512)} %first_bias.1) | copy-start | bytes 4612
  0.5 22.6 %copy-start.3 = (f32[384]{0:T(512)S(1)}, f32[384]{0:T(512)}, u32[]{:S(2)}) copy-start(f32[384]{0:T(512)} %second_bias.1) | copy-start | bytes 4612
  28.1 1.5 %collective-permute-start.2 = (f32[128,384]{1,0:T(8,128)S(1)}, f32[128,384]{1,0:T(8,128)S(1)}, u32[]{:S(2)}, u32[]{:S(2)}) collective-permute-start(f32[128,384]{1,0:T(8,128)S(1)} %bitcast.12), channel_id=1, source_target_pairs={{0,16},{16,0},{1,17},{17,1},{2,18},{18,2},{3,19},{19,3},{4,20},{20... | collective-permute-start | bytes 589832 | tf_op jit(solution)/shard_map/ppermute | solution.py:293

commit v4 on v3

--- a/solution.py
+++ b/solution.py
@@ -1,3 +1,4 @@
+import functools
 import math
 
 import jax
@@ -128,16 +129,20 @@
         base = held[1].astype(F32)
         diff = held[0].astype(F32) - base
         field = (base + mix * diff).astype(BF16)
-        for i, values in enumerate((field, held[2])):
-            moved = jnp.dot(order, values, preferred_element_type=F32)
-            sent[:, i * part : (i + 1) * part, :] = moved.reshape(NEAR * NEAR, part, depth).astype(BF16)
+        moved = jnp.dot(order, field, preferred_element_type=F32)
+        sent[:, :part, :] = moved.reshape(NEAR * NEAR, part, depth).astype(BF16)
+        moved = jnp.dot(order, held[2], preferred_element_type=F32).reshape(NEAR * NEAR, points, part // points, depth)
+        own = moved[:, 0]
+        for k in range(1, points):
+            own = jnp.where(mine == k, moved[:, k], own)
+        sent[:, part:, :] = own.astype(BF16)
         half = pl.ds(pl.multiple_of(mine * (cells // points), cells // points), cells // points)
         own = held[1, half, :].astype(F32)
         diff_rows[...] = (held[0, half, :].astype(F32) - own) * (1 / points)
 
     return call(
         kernel,
-        [((NEAR * NEAR, 2 * part, depth), BF16), ((cells // points, depth), F32)],
+        [((NEAR * NEAR, part + part // points, depth), BF16), ((cells // points, depth), F32)],
         [pltpu.VMEM((3, cells, depth), BF16), pltpu.SemaphoreType.DMA((3,))],
         "pack_classes",
         8,
@@ -147,107 +152,136 @@
     )
 
 
-def adjoint_of_class(got, first_halves, first_bias, second_halves, second_bias, sizes):
+def class_tools(sizes, depth, edged):
     group_lon, group_lat, row_part, col_part = sizes
-    points = lax.axis_size("path")
-    depth = got.shape[-1]
     rows, cols = group_lon * row_part, group_lat * col_part
-    cells, part = rows * cols, row_part * col_part
-    span = row_part // points
+    cells = rows * cols
+
+    def spread(values, step, at, target):
+        span = slice(at, at + values.shape[1])
+        edged[:, EDGE : EDGE + rows, span] = values.reshape(cols, rows, -1)
+        for i in range(3):
+            start = EDGE + (i - 1) * step
+            shifted = edged[:, start : start + rows, span].reshape(cells, -1)
+            target[:, i * depth + at : i * depth + at + values.shape[1]] = shifted.astype(BF16)
+
+    def stencil_part(source, weights, step, at, end, forward):
+        def weigh(values, col):
+            if forward:
+                blocks = [part[i, col, :, at:end] for i in range(3) for part in weights]
+                return jnp.dot(values, jnp.concatenate(blocks, axis=0), preferred_element_type=F32)
+            taps_of = [jnp.concatenate([part[2 - i, 2 - col] for part in weights], axis=0)[at:end] for i in range(3)]
+            return lax.dot_general(
+                values, jnp.concatenate(taps_of, axis=1), (((1,), (1,)), ((), ())), preferred_element_type=F32
+            )
+
+        shift = step * rows
+        fill = jnp.zeros((shift, end - at), F32)
+        same = weigh(source[...], 1)
+        after = weigh(source[shift:, :], 2)
+        before = weigh(source[: cells - shift, :], 0)
+        return same + jnp.concatenate([after, fill], axis=0) + jnp.concatenate([fill, before], axis=0)
+
+    edged[:, :EDGE, :] = jnp.zeros((cols, EDGE, depth), F32)
+    edged[:, EDGE + rows :, :] = jnp.zeros((cols, EDGE, depth), F32)
+    return spread, stencil_part
+
+
+def by_place(points, run, *halves):
+    for place in range(points):
+        owners = [(place - k) % points for k in range(points)]
+        lists = [[parts[k] for k in owners] for parts in halves]
+        pl.when(lax.axis_index("path") == place)(functools.partial(run, place, *lists))
+
+
+def channel_parts(depth):
+    return [(at, min(at + 2 * LANES, depth)) for at in range(0, depth, 2 * LANES)]
+
+
+def slopes_of_class(got, first_halves, first_bias, second_halves, second_bias, sizes):
+    group_lon, group_lat, row_part, col_part = sizes
+    points, depth = len(first_halves), got.shape[-1]
+    rows, cols, part = group_lon * row_part, group_lat * col_part, row_part * col_part
+    cells = rows * cols
 
     def kernel(got, first_bias, second_bias, *refs):
-        mine = lax.axis_index("path")
-        for owner in range(points):
-            inputs = [(owner - k) % points for k in range(points)]
-            first, second = ([refs[j * points + k] for k in inputs] for j in range(2))
-            pl.when(mine == owner)(lambda: run(owner, got, first, first_bias, second, second_bias, *refs[2 * points :]))
-
-    def run(mine, got, first, first_bias, second, second_bias, kept, sent, edged, taps, slope, grad, laned):
-        order = ordering((group_lon, group_lat, row_part, col_part), (1, 3, 0, 2))
-
-        def tap_weight(parts, row, col):
-            return jnp.concatenate([part[row, col] for part in parts], axis=0)
-
-        def spread(values, step):
-            edged[:, EDGE : EDGE + rows, :] = values.reshape(cols, rows, depth)
-            for i in range(3):
-                start = EDGE + (i - 1) * step
-                taps[:, i * depth : (i + 1) * depth] = (
-                    edged[:, start : start + rows, :].reshape(cells, depth).astype(BF16)
-                )
-
-        def both_sides(weigh, step):
-            shift = step * rows
-            fill = jnp.zeros((shift, depth), F32)
-            same = weigh(taps[...], 1)
-            after = weigh(taps[shift:, :], 2)
-            before = weigh(taps[: cells - shift, :], 0)
-            return same + jnp.concatenate([after, fill], axis=0) + jnp.concatenate([fill, before], axis=0)
-
-        def forward(weights, step):
-            def weigh(values, col):
-                column = jnp.concatenate([tap_weight(weights, i, col) for i in range(3)], axis=0)
-                return jnp.dot(values, column, preferred_element_type=F32)
-
-            return both_sides(weigh, step)
-
-        def backward(weights, step):
-            def weigh(values, col):
-                total = None
-                for i in range(3):
-                    term = lax.dot_general(
-                        values[:, i * depth : (i + 1) * depth],
-                        tap_weight(weights, 2 - i, 2 - col),
-                        (((1,), (1,)), ((), ())),
-                        preferred_element_type=F32,
-                    )
-                    total = term if total is None else total + term
-                return total
-
-            return both_sides(weigh, step)
-
-        edged[:, :EDGE, :] = jnp.zeros((cols, EDGE, depth), F32)
-        edged[:, EDGE + rows :, :] = jnp.zeros((cols, EDGE, depth), F32)
-        field, upstream = (
-            jnp.dot(order, got[:, i * part : (i + 1) * part, :].reshape(cells, depth), preferred_element_type=F32)
-            for i in range(2)
-        )
-        spread(field, 1)
-        act, slope[...] = gelu_and_slope(forward(first, 1) + first_bias[...].reshape(1, depth))
-        spread(field + act, FAR // NEAR)
-        second_pre = forward(second, FAR // NEAR) + second_bias[...].reshape(1, depth)
-        spread(gelu_and_slope(second_pre)[1] * upstream, FAR // NEAR)
-        hidden_adj = upstream + backward(second, FAR // NEAR)
-        grad[...] = hidden_adj
-        spread(slope[...] * hidden_adj, 1)
-        grad[...] += backward(first, 1)
-        for b in range(depth // LANES):
-            laned[b] = grad[:, b * LANES : (b + 1) * LANES].reshape(cols, rows, LANES)
-        for k in range(points):
-            owner = (mine + k) % points
-            for i in range(span):
+        first_slope, second_slope, edged, near_taps, far_taps = refs[2 * points :]
+
+        def run(place, first, second):
+            spread, stencil_part = class_tools(sizes, depth, edged)
+            order = ordering((group_lon, group_lat, row_part, col_part), (1, 3, 0, 2))
+            field = jnp.dot(order, got[:, :part, :].reshape(cells, depth), preferred_element_type=F32)
+            spread(field, 1, 0, near_taps)
+            for at, end in channel_parts(depth):
+                pre = stencil_part(near_taps, first, 1, at, end, True) + first_bias[at:end].reshape(1, -1)
+                act, first_slope[:, at:end] = gelu_and_slope(pre)
+                spread(field[:, at:end] + act, FAR // NEAR, at, far_taps)
+            for at, end in channel_parts(depth):
+                pre = stencil_part(far_taps, second, FAR // NEAR, at, end, True) + second_bias[at:end].reshape(1, -1)
+                second_slope[:, at:end] = gelu_and_slope(pre)[1]
+
+        by_place(points, run, refs[:points], refs[points : 2 * points])
+
+    return call(
+        kernel,
+        [((cells, depth), F32)] * 2,
+        [pltpu.VMEM((cols, rows + 2 * EDGE, depth), F32)] + [pltpu.VMEM((cells, 3 * depth), BF16)] * 2,
+        "slopes_of_class",
+        16,
+        got,
+        first_bias,
+        second_bias,
+        *first_halves,
+        *second_halves,
+    )
+
+
+def adjoint_of_class(cotangents, first_slope, second_slope, first_halves, second_halves, sizes):
+    group_lon, group_lat, row_part, col_part = sizes
+    points, depth = len(first_halves), first_slope.shape[-1]
+    rows, cols = group_lon * row_part, group_lat * col_part
+    cells, span = rows * cols, row_part // points
+
+    def kernel(first_slope, second_slope, *refs):
+        kept, sent, edged, near_taps, far_taps, grad, laned = refs[3 * points :]
+
+        def run(place, cotangent, first, second):
+            spread, stencil_part = class_tools(sizes, depth, edged)
+            order = ordering((group_lon, group_lat, row_part, col_part), (1, 3, 0, 2))
+            upstream = jnp.concatenate([share[...].astype(F32) for share in cotangent], axis=1)
+            upstream = jnp.dot(order, upstream.reshape(cells, depth).astype(BF16), preferred_element_type=F32)
+            spread(second_slope[...] * upstream, FAR // NEAR, 0, far_taps)
+            for at, end in channel_parts(depth):
+                hidden_adj = upstream[:, at:end] + stencil_part(far_taps, second, FAR // NEAR, at, end, False)
+                grad[:, at:end] = hidden_adj
+                spread(first_slope[:, at:end] * hidden_adj, 1, at, near_taps)
+            for at, end in channel_parts(depth):
+                grad[:, at:end] += stencil_part(near_taps, first, 1, at, end, False)
+                for b in range(at // LANES, end // LANES):
+                    laned[b] = grad[:, b * LANES : (b + 1) * LANES].reshape(cols, rows, LANES)
+            for k in range(points):
+                owner = (place + k) % points
                 target = kept if k == 0 else sent.at[k - 1]
-                place = slice(i * (cells // row_part), (i + 1) * (cells // row_part))
-                for b in range(depth // LANES):
-                    rows_of = laned[b, :, pl.ds(owner * span + i, group_lon, stride=row_part), :]
-                    target[place, b * LANES : (b + 1) * LANES] = rows_of.reshape(-1, LANES)
+                for i in range(span):
+                    here = slice(i * (cells // row_part), (i + 1) * (cells // row_part))
+                    for b in range(depth // LANES):
+                        rows_of = laned[b, :, pl.ds(owner * span + i, group_lon, stride=row_part), :]
+                        target[here, b * LANES : (b + 1) * LANES] = rows_of.reshape(-1, LANES)
+
+        by_place(points, run, refs[:points], refs[points : 2 * points], refs[2 * points : 3 * points])
 
     share = cells // points
     return call(
         kernel,
         [((share, depth), F32), ((points - 1, share, depth), F32)],
-        [
-            pltpu.VMEM((cols, rows + 2 * EDGE, depth), F32),
-            pltpu.VMEM((cells, 3 * depth), BF16),
-            pltpu.VMEM((cells, depth), F32),
-            pltpu.VMEM((cells, depth), F32),
-            pltpu.VMEM((depth // LANES, cols, rows, LANES), F32),
-        ],
+        [pltpu.VMEM((cols, rows + 2 * EDGE, depth), F32)]
+        + [pltpu.VMEM((cells, 3 * depth), BF16)] * 2
+        + [pltpu.VMEM((cells, depth), F32), pltpu.VMEM((depth // LANES, cols, rows, LANES), F32)],
         "adjoint_of_class",
-        24,
-        got,
-        first_bias,
-        second_bias,
+        16,
+        first_slope,
+        second_slope,
+        *cotangents,
         *first_halves,
         *second_halves,
     )
@@ -299,7 +333,10 @@
     ]
     sent, diff_rows = pack_classes(observed, baseline, cotangent)
     got = swap(sent)
-    kept, others = adjoint_of_class(got, halves[0], first_bias, halves[1], second_bias, sizes)
+    own = got[:, sizes[2] * sizes[3] :, :]
+    cotangents = [own] + [turned(own, step) for step in range(1, points)]
+    first_slope, second_slope = slopes_of_class(got, halves[0], first_bias, halves[1], second_bias, sizes)
+    kept, others = adjoint_of_class(cotangents, first_slope, second_slope, *halves, sizes)
     others = [turned(others[step - 1], step) for step in range(1, points)]
     home = swap(total_for_homes(kept, others, sizes))
     return attribution_rows(home, diff_rows, rows // points, cols)

time: 41.9 us -> 39.8 us (0.950)
  blocking collectives: 32 us -> 29.9 us
  starting transfers between devices: 0.58 us -> 1.12 us
    all_to_all x2, blocking collectives: 32 us -> 29.9 us  [swap(): return lax.all_to_all(chunks, ('lon', 'lat'), 0, 0, tiled=True)]
    ppermute x3 -> x4, starting transfers between devices: 0.58 us -> 1.12 us  [turned(): lax.ppermute(values, 'path', [(i, (i + step) % points) for i in range(poi...]
    ppermute x3 -> x4, waiting for transfers between devices: 1.43 us -> 1.08 us  [turned(): lax.ppermute(values, 'path', [(i, (i + step) % points) for i in range(poi...]
    pallas_call x4 -> x5, Pallas kernels: 6.99 us -> 6.76 us  [call(): pl.pallas_call(kernel, out_shape=[pltpu.VMEM(shape, dtype) for shape, dty...]
  transfers between devices with their start and end apart: 3 -> 4, of which waited for: 1 -> 1; matrix products, arithmetic and copies ran while one was open for 0% -> 0% of each run, Pallas kernels for 4% -> 10%
where the time goes in v4:
time: 39.8 us; the launch traced here: 39.6 us
  blocking collectives  29.9 us (75%)
  Pallas kernels  6.76 us (17%)
  starting transfers between devices  1.12 us (3%)
  waiting for transfers between devices  1.08 us (3%)
  local copies, waits for them, and re-layouts  0.67 us (2%)
    all_to_all x2, blocking collectives, swap(): return lax.all_to_all(chunks, ('lon', 'lat'), 0, 0, tiled=True)  29.9 us
    pallas_call x5, Pallas kernels, call(): pl.pallas_call(kernel, out_shape=[pltpu.VMEM(shape, dtype) for shape, dty...  6.76 us
    ppermute x4, starting transfers between devices, turned(): lax.ppermute(values, 'path', [(i, (i + step) % points) for i in range(poi...  1.12 us
    ppermute x4, waiting for transfers between devices, turned(): lax.ppermute(values, 'path', [(i, (i + step) % points) for i in range(poi...  1.08 us
  transfers between devices with their start and end apart: 4, of which 1 were waited for; matrix products, arithmetic and copies ran while one was open for 0% of the time, Pallas kernels for 10%

profile of v4, /device:TPU:0, one launch (start us, length us, event | category | flops | bytes accessed | tf_op | source)
XLA Modules:
  0.0 39.6 jit_solution(14843277872851569136)
XLA Ops:
  0.0 0.5 %collective-permute-start = (bf16[9,192,384]{2,1,0:T(8,128)(2,1)}, bf16[9,192,384]{2,1,0:T(8,128)(2,1)S(1)}, u32[]{:S(2)}, u32[]{:S(2)}) collective-permute-start(bf16[9,192,384]{2,1,0:T(8,128)(2,1)} %param.10), channel_id=1, source_target_pairs={{0,16},{16,0},{1,17},{17,1},{2,18},{18,2},{3,19},{19,3},{4,20},{20... | collective-permute-start | bytes 3981320 | tf_op jit(solution)/shard_map/ppermute | solution.py:327
  0.5 0.1 collective-permute-start.1
  0.5 0.0 copy-start
  0.5 0.0 copy-start.1
  0.5 0.0 copy-start.2
  0.5 0.0 copy-start.3
  0.5 1.7 %pack_classes.1 = (bf16[16,24,384]{2,1,0:T(8,128)(2,1)S(1)}, f32[128,384]{1,0:T(8,128)S(1)}) custom-call(bf16[256,384]{1,0:T(8,128)(2,1)} %bitcast.17, bf16[256,384]{1,0:T(8,128)(2,1)} %bitcast.18, bf16[256,384]{1,0:T(8,128)(2,1)} %bitcast.19), custom_call_target="tpu_custom_call" | custom-call | flops 4000000000 | bytes 589824 | tf_op jit(solution)/shard_map/pack_classes/pallas_call | solution.py:100
  2.2 19.0 %all_to_all.10.got = bf16[16,24,384]{2,1,0:T(8,128)(2,1)S(1)} all-to-all(bf16[16,24,384]{2,1,0:T(8,128)(2,1)S(1)} %get-tuple-element.11), channel_id=1, replica_groups=mesh['path'=2,'lon'=8,'lat'=2] {'lon','lat'}, dimensions={0} | all-to-all | bytes 589824 | tf_op jit(solution)/shard_map/all_to_all | solution.py:37
  21.2 0.1 collective-permute-start.2
  21.3 0.0 collective-permute-done
  21.3 0.0 collective-permute-done.1
  21.3 0.0 copy-done
  21.3 0.0 copy-done.1
  21.3 0.0 copy-done.2
  21.3 0.0 copy-done.3
  21.3 2.4 %slopes_of_class.1 = (f32[256,384]{1,0:T(8,128)S(1)}, f32[256,384]{1,0:T(8,128)S(1)}) custom-call(bf16[16,24,384]{2,1,0:T(8,128)(2,1)S(1)} %all_to_all.10.got, f32[384]{0:T(512)S(1)} %copy-done.2, f32[384]{0:T(512)S(1)} %copy-done.3, bf16[3,3,192,384]{3,2,1,0:T(8,128)(2,1)S(1)} %bitcast.8, bf16[3,3,192,384]{3,2,1,0:T(8,128)(2,1)S(1)} %bitcast.12, ...), custom_call_target="tpu_custom_call" | custom-call | bytes 5606400 | tf_op jit(solution)/shard_map/slopes_of_class/pallas_call | solution.py:100
  23.7 0.0 collective-permute-done.2.refs_1_
  23.7 2.4 %adjoint_of_class.1 = (f32[128,384]{1,0:T(8,128)S(1)}, f32[1,128,384]{2,1,0:T(8,128)S(1)}) custom-call(f32[256,384]{1,0:T(8,128)S(1)} %get-tuple-element.12.first_slope, f32[256,384]{1,0:T(8,128)S(1)} %get-tuple-element.13.second_slope, bf16[16,8,384]{2,1,0:T(8,128)(2,1)S(1)} %slice.4.refs_0_, bf16[16,8,384]{2,1,0:T(8,128)(2,1)S(1)} %collective-permute-done.2.refs_1_, ...), custom_call_target="tpu_custom_call" | custom-call | bytes 6291456 | tf_op jit(solution)/shard_map/adjoint_of_class/pallas_call | solution.py:100
  26.1 0.5 %collective-permute-start.3 = (f32[128,384]{1,0:T(8,128)S(1)}, f32[128,384]{1,0:T(8,128)S(1)}, u32[]{:S(2)}, u32[]{:S(2)}) collective-permute-start(f32[128,384]{1,0:T(8,128)S(1)} %bitcast.16), channel_id=1, source_target_pairs={{0,16},{16,0},{1,17},{17,1},{2,18},{18,2},{3,19},{19,3},{4,20},{20... | collective-permute-start | bytes 589832 | tf_op jit(solution)/shard_map/ppermute | solution.py:327
  26.6 1.1 %collective-permute-done.3.refs_0_ = f32[128,384]{1,0:T(8,128)S(1)} collective-permute-done((f32[128,384]{1,0:T(8,128)S(1)}, f32[128,384]{1,0:T(8,128)S(1)}, u32[]{:S(2)}, u32[]{:S(2)}) %collective-permute-start.3) | collective-permute-done | bytes 196640 | tf_op jit(solution)/shard_map/ppermute | solution.py:327
  27.7 0.2 total_for_homes.1
  27.9 10.9 %all_to_all.11.home = bf16[16,8,384]{2,1,0:T(8,128)(2,1)S(1)} all-to-all(bf16[16,8,384]{2,1,0:T(8,128)(2,1)S(1)} %total_for_homes.1), channel_id=1, replica_groups=mesh['path'=2,'lon'=8,'lat'=2] {'lon','lat'}, dimensions={0} | all-to-all | bytes 196608 | tf_op jit(solution)/shard_map/all_to_all | solution.py:37
  38.8 0.2 attribution_rows.1
  39.0 0.6 %copy.8 = bf16[8,16,384]{2,1,0:T(8,128)(2,1)} copy(bf16[8,16,384]{2,1,0:T(8,128)(2,1)S(1)} %attribution_rows.1) | data formatting | bytes 196608
  (1 shorter events, 0.0 us)
Async XLA Ops:
  0.0 21.3 %collective-permute-start = (bf16[9,192,384]{2,1,0:T(8,128)(2,1)}, bf16[9,192,384]{2,1,0:T(8,128)(2,1)S(1)}, u32[]{:S(2)}, u32[]{:S(2)}) collective-permute-start(bf16[9,192,384]{2,1,0:T(8,128)(2,1)} %param.10), channel_id=1, source_target_pairs={{0,16},{16,0},{1,17},{17,1},{2,18},{18,2},{3,19},{19,3},{4,20},{20... | collective-permute-start | bytes 3981320 | tf_op jit(solution)/shard_map/ppermute | solution.py:327
  0.5 20.8 %collective-permute-start.1 = (bf16[9,192,384]{2,1,0:T(8,128)(2,1)}, bf16[9,192,384]{2,1,0:T(8,128)(2,1)S(1)}, u32[]{:S(2)}, u32[]{:S(2)}) collective-permute-start(bf16[9,192,384]{2,1,0:T(8,128)(2,1)} %param.12), channel_id=1, source_target_pairs={{0,16},{16,0},{1,17},{17,1},{2,18},{18,2},{3,19},{19,3},{4,20},{20... | collective-permute-start | bytes 3981320 | tf_op jit(solution)/shard_map/ppermute | solution.py:327
  0.5 20.8 %copy-start = (bf16[9,192,384]{2,1,0:T(8,128)(2,1)S(1)}, bf16[9,192,384]{2,1,0:T(8,128)(2,1)}, u32[]{:S(2)}) copy-start(bf16[9,192,384]{2,1,0:T(8,128)(2,1)} %param.10) | copy-start | bytes 3981316
  0.5 20.8 %copy-start.1 = (bf16[9,192,384]{2,1,0:T(8,128)(2,1)S(1)}, bf16[9,192,384]{2,1,0:T(8,128)(2,1)}, u32[]{:S(2)}) copy-start(bf16[9,192,384]{2,1,0:T(8,128)(2,1)} %param.12) | copy-start | bytes 3981316
  0.5 20.8 %copy-start.2 = (f32[384]{0:T(512)S(1)}, f32[384]{0:T(512)}, u32[]{:S(2)}) copy-start(f32[384]{0:T(512)} %first_bias.1) | copy-start | bytes 4612
  0.5 20.8 %copy-start.3 = (f32[384]{0:T(512)S(1)}, f32[384]{0:T(512)}, u32[]{:S(2)}) copy-start(f32[384]{0:T(512)} %second_bias.1) | copy-start | bytes 4612
  21.2 2.5 %collective-permute-start.2 = (bf16[16,8,384]{2,1,0:T(8,128)(2,1)S(1)}, bf16[16,8,384]{2,1,0:T(8,128)(2,1)S(1)}, u32[]{:S(2)}, u32[]{:S(2)}) collective-permute-start(bf16[16,8,384]{2,1,0:T(8,128)(2,1)S(1)} %slice.4.refs_0_), channel_id=1, source_target_pairs={{0,16},{16,0},{1,17},{17,1},{2,18},{18,2},{3,19},{19,3},{4,20},{20... | collective-permute-start | bytes 294920 | tf_op jit(solution)/shard_map/ppermute | solution.py:327
  26.1 1.6 %collective-permute-start.3 = (f32[128,384]{1,0:T(8,128)S(1)}, f32[128,384]{1,0:T(8,128)S(1)}, u32[]{:S(2)}, u32[]{:S(2)}) collective-permute-start(f32[128,384]{1,0:T(8,128)S(1)} %bitcast.16), channel_id=1, source_target_pairs={{0,16},{16,0},{1,17},{17,1},{2,18},{18,2},{3,19},{19,3},{4,20},{20... | collective-permute-start | bytes 589832 | tf_op jit(solution)/shard_map/ppermute | solution.py:327

commit v5 on v4

--- a/solution.py
+++ b/solution.py
@@ -14,7 +14,6 @@
 LANES = 128
 F32, BF16 = jnp.float32, jnp.bfloat16
 VMEM = pl.BlockSpec(memory_space=pltpu.VMEM)
-HBM = pl.BlockSpec(memory_space=pltpu.HBM)
 
 def smooth_act(value):
     return jax.nn.gelu(value, approximate=True)
@@ -109,45 +108,47 @@
     )(*args)
 
 
-def pack_classes(observed, baseline, cotangent):
+def row_orders(rows, cols, sizes):
+    group_lon, group_lat, row_part, col_part = sizes
+    cells = rows * cols
+
+    def kernel(to_classes, to_grid):
+        to_classes[...] = ordering((row_part, NEAR, col_part, NEAR), (1, 3, 0, 2))
+        to_grid[...] = ordering((group_lon, group_lat, row_part, col_part), (1, 3, 0, 2))
+
+    return call(kernel, [((cells, cells), BF16)] * 2, [], "row_orders", 4, flops=4 * 10**9)
+
+
+def pack_classes(order, observed, baseline, cotangent):
     rows, cols, depth = observed.shape
-    points, point = lax.axis_size("path"), lax.axis_index("path")
+    points = lax.axis_size("path")
     cells, part = rows * cols, rows * cols // (NEAR * NEAR)
 
-    def kernel(observed, baseline, cotangent, sent, diff_rows, held, sems):
-        copies = [
-            pltpu.make_async_copy(ref, held.at[i], sems.at[i])
-            for i, ref in enumerate((observed, baseline, cotangent))
-        ]
-        for copy in copies:
-            copy.start()
-        order = ordering((rows // NEAR, NEAR, cols // NEAR, NEAR), (1, 3, 0, 2))
-        for copy in copies:
-            copy.wait()
+    def kernel(order, observed, baseline, cotangent, sent, diff_rows):
         mine = lax.axis_index("path")
         mix = (mine.astype(F32) + 0.5) / points
-        base = held[1].astype(F32)
-        diff = held[0].astype(F32) - base
+        base = baseline[...].astype(F32)
+        diff = observed[...].astype(F32) - base
         field = (base + mix * diff).astype(BF16)
-        moved = jnp.dot(order, field, preferred_element_type=F32)
+        moved = jnp.dot(order[...], field, preferred_element_type=F32)
         sent[:, :part, :] = moved.reshape(NEAR * NEAR, part, depth).astype(BF16)
-        moved = jnp.dot(order, held[2], preferred_element_type=F32).reshape(NEAR * NEAR, points, part // points, depth)
+        moved = jnp.dot(order[...], cotangent[...], preferred_element_type=F32)
+        moved = moved.reshape(NEAR * NEAR, points, part // points, depth)
         own = moved[:, 0]
         for k in range(1, points):
             own = jnp.where(mine == k, moved[:, k], own)
         sent[:, part:, :] = own.astype(BF16)
         half = pl.ds(pl.multiple_of(mine * (cells // points), cells // points), cells // points)
-        own = held[1, half, :].astype(F32)
-        diff_rows[...] = (held[0, half, :].astype(F32) - own) * (1 / points)
+        diff_rows[...] = (observed[half, :].astype(F32) - baseline[half, :].astype(F32)) * (1 / points)
 
     return call(
         kernel,
         [((NEAR * NEAR, part + part // points, depth), BF16), ((cells // points, depth), F32)],
-        [pltpu.VMEM((3, cells, depth), BF16), pltpu.SemaphoreType.DMA((3,))],
+        [],
         "pack_classes",
         8,
+        order,
         *(x.reshape(cells, depth) for x in (observed, baseline, cotangent)),
-        specs=[HBM] * 3,
         flops=4 * 10**9,
     )
 
@@ -198,19 +199,18 @@
     return [(at, min(at + 2 * LANES, depth)) for at in range(0, depth, 2 * LANES)]
 
 
-def slopes_of_class(got, first_halves, first_bias, second_halves, second_bias, sizes):
+def slopes_of_class(order, got, first_halves, first_bias, second_halves, second_bias, sizes):
     group_lon, group_lat, row_part, col_part = sizes
     points, depth = len(first_halves), got.shape[-1]
     rows, cols, part = group_lon * row_part, group_lat * col_part, row_part * col_part
     cells = rows * cols
 
-    def kernel(got, first_bias, second_bias, *refs):
+    def kernel(order, got, first_bias, second_bias, *refs):
         first_slope, second_slope, edged, near_taps, far_taps = refs[2 * points :]
 
         def run(place, first, second):
             spread, stencil_part = class_tools(sizes, depth, edged)
-            order = ordering((group_lon, group_lat, row_part, col_part), (1, 3, 0, 2))
-            field = jnp.dot(order, got[:, :part, :].reshape(cells, depth), preferred_element_type=F32)
+            field = jnp.dot(order[...], got[:, :part, :].reshape(cells, depth), preferred_element_type=F32)
             spread(field, 1, 0, near_taps)
             for at, end in channel_parts(depth):
                 pre = stencil_part(near_taps, first, 1, at, end, True) + first_bias[at:end].reshape(1, -1)
@@ -228,6 +228,7 @@
         [pltpu.VMEM((cols, rows + 2 * EDGE, depth), F32)] + [pltpu.VMEM((cells, 3 * depth), BF16)] * 2,
         "slopes_of_class",
         16,
+        order,
         got,
         first_bias,
         second_bias,
@@ -236,20 +237,19 @@
     )
 
 
-def adjoint_of_class(cotangents, first_slope, second_slope, first_halves, second_halves, sizes):
+def adjoint_of_class(order, cotangents, first_slope, second_slope, first_halves, second_halves, sizes):
     group_lon, group_lat, row_part, col_part = sizes
     points, depth = len(first_halves), first_slope.shape[-1]
     rows, cols = group_lon * row_part, group_lat * col_part
     cells, span = rows * cols, row_part // points
 
-    def kernel(first_slope, second_slope, *refs):
+    def kernel(order, first_slope, second_slope, *refs):
         kept, sent, edged, near_taps, far_taps, grad, laned = refs[3 * points :]
 
         def run(place, cotangent, first, second):
             spread, stencil_part = class_tools(sizes, depth, edged)
-            order = ordering((group_lon, group_lat, row_part, col_part), (1, 3, 0, 2))
             upstream = jnp.concatenate([share[...].astype(F32) for share in cotangent], axis=1)
-            upstream = jnp.dot(order, upstream.reshape(cells, depth).astype(BF16), preferred_element_type=F32)
+            upstream = jnp.dot(order[...], upstream.reshape(cells, depth).astype(BF16), preferred_element_type=F32)
             spread(second_slope[...] * upstream, FAR // NEAR, 0, far_taps)
             for at, end in channel_parts(depth):
                 hidden_adj = upstream[:, at:end] + stencil_part(far_taps, second, FAR // NEAR, at, end, False)
@@ -279,6 +279,7 @@
         + [pltpu.VMEM((cells, depth), F32), pltpu.VMEM((depth // LANES, cols, rows, LANES), F32)],
         "adjoint_of_class",
         16,
+        order,
         first_slope,
         second_slope,
         *cotangents,
@@ -331,12 +332,13 @@
         [x.reshape((side, side) + x.shape[1:]) for x in [part] + [turned(part, step) for step in range(1, points)]]
         for part in (first_weight, second_weight)
     ]
-    sent, diff_rows = pack_classes(observed, baseline, cotangent)
+    to_classes, to_grid = row_orders(rows, cols, sizes)
+    sent, diff_rows = pack_classes(to_classes, observed, baseline, cotangent)
     got = swap(sent)
     own = got[:, sizes[2] * sizes[3] :, :]
     cotangents = [own] + [turned(own, step) for step in range(1, points)]
-    first_slope, second_slope = slopes_of_class(got, halves[0], first_bias, halves[1], second_bias, sizes)
-    kept, others = adjoint_of_class(cotangents, first_slope, second_slope, *halves, sizes)
+    first_slope, second_slope = slopes_of_class(to_grid, got, halves[0], first_bias, halves[1], second_bias, sizes)
+    kept, others = adjoint_of_class(to_grid, cotangents, first_slope, second_slope, *halves, sizes)
     others = [turned(others[step - 1], step) for step in range(1, points)]
     home = swap(total_for_homes(kept, others, sizes))
     return attribution_rows(home, diff_rows, rows // points, cols)

time: 39.8 us -> 39.1 us (0.982)
  Pallas kernels: 6.76 us -> 5.6 us
    pallas_call x5 -> x6, Pallas kernels: 6.76 us -> 5.6 us  [call(): pl.pallas_call(kernel, out_shape=[pltpu.VMEM(shape, dtype) for shape, dty...]
    unnamed x9 -> x15, local copies, waits for them, and re-layouts: 0.66 us -> 1 us
  transfers between devices with their start and end apart: 4 -> 4, of which waited for: 1 -> 1; matrix products, arithmetic and copies ran while one was open for 0% -> 0% of each run, Pallas kernels for 10% -> 7%
where the time goes in v5:
time: 39.1 us; the launch traced here: 38.9 us
  blocking collectives  29.8 us (76%)
  Pallas kernels  5.6 us (14%)
  starting transfers between devices  1.22 us (3%)
  waiting for transfers between devices  1.08 us (3%)
  local copies, waits for them, and re-layouts  1.01 us (3%)
    all_to_all x2, blocking collectives, swap(): return lax.all_to_all(chunks, ('lon', 'lat'), 0, 0, tiled=True)  29.8 us
    pallas_call x6, Pallas kernels, call(): pl.pallas_call(kernel, out_shape=[pltpu.VMEM(shape, dtype) for shape, dty...  5.6 us
    ppermute x4, starting transfers between devices, turned(): lax.ppermute(values, 'path', [(i, (i + step) % points) for i in range(poi...  1.22 us
    ppermute x4, waiting for transfers between devices, turned(): lax.ppermute(values, 'path', [(i, (i + step) % points) for i in range(poi...  1.08 us
    unnamed x15, local copies, waits for them, and re-layouts  1 us
  transfers between devices with their start and end apart: 4, of which 1 were waited for; matrix products, arithmetic and copies ran while one was open for 0% of the time, Pallas kernels for 7%

profile of v5, /device:TPU:0, one launch (start us, length us, event | category | flops | bytes accessed | tf_op | source)
XLA Modules:
  0.0 38.9 jit_solution(11616085767414981251)
XLA Ops:
  0.0 0.0 copy-start.6
  0.0 0.0 copy-start.5
  0.0 0.0 copy-start.4
  0.0 0.5 %collective-permute-start = (bf16[9,192,384]{2,1,0:T(8,128)(2,1)}, bf16[9,192,384]{2,1,0:T(8,128)(2,1)S(1)}, u32[]{:S(2)}, u32[]{:S(2)}) collective-permute-start(bf16[9,192,384]{2,1,0:T(8,128)(2,1)} %param.10), channel_id=1, source_target_pairs={{0,16},{16,0},{1,17},{17,1},{2,18},{18,2},{3,19},{19,3},{4,20},{20... | collective-permute-start | bytes 3981320 | tf_op jit(solution)/shard_map/ppermute | solution.py:328
  0.5 0.1 collective-permute-start.1
  0.6 0.2 row_orders.1
  0.8 0.1 copy-done.6
  0.9 0.1 copy-done.5
  1.0 0.1 copy-done.4
  1.1 0.0 copy-start
  1.1 0.0 copy-start.1
  1.1 0.0 copy-start.2
  1.1 0.0 copy-start.3
  1.1 0.3 pack_classes.1
  1.5 18.9 %all_to_all.10.got = bf16[16,24,384]{2,1,0:T(8,128)(2,1)S(1)} all-to-all(bf16[16,24,384]{2,1,0:T(8,128)(2,1)S(1)} %get-tuple-element.15), channel_id=1, replica_groups=mesh['path'=2,'lon'=8,'lat'=2] {'lon','lat'}, dimensions={0} | all-to-all | bytes 589824 | tf_op jit(solution)/shard_map/all_to_all | solution.py:36
  20.4 0.1 collective-permute-start.2
  20.5 0.0 collective-permute-done
  20.5 0.0 collective-permute-done.1
  20.5 0.0 copy-done
  20.5 0.0 copy-done.1
  20.5 0.0 copy-done.2
  20.5 0.0 copy-done.3
  20.5 2.4 %slopes_of_class.1 = (f32[256,384]{1,0:T(8,128)S(1)}, f32[256,384]{1,0:T(8,128)S(1)}) custom-call(bf16[256,256]{1,0:T(8,128)(2,1)S(1)} %get-tuple-element.13.order, bf16[16,24,384]{2,1,0:T(8,128)(2,1)S(1)} %all_to_all.10.got, f32[384]{0:T(512)S(1)} %copy-done.2, f32[384]{0:T(512)S(1)} %copy-done.3, bf16[3,3,192,384]{3,2,1,0:T(8,128)(2,1)S(1)} %bitcast.8, ...), custom_call_target="tpu_custom_call" | custom-call | bytes 5737472 | tf_op jit(solution)/shard_map/slopes_of_class/pallas_call | solution.py:99
  22.9 0.0 collective-permute-done.2.refs_1_
  23.0 2.4 %adjoint_of_class.1 = (f32[128,384]{1,0:T(8,128)S(1)}, f32[1,128,384]{2,1,0:T(8,128)S(1)}) custom-call(bf16[256,256]{1,0:T(8,128)(2,1)S(1)} %get-tuple-element.13.order, f32[256,384]{1,0:T(8,128)S(1)} %get-tuple-element.16.first_slope, f32[256,384]{1,0:T(8,128)S(1)} %get-tuple-element.17.second_slope, bf16[16,8,384]{2,1,0:T(8,128)(2,1)S(1)} %slice.4.refs_0_, ...), custom_call_target="tpu_custom_call" | custom-call | bytes 6422528 | tf_op jit(solution)/shard_map/adjoint_of_class/pallas_call | solution.py:99
  25.3 0.5 %collective-permute-start.3 = (f32[128,384]{1,0:T(8,128)S(1)}, f32[128,384]{1,0:T(8,128)S(1)}, u32[]{:S(2)}, u32[]{:S(2)}) collective-permute-start(f32[128,384]{1,0:T(8,128)S(1)} %bitcast.19), channel_id=1, source_target_pairs={{0,16},{16,0},{1,17},{17,1},{2,18},{18,2},{3,19},{19,3},{4,20},{20... | collective-permute-start | bytes 589832 | tf_op jit(solution)/shard_map/ppermute | solution.py:328
  25.9 1.1 %collective-permute-done.3.refs_0_ = f32[128,384]{1,0:T(8,128)S(1)} collective-permute-done((f32[128,384]{1,0:T(8,128)S(1)}, f32[128,384]{1,0:T(8,128)S(1)}, u32[]{:S(2)}, u32[]{:S(2)}) %collective-permute-start.3) | collective-permute-done | bytes 196640 | tf_op jit(solution)/shard_map/ppermute | solution.py:328
  26.9 0.2 total_for_homes.1
  27.1 10.9 %all_to_all.11.home = bf16[16,8,384]{2,1,0:T(8,128)(2,1)S(1)} all-to-all(bf16[16,8,384]{2,1,0:T(8,128)(2,1)S(1)} %total_for_homes.1), channel_id=1, replica_groups=mesh['path'=2,'lon'=8,'lat'=2] {'lon','lat'}, dimensions={0} | all-to-all | bytes 196608 | tf_op jit(solution)/shard_map/all_to_all | solution.py:36
  38.0 0.2 attribution_rows.1
  38.2 0.6 %copy.8 = bf16[8,16,384]{2,1,0:T(8,128)(2,1)} copy(bf16[8,16,384]{2,1,0:T(8,128)(2,1)S(1)} %attribution_rows.1) | data formatting | bytes 196608
  (1 shorter events, 0.0 us)
Async XLA Ops:
  0.0 0.9 %copy-start.6 = (bf16[16,16,384]{2,1,0:T(8,128)(2,1)S(1)}, bf16[16,16,384]{2,1,0:T(8,128)(2,1)}, u32[]{:S(2)}) copy-start(bf16[16,16,384]{2,1,0:T(8,128)(2,1)} %param.9) | copy-start | bytes 589828
  0.0 1.0 %copy-start.5 = (bf16[16,16,384]{2,1,0:T(8,128)(2,1)S(1)}, bf16[16,16,384]{2,1,0:T(8,128)(2,1)}, u32[]{:S(2)}) copy-start(bf16[16,16,384]{2,1,0:T(8,128)(2,1)} %param.8) | copy-start | bytes 589828
  0.0 1.1 %copy-start.4 = (bf16[16,16,384]{2,1,0:T(8,128)(2,1)S(1)}, bf16[16,16,384]{2,1,0:T(8,128)(2,1)}, u32[]{:S(2)}) copy-start(bf16[16,16,384]{2,1,0:T(8,128)(2,1)} %param.7) | copy-start | bytes 589828
  0.0 20.5 %collective-permute-start = (bf16[9,192,384]{2,1,0:T(8,128)(2,1)}, bf16[9,192,384]{2,1,0:T(8,128)(2,1)S(1)}, u32[]{:S(2)}, u32[]{:S(2)}) collective-permute-start(bf16[9,192,384]{2,1,0:T(8,128)(2,1)} %param.10), channel_id=1, source_target_pairs={{0,16},{16,0},{1,17},{17,1},{2,18},{18,2},{3,19},{19,3},{4,20},{20... | collective-permute-start | bytes 3981320 | tf_op jit(solution)/shard_map/ppermute | solution.py:328
  0.5 20.0 %collective-permute-start.1 = (bf16[9,192,384]{2,1,0:T(8,128)(2,1)}, bf16[9,192,384]{2,1,0:T(8,128)(2,1)S(1)}, u32[]{:S(2)}, u32[]{:S(2)}) collective-permute-start(bf16[9,192,384]{2,1,0:T(8,128)(2,1)} %param.12), channel_id=1, source_target_pairs={{0,16},{16,0},{1,17},{17,1},{2,18},{18,2},{3,19},{19,3},{4,20},{20... | collective-permute-start | bytes 3981320 | tf_op jit(solution)/shard_map/ppermute | solution.py:328
  1.1 19.4 %copy-start = (bf16[9,192,384]{2,1,0:T(8,128)(2,1)S(1)}, bf16[9,192,384]{2,1,0:T(8,128)(2,1)}, u32[]{:S(2)}) copy-start(bf16[9,192,384]{2,1,0:T(8,128)(2,1)} %param.10) | copy-start | bytes 3981316
  1.1 19.4 %copy-start.1 = (bf16[9,192,384]{2,1,0:T(8,128)(2,1)S(1)}, bf16[9,192,384]{2,1,0:T(8,128)(2,1)}, u32[]{:S(2)}) copy-start(bf16[9,192,384]{2,1,0:T(8,128)(2,1)} %param.12) | copy-start | bytes 3981316
  1.1 19.4 %copy-start.2 = (f32[384]{0:T(512)S(1)}, f32[384]{0:T(512)}, u32[]{:S(2)}) copy-start(f32[384]{0:T(512)} %first_bias.1) | copy-start | bytes 4612
  1.1 19.4 %copy-start.3 = (f32[384]{0:T(512)S(1)}, f32[384]{0:T(512)}, u32[]{:S(2)}) copy-start(f32[384]{0:T(512)} %second_bias.1) | copy-start | bytes 4612
  20.4 2.5 %collective-permute-start.2 = (bf16[16,8,384]{2,1,0:T(8,128)(2,1)S(1)}, bf16[16,8,384]{2,1,0:T(8,128)(2,1)S(1)}, u32[]{:S(2)}, u32[]{:S(2)}) collective-permute-start(bf16[16,8,384]{2,1,0:T(8,128)(2,1)S(1)} %slice.4.refs_0_), channel_id=1, source_target_pairs={{0,16},{16,0},{1,17},{17,1},{2,18},{18,2},{3,19},{19,3},{4,20},{20... | collective-permute-start | bytes 294920 | tf_op jit(solution)/shard_map/ppermute | solution.py:328
  25.3 1.6 %collective-permute-start.3 = (f32[128,384]{1,0:T(8,128)S(1)}, f32[128,384]{1,0:T(8,128)S(1)}, u32[]{:S(2)}, u32[]{:S(2)}) collective-permute-start(f32[128,384]{1,0:T(8,128)S(1)} %bitcast.19), channel_id=1, source_target_pairs={{0,16},{16,0},{1,17},{17,1},{2,18},{18,2},{3,19},{19,3},{4,20},{20... | collective-permute-start | bytes 589832 | tf_op jit(solution)/shard_map/ppermute | solution.py:328

commit v6 on v5

--- a/solution.py
+++ b/solution.py
@@ -241,10 +241,10 @@
     group_lon, group_lat, row_part, col_part = sizes
     points, depth = len(first_halves), first_slope.shape[-1]
     rows, cols = group_lon * row_part, group_lat * col_part
-    cells, span = rows * cols, row_part // points
+    cells, part = rows * cols, row_part // points * col_part
 
     def kernel(order, first_slope, second_slope, *refs):
-        kept, sent, edged, near_taps, far_taps, grad, laned = refs[3 * points :]
+        sent, edged, near_taps, far_taps, grad = refs[3 * points :]
 
         def run(place, cotangent, first, second):
             spread, stencil_part = class_tools(sizes, depth, edged)
@@ -255,28 +255,20 @@
                 hidden_adj = upstream[:, at:end] + stencil_part(far_taps, second, FAR // NEAR, at, end, False)
                 grad[:, at:end] = hidden_adj
                 spread(first_slope[:, at:end] * hidden_adj, 1, at, near_taps)
+            home = ordering((group_lat, col_part, group_lon, row_part), (2, 0, 3, 1))
             for at, end in channel_parts(depth):
                 grad[:, at:end] += stencil_part(near_taps, first, 1, at, end, False)
-                for b in range(at // LANES, end // LANES):
-                    laned[b] = grad[:, b * LANES : (b + 1) * LANES].reshape(cols, rows, LANES)
-            for k in range(points):
-                owner = (place + k) % points
-                target = kept if k == 0 else sent.at[k - 1]
-                for i in range(span):
-                    here = slice(i * (cells // row_part), (i + 1) * (cells // row_part))
-                    for b in range(depth // LANES):
-                        rows_of = laned[b, :, pl.ds(owner * span + i, group_lon, stride=row_part), :]
-                        target[here, b * LANES : (b + 1) * LANES] = rows_of.reshape(-1, LANES)
+            moved = jnp.dot(home, grad[...].astype(BF16), preferred_element_type=F32)
+            sent[...] = moved.reshape(cells // part, part, depth).astype(BF16)
 
         by_place(points, run, refs[:points], refs[points : 2 * points], refs[2 * points : 3 * points])
 
-    share = cells // points
     return call(
         kernel,
-        [((share, depth), F32), ((points - 1, share, depth), F32)],
+        [((cells // part, part, depth), BF16)],
         [pltpu.VMEM((cols, rows + 2 * EDGE, depth), F32)]
         + [pltpu.VMEM((cells, 3 * depth), BF16)] * 2
-        + [pltpu.VMEM((cells, depth), F32), pltpu.VMEM((depth // LANES, cols, rows, LANES), F32)],
+        + [pltpu.VMEM((cells, depth), F32)],
         "adjoint_of_class",
         16,
         order,
@@ -285,34 +277,17 @@
         *cotangents,
         *first_halves,
         *second_halves,
-    )
-
-
-def total_for_homes(kept, others, sizes):
-    group_lon, group_lat, row_part, col_part = sizes
-    share, depth = kept.shape
-    span = row_part // lax.axis_size("path")
-    part = span * col_part
-
-    def kernel(kept, *refs):
-        order = ordering((span, group_lat, col_part, group_lon), (3, 1, 0, 2))
-        others, sent = refs[:-1], refs[-1]
-        total = kept[...]
-        for other in others:
-            total = total + other[...]
-        moved = jnp.dot(order, total.astype(BF16), preferred_element_type=F32)
-        sent[...] = moved.reshape(share // part, part, depth).astype(BF16)
-
-    return call(kernel, [((share // part, part, depth), BF16)], [], "total_for_homes", 4, kept, *others)[0]
+    )[0]
 
 
 def attribution_rows(home, diff_rows, rows, cols):
-    depth = home.shape[-1]
+    points, depth = lax.axis_size("path"), home.shape[-1]
     cells = rows * cols
 
     def kernel(home, diff_rows, out):
-        order = ordering((NEAR, NEAR, rows // NEAR, cols // NEAR), (2, 0, 3, 1))
-        values = home[...].astype(F32).reshape(cells, depth).astype(BF16)
+        order = ordering((NEAR, NEAR, points, rows // NEAR, cols // NEAR), (2, 3, 0, 4, 1))
+        order = sum(order[k * cells : (k + 1) * cells] for k in range(points))
+        values = home[...].astype(F32).reshape(points * cells, depth).astype(BF16)
         moved = jnp.dot(order, values, preferred_element_type=F32)
         out[...] = (diff_rows[...] * moved).reshape(rows, cols, depth).astype(BF16)
 
@@ -338,9 +313,8 @@
     own = got[:, sizes[2] * sizes[3] :, :]
     cotangents = [own] + [turned(own, step) for step in range(1, points)]
     first_slope, second_slope = slopes_of_class(to_grid, got, halves[0], first_bias, halves[1], second_bias, sizes)
-    kept, others = adjoint_of_class(to_grid, cotangents, first_slope, second_slope, *halves, sizes)
-    others = [turned(others[step - 1], step) for step in range(1, points)]
-    home = swap(total_for_homes(kept, others, sizes))
+    grad = adjoint_of_class(to_grid, cotangents, first_slope, second_slope, *halves, sizes)
+    home = lax.all_to_all(grad, ("lon", "lat", "path"), 0, 0, tiled=True)
     return attribution_rows(home, diff_rows, rows // points, cols)
 
 

time: 39.1 us -> 37.9 us (0.969)
  waiting for transfers between devices: 1.08 us -> 0.01 us
  starting transfers between devices: 1.22 us -> 0.67 us
    all_to_all x0 -> x1, blocking collectives: none -> 11.2 us  [one_group(): home = lax.all_to_all(grad, ('lon', 'lat', 'path'), 0, 0, tiled=True)]
    all_to_all x2 -> x1, blocking collectives: 29.8 us -> 18.9 us  [swap(): return lax.all_to_all(chunks, ('lon', 'lat'), 0, 0, tiled=True)]
    ppermute x4 -> x3, waiting for transfers between devices: 1.08 us -> 0.01 us  [turned(): lax.ppermute(values, 'path', [(i, (i + step) % points) for i in range(poi...]
    ppermute x4 -> x3, starting transfers between devices: 1.22 us -> 0.67 us  [turned(): lax.ppermute(values, 'path', [(i, (i + step) % points) for i in range(poi...]
    pallas_call x6 -> x5, Pallas kernels: 5.6 us -> 5.65 us  [call(): pl.pallas_call(kernel, out_shape=[pltpu.VMEM(shape, dtype) for shape, dty...]
  transfers between devices with their start and end apart: 4 -> 3, of which waited for: 1 -> 0; matrix products, arithmetic and copies ran while one was open for 0% -> 0% of each run, Pallas kernels for 7% -> 8%
where the time goes in v6:
time: 37.9 us; the launch traced here: 37.6 us
  blocking collectives  30.1 us (79%)
  Pallas kernels  5.65 us (15%)
  local copies, waits for them, and re-layouts  1.01 us (3%)
  starting transfers between devices  0.67 us (2%)
    all_to_all x1, blocking collectives, swap(): return lax.all_to_all(chunks, ('lon', 'lat'), 0, 0, tiled=True)  18.9 us
    all_to_all x1, blocking collectives, one_group(): home = lax.all_to_all(grad, ('lon', 'lat', 'path'), 0, 0, tiled=True)  11.2 us
    pallas_call x5, Pallas kernels, call(): pl.pallas_call(kernel, out_shape=[pltpu.VMEM(shape, dtype) for shape, dty...  5.65 us
    unnamed x15, local copies, waits for them, and re-layouts  1 us
  transfers between devices with their start and end apart: 3, of which 0 were waited for; matrix products, arithmetic and copies ran while one was open for 0% of the time, Pallas kernels for 8%

profile of v6, /device:TPU:0, one launch (start us, length us, event | category | flops | bytes accessed | tf_op | source)
XLA Modules:
  0.0 37.6 jit_solution(7286703755340591814)
XLA Ops:
  0.0 0.0 copy-start.4
  0.0 0.0 copy-start.5
  0.0 0.0 copy-start.6
  0.0 0.5 %collective-permute-start = (bf16[9,192,384]{2,1,0:T(8,128)(2,1)}, bf16[9,192,384]{2,1,0:T(8,128)(2,1)S(1)}, u32[]{:S(2)}, u32[]{:S(2)}) collective-permute-start(bf16[9,192,384]{2,1,0:T(8,128)(2,1)} %param.10), channel_id=1, source_target_pairs={{0,16},{16,0},{1,17},{17,1},{2,18},{18,2},{3,19},{19,3},{4,20},{20... | collective-permute-start | bytes 3981320 | tf_op jit(solution)/shard_map/ppermute | solution.py:303
  0.5 0.1 collective-permute-start.1
  0.6 0.2 row_orders.1
  0.8 0.1 copy-done.4
  0.9 0.1 copy-done.5
  1.0 0.1 copy-done.6
  1.1 0.0 copy-start
  1.1 0.0 copy-start.1
  1.1 0.0 copy-start.2
  1.1 0.0 copy-start.3
  1.1 0.3 pack_classes.1
  1.5 18.9 %all_to_all.10.got = bf16[16,24,384]{2,1,0:T(8,128)(2,1)S(1)} all-to-all(bf16[16,24,384]{2,1,0:T(8,128)(2,1)S(1)} %get-tuple-element.13), channel_id=1, replica_groups=mesh['path'=2,'lon'=8,'lat'=2] {'lon','lat'}, dimensions={0} | all-to-all | bytes 589824 | tf_op jit(solution)/shard_map/all_to_all | solution.py:36
  20.4 0.1 collective-permute-start.2
  20.5 0.0 collective-permute-done
  20.5 0.0 collective-permute-done.1
  20.5 0.0 copy-done
  20.5 0.0 copy-done.1
  20.5 0.0 copy-done.2
  20.5 0.0 copy-done.3
  20.5 2.4 %slopes_of_class.1 = (f32[256,384]{1,0:T(8,128)S(1)}, f32[256,384]{1,0:T(8,128)S(1)}) custom-call(bf16[256,256]{1,0:T(8,128)(2,1)S(1)} %get-tuple-element.11.order, bf16[16,24,384]{2,1,0:T(8,128)(2,1)S(1)} %all_to_all.10.got, f32[384]{0:T(512)S(1)} %copy-done.2, f32[384]{0:T(512)S(1)} %copy-done.3, bf16[3,3,192,384]{3,2,1,0:T(8,128)(2,1)S(1)} %bitcast.7, ...), custom_call_target="tpu_custom_call" | custom-call | bytes 5737472 | tf_op jit(solution)/shard_map/slopes_of_class/pallas_call | solution.py:99
  22.9 0.0 collective-permute-done.2.refs_1_
  23.0 2.5 %adjoint_of_class.1 = bf16[32,8,384]{2,1,0:T(8,128)(2,1)S(1)} custom-call(bf16[256,256]{1,0:T(8,128)(2,1)S(1)} %get-tuple-element.11.order, f32[256,384]{1,0:T(8,128)S(1)} %get-tuple-element.14.first_slope, f32[256,384]{1,0:T(8,128)S(1)} %get-tuple-element.15.second_slope, bf16[16,8,384]{2,1,0:T(8,128)(2,1)S(1)} %slice.4.refs_0_, ...), custom_call_target="tpu_custom_call" | custom-call | bytes 6422528 | tf_op jit(solution)/shard_map/adjoint_of_class/pallas_call | solution.py:99
  25.5 11.2 %all_to_all.11.home = bf16[32,8,384]{2,1,0:T(8,128)(2,1)S(1)} all-to-all(bf16[32,8,384]{2,1,0:T(8,128)(2,1)S(1)} %adjoint_of_class.1), channel_id=1, replica_groups=mesh['path'=2,'lon'=8,'lat'=2] {'lon','lat','path'}, dimensions={0} | all-to-all | bytes 393216 | tf_op jit(solution)/shard_map/all_to_all | solution.py:317
  36.7 0.2 attribution_rows.1
  36.9 0.6 %copy.8 = bf16[8,16,384]{2,1,0:T(8,128)(2,1)} copy(bf16[8,16,384]{2,1,0:T(8,128)(2,1)S(1)} %attribution_rows.1) | data formatting | bytes 196608
  (1 shorter events, 0.0 us)
Async XLA Ops:
  0.0 0.9 %copy-start.4 = (bf16[16,16,384]{2,1,0:T(8,128)(2,1)S(1)}, bf16[16,16,384]{2,1,0:T(8,128)(2,1)}, u32[]{:S(2)}) copy-start(bf16[16,16,384]{2,1,0:T(8,128)(2,1)} %param.7) | copy-start | bytes 589828
  0.0 1.0 %copy-start.5 = (bf16[16,16,384]{2,1,0:T(8,128)(2,1)S(1)}, bf16[16,16,384]{2,1,0:T(8,128)(2,1)}, u32[]{:S(2)}) copy-start(bf16[16,16,384]{2,1,0:T(8,128)(2,1)} %param.8) | copy-start | bytes 589828
  0.0 1.1 %copy-start.6 = (bf16[16,16,384]{2,1,0:T(8,128)(2,1)S(1)}, bf16[16,16,384]{2,1,0:T(8,128)(2,1)}, u32[]{:S(2)}) copy-start(bf16[16,16,384]{2,1,0:T(8,128)(2,1)} %param.9) | copy-start | bytes 589828
  0.0 20.5 %collective-permute-start = (bf16[9,192,384]{2,1,0:T(8,128)(2,1)}, bf16[9,192,384]{2,1,0:T(8,128)(2,1)S(1)}, u32[]{:S(2)}, u32[]{:S(2)}) collective-permute-start(bf16[9,192,384]{2,1,0:T(8,128)(2,1)} %param.10), channel_id=1, source_target_pairs={{0,16},{16,0},{1,17},{17,1},{2,18},{18,2},{3,19},{19,3},{4,20},{20... | collective-permute-start | bytes 3981320 | tf_op jit(solution)/shard_map/ppermute | solution.py:303
  0.5 20.0 %collective-permute-start.1 = (bf16[9,192,384]{2,1,0:T(8,128)(2,1)}, bf16[9,192,384]{2,1,0:T(8,128)(2,1)S(1)}, u32[]{:S(2)}, u32[]{:S(2)}) collective-permute-start(bf16[9,192,384]{2,1,0:T(8,128)(2,1)} %param.12), channel_id=1, source_target_pairs={{0,16},{16,0},{1,17},{17,1},{2,18},{18,2},{3,19},{19,3},{4,20},{20... | collective-permute-start | bytes 3981320 | tf_op jit(solution)/shard_map/ppermute | solution.py:303
  1.1 19.4 %copy-start = (bf16[9,192,384]{2,1,0:T(8,128)(2,1)S(1)}, bf16[9,192,384]{2,1,0:T(8,128)(2,1)}, u32[]{:S(2)}) copy-start(bf16[9,192,384]{2,1,0:T(8,128)(2,1)} %param.10) | copy-start | bytes 3981316
  1.1 19.4 %copy-start.1 = (bf16[9,192,384]{2,1,0:T(8,128)(2,1)S(1)}, bf16[9,192,384]{2,1,0:T(8,128)(2,1)}, u32[]{:S(2)}) copy-start(bf16[9,192,384]{2,1,0:T(8,128)(2,1)} %param.12) | copy-start | bytes 3981316
  1.1 19.4 %copy-start.2 = (f32[384]{0:T(512)S(1)}, f32[384]{0:T(512)}, u32[]{:S(2)}) copy-start(f32[384]{0:T(512)} %first_bias.1) | copy-start | bytes 4612
  1.1 19.4 %copy-start.3 = (f32[384]{0:T(512)S(1)}, f32[384]{0:T(512)}, u32[]{:S(2)}) copy-start(f32[384]{0:T(512)} %second_bias.1) | copy-start | bytes 4612
  20.4 2.5 %collective-permute-start.2 = (bf16[16,8,384]{2,1,0:T(8,128)(2,1)S(1)}, bf16[16,8,384]{2,1,0:T(8,128)(2,1)S(1)}, u32[]{:S(2)}, u32[]{:S(2)}) collective-permute-start(bf16[16,8,384]{2,1,0:T(8,128)(2,1)S(1)} %slice.4.refs_0_), channel_id=1, source_target_pairs={{0,16},{16,0},{1,17},{17,1},{2,18},{18,2},{3,19},{19,3},{4,20},{20... | collective-permute-start | bytes 294920 | tf_op jit(solution)/shard_map/ppermute | solution.py:303

commit v7 on v6

--- a/solution.py
+++ b/solution.py
@@ -166,11 +166,27 @@
             shifted = edged[:, start : start + rows, span].reshape(cells, -1)
             target[:, i * depth + at : i * depth + at + values.shape[1]] = shifted.astype(BF16)
 
-    def stencil_part(source, weights, step, at, end, forward):
+    def convolution(source, weights, step):
+        shift = step * rows
+
+        def products(values, *columns):
+            blocks = [
+                jnp.concatenate([part[i, col] for i in range(3) for part in weights], axis=0) for col in columns
+            ]
+            joint = jnp.dot(values, jnp.concatenate(blocks, axis=1), preferred_element_type=F32)
+            return [joint[:, i * depth : (i + 1) * depth] for i in range(len(columns))]
+
+        if 2 * shift == cells:
+            same_low, before = products(source[:shift, :], 1, 0)
+            same_high, after = products(source[shift:, :], 1, 2)
+            return jnp.concatenate([same_low + after, same_high + before], axis=0)
+        before, same, after = products(source[...], 0, 1, 2)
+        fill = jnp.zeros((shift, depth), F32)
+        after = jnp.concatenate([after[shift:], fill], axis=0)
+        return same + after + jnp.concatenate([fill, before[: cells - shift]], axis=0)
+
+    def transposed_part(source, weights, step, at, end):
         def weigh(values, col):
-            if forward:
-                blocks = [part[i, col, :, at:end] for i in range(3) for part in weights]
-                return jnp.dot(values, jnp.concatenate(blocks, axis=0), preferred_element_type=F32)
             taps_of = [jnp.concatenate([part[2 - i, 2 - col] for part in weights], axis=0)[at:end] for i in range(3)]
             return lax.dot_general(
                 values, jnp.concatenate(taps_of, axis=1), (((1,), (1,)), ((), ())), preferred_element_type=F32
@@ -185,7 +201,7 @@
 
     edged[:, :EDGE, :] = jnp.zeros((cols, EDGE, depth), F32)
     edged[:, EDGE + rows :, :] = jnp.zeros((cols, EDGE, depth), F32)
-    return spread, stencil_part
+    return spread, convolution, transposed_part
 
 
 def by_place(points, run, *halves):
@@ -209,16 +225,13 @@
         first_slope, second_slope, edged, near_taps, far_taps = refs[2 * points :]
 
         def run(place, first, second):
-            spread, stencil_part = class_tools(sizes, depth, edged)
+            spread, convolution, _ = class_tools(sizes, depth, edged)
             field = jnp.dot(order[...], got[:, :part, :].reshape(cells, depth), preferred_element_type=F32)
             spread(field, 1, 0, near_taps)
-            for at, end in channel_parts(depth):
-                pre = stencil_part(near_taps, first, 1, at, end, True) + first_bias[at:end].reshape(1, -1)
-                act, first_slope[:, at:end] = gelu_and_slope(pre)
-                spread(field[:, at:end] + act, FAR // NEAR, at, far_taps)
-            for at, end in channel_parts(depth):
-                pre = stencil_part(far_taps, second, FAR // NEAR, at, end, True) + second_bias[at:end].reshape(1, -1)
-                second_slope[:, at:end] = gelu_and_slope(pre)[1]
+            act, first_slope[...] = gelu_and_slope(convolution(near_taps, first, 1) + first_bias[...].reshape(1, -1))
+            spread(field + act, FAR // NEAR, 0, far_taps)
+            pre = convolution(far_taps, second, FAR // NEAR) + second_bias[...].reshape(1, -1)
+            second_slope[...] = gelu_and_slope(pre)[1]
 
         by_place(points, run, refs[:points], refs[points : 2 * points])
 
@@ -247,17 +260,17 @@
         sent, edged, near_taps, far_taps, grad = refs[3 * points :]
 
         def run(place, cotangent, first, second):
-            spread, stencil_part = class_tools(sizes, depth, edged)
+            spread, _, transposed_part = class_tools(sizes, depth, edged)
             upstream = jnp.concatenate([share[...].astype(F32) for share in cotangent], axis=1)
             upstream = jnp.dot(order[...], upstream.reshape(cells, depth).astype(BF16), preferred_element_type=F32)
             spread(second_slope[...] * upstream, FAR // NEAR, 0, far_taps)
             for at, end in channel_parts(depth):
-                hidden_adj = upstream[:, at:end] + stencil_part(far_taps, second, FAR // NEAR, at, end, False)
+                hidden_adj = upstream[:, at:end] + transposed_part(far_taps, second, FAR // NEAR, at, end)
                 grad[:, at:end] = hidden_adj
                 spread(first_slope[:, at:end] * hidden_adj, 1, at, near_taps)
             home = ordering((group_lat, col_part, group_lon, row_part), (2, 0, 3, 1))
             for at, end in channel_parts(depth):
-                grad[:, at:end] += stencil_part(near_taps, first, 1, at, end, False)
+                grad[:, at:end] += transposed_part(near_taps, first, 1, at, end)
             moved = jnp.dot(home, grad[...].astype(BF16), preferred_element_type=F32)
             sent[...] = moved.reshape(cells // part, part, depth).astype(BF16)
 

time: 37.9 us -> 37.7 us (level)
  transfers between devices with their start and end apart: 3 -> 3, of which waited for: 0 -> 0; matrix products, arithmetic and copies ran while one was open for 0% -> 0% of each run, Pallas kernels for 8% -> 7%
where the time goes in v7:
time: 37.7 us; the launch traced here: 37.3 us
  blocking collectives  30.1 us (80%)
  Pallas kernels  5.42 us (14%)
  local copies, waits for them, and re-layouts  1.01 us (3%)
  starting transfers between devices  0.67 us (2%)
    all_to_all x1, blocking collectives, swap(): return lax.all_to_all(chunks, ('lon', 'lat'), 0, 0, tiled=True)  18.9 us
    all_to_all x1, blocking collectives, one_group(): home = lax.all_to_all(grad, ('lon', 'lat', 'path'), 0, 0, tiled=True)  11.2 us
    pallas_call x5, Pallas kernels, call(): pl.pallas_call(kernel, out_shape=[pltpu.VMEM(shape, dtype) for shape, dty...  5.42 us
    unnamed x15, local copies, waits for them, and re-layouts  1 us
  transfers between devices with their start and end apart: 3, of which 0 were waited for; matrix products, arithmetic and copies ran while one was open for 0% of the time, Pallas kernels for 7%

profile of v7, /device:TPU:0, one launch (start us, length us, event | category | flops | bytes accessed | tf_op | source)
XLA Modules:
  0.0 37.3 jit_solution(12995532152319879823)
XLA Ops:
  0.0 0.0 copy-start.4
  0.0 0.0 copy-start.5
  0.0 0.0 copy-start.6
  0.0 0.5 %collective-permute-start = (bf16[9,192,384]{2,1,0:T(8,128)(2,1)}, bf16[9,192,384]{2,1,0:T(8,128)(2,1)S(1)}, u32[]{:S(2)}, u32[]{:S(2)}) collective-permute-start(bf16[9,192,384]{2,1,0:T(8,128)(2,1)} %param.10), channel_id=1, source_target_pairs={{0,16},{16,0},{1,17},{17,1},{2,18},{18,2},{3,19},{19,3},{4,20},{20... | collective-permute-start | bytes 3981320 | tf_op jit(solution)/shard_map/ppermute | solution.py:316
  0.5 0.1 collective-permute-start.1
  0.6 0.2 row_orders.1
  0.8 0.1 copy-done.4
  0.9 0.1 copy-done.5
  1.0 0.1 copy-done.6
  1.1 0.0 copy-start
  1.1 0.0 copy-start.1
  1.1 0.0 copy-start.2
  1.1 0.0 copy-start.3
  1.1 0.3 pack_classes.1
  1.5 18.9 %all_to_all.10.got = bf16[16,24,384]{2,1,0:T(8,128)(2,1)S(1)} all-to-all(bf16[16,24,384]{2,1,0:T(8,128)(2,1)S(1)} %get-tuple-element.13), channel_id=1, replica_groups=mesh['path'=2,'lon'=8,'lat'=2] {'lon','lat'}, dimensions={0} | all-to-all | bytes 589824 | tf_op jit(solution)/shard_map/all_to_all | solution.py:36
  20.4 0.1 collective-permute-start.2
  20.5 0.0 collective-permute-done
  20.5 0.0 collective-permute-done.1
  20.5 0.0 copy-done
  20.5 0.0 copy-done.1
  20.5 0.0 copy-done.2
  20.5 0.0 copy-done.3
  20.5 2.2 %slopes_of_class.1 = (f32[256,384]{1,0:T(8,128)S(1)}, f32[256,384]{1,0:T(8,128)S(1)}) custom-call(bf16[256,256]{1,0:T(8,128)(2,1)S(1)} %get-tuple-element.11.order, bf16[16,24,384]{2,1,0:T(8,128)(2,1)S(1)} %all_to_all.10.got, f32[384]{0:T(512)S(1)} %copy-done.2, f32[384]{0:T(512)S(1)} %copy-done.3, bf16[3,3,192,384]{3,2,1,0:T(8,128)(2,1)S(1)} %bitcast.7, ...), custom_call_target="tpu_custom_call" | custom-call | bytes 5737472 | tf_op jit(solution)/shard_map/slopes_of_class/pallas_call | solution.py:99
  22.7 0.0 collective-permute-done.2.refs_1_
  22.7 2.5 %adjoint_of_class.1 = bf16[32,8,384]{2,1,0:T(8,128)(2,1)S(1)} custom-call(bf16[256,256]{1,0:T(8,128)(2,1)S(1)} %get-tuple-element.11.order, f32[256,384]{1,0:T(8,128)S(1)} %get-tuple-element.14.first_slope, f32[256,384]{1,0:T(8,128)S(1)} %get-tuple-element.15.second_slope, bf16[16,8,384]{2,1,0:T(8,128)(2,1)S(1)} %slice.4.refs_0_, ...), custom_call_target="tpu_custom_call" | custom-call | bytes 6422528 | tf_op jit(solution)/shard_map/adjoint_of_class/pallas_call | solution.py:99
  25.3 11.2 %all_to_all.11.home = bf16[32,8,384]{2,1,0:T(8,128)(2,1)S(1)} all-to-all(bf16[32,8,384]{2,1,0:T(8,128)(2,1)S(1)} %adjoint_of_class.1), channel_id=1, replica_groups=mesh['path'=2,'lon'=8,'lat'=2] {'lon','lat','path'}, dimensions={0} | all-to-all | bytes 393216 | tf_op jit(solution)/shard_map/all_to_all | solution.py:330
  36.5 0.2 attribution_rows.1
  36.7 0.6 %copy.8 = bf16[8,16,384]{2,1,0:T(8,128)(2,1)} copy(bf16[8,16,384]{2,1,0:T(8,128)(2,1)S(1)} %attribution_rows.1) | data formatting | bytes 196608
  (1 shorter events, 0.0 us)
Async XLA Ops:
  0.0 0.9 %copy-start.4 = (bf16[16,16,384]{2,1,0:T(8,128)(2,1)S(1)}, bf16[16,16,384]{2,1,0:T(8,128)(2,1)}, u32[]{:S(2)}) copy-start(bf16[16,16,384]{2,1,0:T(8,128)(2,1)} %param.7) | copy-start | bytes 589828
  0.0 1.0 %copy-start.5 = (bf16[16,16,384]{2,1,0:T(8,128)(2,1)S(1)}, bf16[16,16,384]{2,1,0:T(8,128)(2,1)}, u32[]{:S(2)}) copy-start(bf16[16,16,384]{2,1,0:T(8,128)(2,1)} %param.8) | copy-start | bytes 589828
  0.0 1.1 %copy-start.6 = (bf16[16,16,384]{2,1,0:T(8,128)(2,1)S(1)}, bf16[16,16,384]{2,1,0:T(8,128)(2,1)}, u32[]{:S(2)}) copy-start(bf16[16,16,384]{2,1,0:T(8,128)(2,1)} %param.9) | copy-start | bytes 589828
  0.0 20.5 %collective-permute-start = (bf16[9,192,384]{2,1,0:T(8,128)(2,1)}, bf16[9,192,384]{2,1,0:T(8,128)(2,1)S(1)}, u32[]{:S(2)}, u32[]{:S(2)}) collective-permute-start(bf16[9,192,384]{2,1,0:T(8,128)(2,1)} %param.10), channel_id=1, source_target_pairs={{0,16},{16,0},{1,17},{17,1},{2,18},{18,2},{3,19},{19,3},{4,20},{20... | collective-permute-start | bytes 3981320 | tf_op jit(solution)/shard_map/ppermute | solution.py:316
  0.5 20.0 %collective-permute-start.1 = (bf16[9,192,384]{2,1,0:T(8,128)(2,1)}, bf16[9,192,384]{2,1,0:T(8,128)(2,1)S(1)}, u32[]{:S(2)}, u32[]{:S(2)}) collective-permute-start(bf16[9,192,384]{2,1,0:T(8,128)(2,1)} %param.12), channel_id=1, source_target_pairs={{0,16},{16,0},{1,17},{17,1},{2,18},{18,2},{3,19},{19,3},{4,20},{20... | collective-permute-start | bytes 3981320 | tf_op jit(solution)/shard_map/ppermute | solution.py:316
  1.1 19.4 %copy-start = (bf16[9,192,384]{2,1,0:T(8,128)(2,1)S(1)}, bf16[9,192,384]{2,1,0:T(8,128)(2,1)}, u32[]{:S(2)}) copy-start(bf16[9,192,384]{2,1,0:T(8,128)(2,1)} %param.10) | copy-start | bytes 3981316
  1.1 19.4 %copy-start.1 = (bf16[9,192,384]{2,1,0:T(8,128)(2,1)S(1)}, bf16[9,192,384]{2,1,0:T(8,128)(2,1)}, u32[]{:S(2)}) copy-start(bf16[9,192,384]{2,1,0:T(8,128)(2,1)} %param.12) | copy-start | bytes 3981316
  1.1 19.4 %copy-start.2 = (f32[384]{0:T(512)S(1)}, f32[384]{0:T(512)}, u32[]{:S(2)}) copy-start(f32[384]{0:T(512)} %first_bias.1) | copy-start | bytes 4612
  1.1 19.4 %copy-start.3 = (f32[384]{0:T(512)S(1)}, f32[384]{0:T(512)}, u32[]{:S(2)}) copy-start(f32[384]{0:T(512)} %second_bias.1) | copy-start | bytes 4612
  20.4 2.3 %collective-permute-start.2 = (bf16[16,8,384]{2,1,0:T(8,128)(2,1)S(1)}, bf16[16,8,384]{2,1,0:T(8,128)(2,1)S(1)}, u32[]{:S(2)}, u32[]{:S(2)}) collective-permute-start(bf16[16,8,384]{2,1,0:T(8,128)(2,1)S(1)} %slice.4.refs_0_), channel_id=1, source_target_pairs={{0,16},{16,0},{1,17},{17,1},{2,18},{18,2},{3,19},{19,3},{4,20},{20... | collective-permute-start | bytes 294920 | tf_op jit(solution)/shard_map/ppermute | solution.py:316

commit v8 on v7

--- a/solution.py
+++ b/solution.py
@@ -14,6 +14,8 @@
 LANES = 128
 F32, BF16 = jnp.float32, jnp.bfloat16
 VMEM = pl.BlockSpec(memory_space=pltpu.VMEM)
+AHEAD = 4 * 10**9
+
 
 def smooth_act(value):
     return jax.nn.gelu(value, approximate=True)
@@ -93,17 +95,17 @@
     return value * half, half + 0.5 * value * (1 - bent * bent) * (scale * (1 + 3 * cubic * square))
 
 
-def call(kernel, outs, scratch, name, megabytes, *args, specs=None, flops=0):
-    specs = specs or [VMEM] * len(args)
-    args = [pltpu.with_memory_space_constraint(x, spec.memory_space) for x, spec in zip(args, specs)]
+def call(kernel, outs, scratch, name, megabytes, *args, flops=0):
+    args = [pltpu.with_memory_space_constraint(x, pltpu.VMEM) for x in args]
+    size = sum(x.size * x.dtype.itemsize for x in args)
     return pl.pallas_call(
         kernel,
         out_shape=[pltpu.VMEM(shape, dtype) for shape, dtype in outs],
-        in_specs=specs,
+        in_specs=[VMEM] * len(args),
         out_specs=[VMEM] * len(outs),
         scratch_shapes=scratch,
         compiler_params=pltpu.CompilerParams(vmem_limit_bytes=megabytes << 20),
-        cost_estimate=pl.CostEstimate(flops=flops, bytes_accessed=sum(x.size * x.dtype.itemsize for x in args), transcendentals=0),
+        cost_estimate=pl.CostEstimate(flops=flops, bytes_accessed=size, transcendentals=0),
         name=name,
     )(*args)
 
@@ -116,7 +118,7 @@
         to_classes[...] = ordering((row_part, NEAR, col_part, NEAR), (1, 3, 0, 2))
         to_grid[...] = ordering((group_lon, group_lat, row_part, col_part), (1, 3, 0, 2))
 
-    return call(kernel, [((cells, cells), BF16)] * 2, [], "row_orders", 4, flops=4 * 10**9)
+    return call(kernel, [((cells, cells), BF16)] * 2, [], "row_orders", 4, flops=AHEAD)
 
 
 def pack_classes(order, observed, baseline, cotangent):
@@ -149,7 +151,7 @@
         8,
         order,
         *(x.reshape(cells, depth) for x in (observed, baseline, cotangent)),
-        flops=4 * 10**9,
+        flops=AHEAD,
     )
 
 
@@ -254,7 +256,7 @@
     group_lon, group_lat, row_part, col_part = sizes
     points, depth = len(first_halves), first_slope.shape[-1]
     rows, cols = group_lon * row_part, group_lat * col_part
-    cells, part = rows * cols, row_part // points * col_part
+    cells = rows * cols
 
     def kernel(order, first_slope, second_slope, *refs):
         sent, edged, near_taps, far_taps, grad = refs[3 * points :]
@@ -271,14 +273,13 @@
             home = ordering((group_lat, col_part, group_lon, row_part), (2, 0, 3, 1))
             for at, end in channel_parts(depth):
                 grad[:, at:end] += transposed_part(near_taps, first, 1, at, end)
-            moved = jnp.dot(home, grad[...].astype(BF16), preferred_element_type=F32)
-            sent[...] = moved.reshape(cells // part, part, depth).astype(BF16)
+            sent[...] = jnp.dot(home, grad[...].astype(BF16), preferred_element_type=F32).astype(BF16)
 
         by_place(points, run, refs[:points], refs[points : 2 * points], refs[2 * points : 3 * points])
 
     return call(
         kernel,
-        [((cells // part, part, depth), BF16)],
+        [((cells, depth), BF16)],
         [pltpu.VMEM((cols, rows + 2 * EDGE, depth), F32)]
         + [pltpu.VMEM((cells, 3 * depth), BF16)] * 2
         + [pltpu.VMEM((cells, depth), F32)],
@@ -300,8 +301,7 @@
     def kernel(home, diff_rows, out):
         order = ordering((NEAR, NEAR, points, rows // NEAR, cols // NEAR), (2, 3, 0, 4, 1))
         order = sum(order[k * cells : (k + 1) * cells] for k in range(points))
-        values = home[...].astype(F32).reshape(points * cells, depth).astype(BF16)
-        moved = jnp.dot(order, values, preferred_element_type=F32)
+        moved = jnp.dot(order, home[...], preferred_element_type=F32)
         out[...] = (diff_rows[...] * moved).reshape(rows, cols, depth).astype(BF16)
 
     return call(kernel, [((rows, cols, depth), BF16)], [], "attribution_rows", 4, home, diff_rows)[0]
@@ -327,8 +327,9 @@
     cotangents = [own] + [turned(own, step) for step in range(1, points)]
     first_slope, second_slope = slopes_of_class(to_grid, got, halves[0], first_bias, halves[1], second_bias, sizes)
     grad = adjoint_of_class(to_grid, cotangents, first_slope, second_slope, *halves, sizes)
-    home = lax.all_to_all(grad, ("lon", "lat", "path"), 0, 0, tiled=True)
-    return attribution_rows(home, diff_rows, rows // points, cols)
+    chunks = grad.reshape(NEAR * NEAR * points, -1, depth)
+    home = lax.all_to_all(chunks, ("lon", "lat", "path"), 0, 0, tiled=True)
+    return attribution_rows(home.reshape(grad.shape), diff_rows, rows // points, cols)
 
 
 def several_groups(observed, baseline, cotangent, first_weight, first_bias, second_weight, second_bias):

time: 37.7 us -> 37.7 us (level)
  no operation moved by 1% of the time
where the time goes in v8:
time: 37.7 us; the launch traced here: 37.3 us
  blocking collectives  30.1 us (80%)
  Pallas kernels  5.42 us (14%)
  local copies, waits for them, and re-layouts  1.01 us (3%)
  starting transfers between devices  0.67 us (2%)
    all_to_all x1, blocking collectives, swap(): return lax.all_to_all(chunks, ('lon', 'lat'), 0, 0, tiled=True)  18.9 us
    all_to_all x1, blocking collectives, one_group(): home = lax.all_to_all(chunks, ('lon', 'lat', 'path'), 0, 0, tiled=True)  11.2 us
    pallas_call x5, Pallas kernels, call(): pl.pallas_call(kernel, out_shape=[pltpu.VMEM(shape, dtype) for shape, dty...  5.42 us
    unnamed x15, local copies, waits for them, and re-layouts  1 us
  transfers between devices with their start and end apart: 3, of which 0 were waited for; matrix products, arithmetic and copies ran while one was open for 0% of the time, Pallas kernels for 7%

profile of v8, /device:TPU:0, one launch (start us, length us, event | category | flops | bytes accessed | tf_op | source)
XLA Modules:
  0.0 37.3 jit_solution(12995532152319879823)
XLA Ops:
  0.0 0.0 copy-start.4
  0.0 0.0 copy-start.5
  0.0 0.0 copy-start.6
  0.0 0.5 %collective-permute-start = (bf16[9,192,384]{2,1,0:T(8,128)(2,1)}, bf16[9,192,384]{2,1,0:T(8,128)(2,1)S(1)}, u32[]{:S(2)}, u32[]{:S(2)}) collective-permute-start(bf16[9,192,384]{2,1,0:T(8,128)(2,1)} %param.10), channel_id=1, source_target_pairs={{0,16},{16,0},{1,17},{17,1},{2,18},{18,2},{3,19},{19,3},{4,20},{20... | collective-permute-start | bytes 3981320 | tf_op jit(solution)/shard_map/ppermute | solution.py:316
  0.5 0.1 collective-permute-start.1
  0.6 0.2 row_orders.1
  0.8 0.1 copy-done.4
  0.9 0.1 copy-done.5
  1.0 0.1 copy-done.6
  1.1 0.0 copy-start
  1.1 0.0 copy-start.1
  1.1 0.0 copy-start.2
  1.1 0.0 copy-start.3
  1.1 0.3 pack_classes.1
  1.5 18.9 %all_to_all.10.got = bf16[16,24,384]{2,1,0:T(8,128)(2,1)S(1)} all-to-all(bf16[16,24,384]{2,1,0:T(8,128)(2,1)S(1)} %get-tuple-element.13), channel_id=1, replica_groups=mesh['path'=2,'lon'=8,'lat'=2] {'lon','lat'}, dimensions={0} | all-to-all | bytes 589824 | tf_op jit(solution)/shard_map/all_to_all | solution.py:38
  20.4 0.1 collective-permute-start.2
  20.5 0.0 collective-permute-done
  20.5 0.0 collective-permute-done.1
  20.5 0.0 copy-done
  20.5 0.0 copy-done.1
  20.5 0.0 copy-done.2
  20.5 0.0 copy-done.3
  20.5 2.2 %slopes_of_class.1 = (f32[256,384]{1,0:T(8,128)S(1)}, f32[256,384]{1,0:T(8,128)S(1)}) custom-call(bf16[256,256]{1,0:T(8,128)(2,1)S(1)} %get-tuple-element.11.order, bf16[16,24,384]{2,1,0:T(8,128)(2,1)S(1)} %all_to_all.10.got, f32[384]{0:T(512)S(1)} %copy-done.2, f32[384]{0:T(512)S(1)} %copy-done.3, bf16[3,3,192,384]{3,2,1,0:T(8,128)(2,1)S(1)} %bitcast.9, ...), custom_call_target="tpu_custom_call" | custom-call | bytes 5737472 | tf_op jit(solution)/shard_map/slopes_of_class/pallas_call | solution.py:101
  22.7 0.0 collective-permute-done.2.refs_1_
  22.7 2.5 %adjoint_of_class.1 = bf16[256,384]{1,0:T(8,128)(2,1)S(1)} custom-call(bf16[256,256]{1,0:T(8,128)(2,1)S(1)} %get-tuple-element.11.order, f32[256,384]{1,0:T(8,128)S(1)} %get-tuple-element.14.first_slope, f32[256,384]{1,0:T(8,128)S(1)} %get-tuple-element.15.second_slope, bf16[16,8,384]{2,1,0:T(8,128)(2,1)S(1)} %slice.4.refs_0_, ...), custom_call_target="tpu_custom_call" | custom-call | bytes 6422528 | tf_op jit(solution)/shard_map/adjoint_of_class/pallas_call | solution.py:101
  25.3 11.2 %all_to_all.11 = bf16[32,8,384]{2,1,0:T(8,128)(2,1)S(1)} all-to-all(bf16[32,8,384]{2,1,0:T(8,128)(2,1)S(1)} %bitcast.17), channel_id=1, replica_groups=mesh['path'=2,'lon'=8,'lat'=2] {'lon','lat','path'}, dimensions={0} | all-to-all | bytes 393216 | tf_op jit(solution)/shard_map/all_to_all | solution.py:331
  36.5 0.2 attribution_rows.1
  36.7 0.6 %copy.8 = bf16[8,16,384]{2,1,0:T(8,128)(2,1)} copy(bf16[8,16,384]{2,1,0:T(8,128)(2,1)S(1)} %attribution_rows.1) | data formatting | bytes 196608
  (1 shorter events, 0.0 us)
Async XLA Ops:
  0.0 0.9 %copy-start.4 = (bf16[16,16,384]{2,1,0:T(8,128)(2,1)S(1)}, bf16[16,16,384]{2,1,0:T(8,128)(2,1)}, u32[]{:S(2)}) copy-start(bf16[16,16,384]{2,1,0:T(8,128)(2,1)} %param.7) | copy-start | bytes 589828
  0.0 1.0 %copy-start.5 = (bf16[16,16,384]{2,1,0:T(8,128)(2,1)S(1)}, bf16[16,16,384]{2,1,0:T(8,128)(2,1)}, u32[]{:S(2)}) copy-start(bf16[16,16,384]{2,1,0:T(8,128)(2,1)} %param.8) | copy-start | bytes 589828
  0.0 1.1 %copy-start.6 = (bf16[16,16,384]{2,1,0:T(8,128)(2,1)S(1)}, bf16[16,16,384]{2,1,0:T(8,128)(2,1)}, u32[]{:S(2)}) copy-start(bf16[16,16,384]{2,1,0:T(8,128)(2,1)} %param.9) | copy-start | bytes 589828
  0.0 20.5 %collective-permute-start = (bf16[9,192,384]{2,1,0:T(8,128)(2,1)}, bf16[9,192,384]{2,1,0:T(8,128)(2,1)S(1)}, u32[]{:S(2)}, u32[]{:S(2)}) collective-permute-start(bf16[9,192,384]{2,1,0:T(8,128)(2,1)} %param.10), channel_id=1, source_target_pairs={{0,16},{16,0},{1,17},{17,1},{2,18},{18,2},{3,19},{19,3},{4,20},{20... | collective-permute-start | bytes 3981320 | tf_op jit(solution)/shard_map/ppermute | solution.py:316
  0.5 20.0 %collective-permute-start.1 = (bf16[9,192,384]{2,1,0:T(8,128)(2,1)}, bf16[9,192,384]{2,1,0:T(8,128)(2,1)S(1)}, u32[]{:S(2)}, u32[]{:S(2)}) collective-permute-start(bf16[9,192,384]{2,1,0:T(8,128)(2,1)} %param.12), channel_id=1, source_target_pairs={{0,16},{16,0},{1,17},{17,1},{2,18},{18,2},{3,19},{19,3},{4,20},{20... | collective-permute-start | bytes 3981320 | tf_op jit(solution)/shard_map/ppermute | solution.py:316
  1.1 19.4 %copy-start = (bf16[9,192,384]{2,1,0:T(8,128)(2,1)S(1)}, bf16[9,192,384]{2,1,0:T(8,128)(2,1)}, u32[]{:S(2)}) copy-start(bf16[9,192,384]{2,1,0:T(8,128)(2,1)} %param.10) | copy-start | bytes 3981316
  1.1 19.4 %copy-start.1 = (bf16[9,192,384]{2,1,0:T(8,128)(2,1)S(1)}, bf16[9,192,384]{2,1,0:T(8,128)(2,1)}, u32[]{:S(2)}) copy-start(bf16[9,192,384]{2,1,0:T(8,128)(2,1)} %param.12) | copy-start | bytes 3981316
  1.1 19.4 %copy-start.2 = (f32[384]{0:T(512)S(1)}, f32[384]{0:T(512)}, u32[]{:S(2)}) copy-start(f32[384]{0:T(512)} %first_bias.1) | copy-start | bytes 4612
  1.1 19.4 %copy-start.3 = (f32[384]{0:T(512)S(1)}, f32[384]{0:T(512)}, u32[]{:S(2)}) copy-start(f32[384]{0:T(512)} %second_bias.1) | copy-start | bytes 4612
  20.4 2.3 %collective-permute-start.2 = (bf16[16,8,384]{2,1,0:T(8,128)(2,1)S(1)}, bf16[16,8,384]{2,1,0:T(8,128)(2,1)S(1)}, u32[]{:S(2)}, u32[]{:S(2)}) collective-permute-start(bf16[16,8,384]{2,1,0:T(8,128)(2,1)S(1)} %slice.4.refs_0_), channel_id=1, source_target_pairs={{0,16},{16,0},{1,17},{17,1},{2,18},{18,2},{3,19},{19,3},{4,20},{20... | collective-permute-start | bytes 294920 | tf_op jit(solution)/shard_map/ppermute | solution.py:316

commit v9 on v8

--- a/solution.py
+++ b/solution.py
@@ -3,6 +3,7 @@
 
 import jax
 import jax.numpy as jnp
+import numpy as np
 from jax import lax
 from jax.experimental import pallas as pl
 from jax.experimental.pallas import tpu as pltpu
@@ -42,6 +43,28 @@
         groups = [list(range(i, i + size)) for i in range(0, count, size)]
         chunks = lax.all_to_all(chunks, axis, dim, dim, tiled=True, axis_index_groups=groups)
     return chunks.reshape((group_lon * group_lat,) + chunks.shape[2:])
+
+
+def lon_parts():
+    group_lon = group_sizes()[0]
+    fast = 2 if group_lon % 2 == 0 else 1
+    slow = group_lon // fast
+    bits = slow.bit_length() - 1
+    listing = [sum(((i ^ (i >> 1)) >> b & 1) << (bits - 1 - b) for b in range(bits)) for i in range(slow)]
+    return slow, fast, listing
+
+
+def listed(points):
+    slow, fast, listing = lon_parts()
+    lat, path = lax.axis_size("lat"), lax.axis_size("path")
+    grid = np.arange(slow * fast * lat * path).reshape(slow, fast, lat, path)[listing]
+    if points:
+        return [grid.transpose(1, 2, 3, 0).reshape(-1).tolist()]
+    return [grid[..., p].transpose(1, 2, 0).reshape(-1).tolist() for p in range(path)]
+
+
+def swap_listed(chunks, points):
+    return lax.all_to_all(chunks, ("lon", "lat", "path"), 0, 0, tiled=True, axis_index_groups=listed(points))
 
 
 def to_classes(cells):
@@ -77,13 +100,28 @@
     return total
 
 
-def ordering(dims, axes):
-    cells = math.prod(dims)
+def digit(place, stride, size):
+    if size & (size - 1) or stride & (stride - 1):
+        return lax.rem(lax.div(place, jnp.int32(stride)), jnp.int32(size))
+    return lax.shift_right_logical(place, jnp.int32(stride.bit_length() - 1)) & (size - 1)
+
+
+def ordering(dims, axes, listing=(None, ())):
+    cells, runs = math.prod(dims), []
+    for axis in axes:
+        if runs and runs[-1][-1] == axis - 1 and listing[0] not in (axis, axis - 1):
+            runs[-1].append(axis)
+        else:
+            runs.append([axis])
     place = lax.broadcasted_iota(jnp.int32, (cells, 1), 0)
     source, stride = jnp.zeros((cells, 1), jnp.int32), 1
-    for axis in reversed(axes):
-        source += lax.rem(lax.div(place, jnp.int32(stride)), jnp.int32(dims[axis])) * math.prod(dims[axis + 1 :])
-        stride *= dims[axis]
+    for run in reversed(runs):
+        size = math.prod(dims[axis] for axis in run)
+        here = digit(place, stride, size)
+        if run == [listing[0]]:
+            here = sum(jnp.where(here == i, value, 0) for i, value in enumerate(listing[1]) if value)
+        source += here * math.prod(dims[run[-1] + 1 :])
+        stride *= size
     return (lax.broadcasted_iota(jnp.int32, (cells, cells), 1) == source).astype(F32).astype(BF16)
 
 
@@ -116,7 +154,9 @@
 
     def kernel(to_classes, to_grid):
         to_classes[...] = ordering((row_part, NEAR, col_part, NEAR), (1, 3, 0, 2))
-        to_grid[...] = ordering((group_lon, group_lat, row_part, col_part), (1, 3, 0, 2))
+        slow, fast, listing = lon_parts()
+        found = [listing.index(i) for i in range(slow)]
+        to_grid[...] = ordering((fast, group_lat, slow, row_part, col_part), (1, 4, 2, 0, 3), (2, found))
 
     return call(kernel, [((cells, cells), BF16)] * 2, [], "row_orders", 4, flops=AHEAD)
 
@@ -270,7 +310,9 @@
                 hidden_adj = upstream[:, at:end] + transposed_part(far_taps, second, FAR // NEAR, at, end)
                 grad[:, at:end] = hidden_adj
                 spread(first_slope[:, at:end] * hidden_adj, 1, at, near_taps)
-            home = ordering((group_lat, col_part, group_lon, row_part), (2, 0, 3, 1))
+            slow, fast, listing = lon_parts()
+            dims = (group_lat, col_part, slow, fast, points, row_part // points)
+            home = ordering(dims, (3, 0, 4, 2, 5, 1), (2, listing))
             for at, end in channel_parts(depth):
                 grad[:, at:end] += transposed_part(near_taps, first, 1, at, end)
             sent[...] = jnp.dot(home, grad[...].astype(BF16), preferred_element_type=F32).astype(BF16)
@@ -296,10 +338,14 @@
 
 def attribution_rows(home, diff_rows, rows, cols):
     points, depth = lax.axis_size("path"), home.shape[-1]
-    cells = rows * cols
+    cells, group_lat = rows * cols, group_sizes()[1]
 
     def kernel(home, diff_rows, out):
-        order = ordering((NEAR, NEAR, points, rows // NEAR, cols // NEAR), (2, 3, 0, 4, 1))
+        bits, ahead = (NEAR * NEAR).bit_length() - 1, (group_lat * lon_parts()[1]).bit_length() - 1
+        of_class = tuple(i + (i >= ahead) for i in range(bits))
+        dims = (2,) * ahead + (points,) + (2,) * (bits - ahead) + (rows // NEAR, cols // NEAR)
+        row_bits, col_bits = of_class[: bits // 2], of_class[bits // 2 :]
+        order = ordering(dims, (ahead, bits + 1) + row_bits + (bits + 2,) + col_bits)
         order = sum(order[k * cells : (k + 1) * cells] for k in range(points))
         moved = jnp.dot(order, home[...], preferred_element_type=F32)
         out[...] = (diff_rows[...] * moved).reshape(rows, cols, depth).astype(BF16)
@@ -322,13 +368,13 @@
     ]
     to_classes, to_grid = row_orders(rows, cols, sizes)
     sent, diff_rows = pack_classes(to_classes, observed, baseline, cotangent)
-    got = swap(sent)
+    got = swap_listed(sent, points=False)
     own = got[:, sizes[2] * sizes[3] :, :]
     cotangents = [own] + [turned(own, step) for step in range(1, points)]
     first_slope, second_slope = slopes_of_class(to_grid, got, halves[0], first_bias, halves[1], second_bias, sizes)
     grad = adjoint_of_class(to_grid, cotangents, first_slope, second_slope, *halves, sizes)
     chunks = grad.reshape(NEAR * NEAR * points, -1, depth)
-    home = lax.all_to_all(chunks, ("lon", "lat", "path"), 0, 0, tiled=True)
+    home = swap_listed(chunks, points=True)
     return attribution_rows(home.reshape(grad.shape), diff_rows, rows // points, cols)
 
 

time: 37.7 us -> 37.2 us (0.987)
  blocking collectives: 30.1 us -> 29.7 us
    all_to_all x2, blocking collectives: 30.1 us -> 29.7 us  [swap_listed(): lax.all_to_all(chunks, ('lon', 'lat', 'path'), 0, 0, tiled=True, axis_ind...]
where the time goes in v9:
time: 37.2 us; the launch traced here: 37 us
  blocking collectives  29.7 us (80%)
  Pallas kernels  5.43 us (15%)
  local copies, waits for them, and re-layouts  1.01 us (3%)
  starting transfers between devices  0.67 us (2%)
    all_to_all x2, blocking collectives, swap_listed(): lax.all_to_all(chunks, ('lon', 'lat', 'path'), 0, 0, tiled=True, axis_ind...  29.7 us
    pallas_call x5, Pallas kernels, call(): pl.pallas_call(kernel, out_shape=[pltpu.VMEM(shape, dtype) for shape, dty...  5.43 us
    unnamed x15, local copies, waits for them, and re-layouts  1 us
  transfers between devices with their start and end apart: 3, of which 0 were waited for; matrix products, arithmetic and copies ran while one was open for 0% of the time, Pallas kernels for 7%

profile of v9, /device:TPU:0, one launch (start us, length us, event | category | flops | bytes accessed | tf_op | source)
XLA Modules:
  0.0 37.0 jit_solution(13364657752160647429)
XLA Ops:
  0.0 0.0 copy-start.4
  0.0 0.0 copy-start.5
  0.0 0.0 copy-start.6
  0.0 0.5 %collective-permute-start = (bf16[9,192,384]{2,1,0:T(8,128)(2,1)}, bf16[9,192,384]{2,1,0:T(8,128)(2,1)S(1)}, u32[]{:S(2)}, u32[]{:S(2)}) collective-permute-start(bf16[9,192,384]{2,1,0:T(8,128)(2,1)} %param.10), channel_id=1, source_target_pairs={{0,16},{16,0},{1,17},{17,1},{2,18},{18,2},{3,19},{19,3},{4,20},{20... | collective-permute-start | bytes 3981320 | tf_op jit(solution)/shard_map/ppermute | solution.py:362
  0.5 0.1 collective-permute-start.1
  0.6 0.2 row_orders.1
  0.8 0.1 copy-done.4
  0.9 0.1 copy-done.5
  1.0 0.1 copy-done.6
  1.1 0.0 copy-start
  1.1 0.0 copy-start.1
  1.1 0.0 copy-start.2
  1.1 0.0 copy-start.3
  1.1 0.3 pack_classes.1
  1.5 18.8 %all_to_all.10.got = bf16[16,24,384]{2,1,0:T(8,128)(2,1)S(1)} all-to-all(bf16[16,24,384]{2,1,0:T(8,128)(2,1)S(1)} %get-tuple-element.13), channel_id=1, replica_groups={{0,8,12,4,1,9,13,5,2,10,14,6,3,11,15,7},{16,24,28,20,17,25,29,21,18,26,..., dimensions={0} | all-to-all | bytes 589824 | tf_op jit(solution)/shard_map/all_to_all | solution.py:67
  20.3 0.1 collective-permute-start.2
  20.4 0.0 collective-permute-done
  20.4 0.0 collective-permute-done.1
  20.4 0.0 copy-done
  20.4 0.0 copy-done.1
  20.4 0.0 copy-done.2
  20.4 0.0 copy-done.3
  20.5 2.2 %slopes_of_class.1 = (f32[256,384]{1,0:T(8,128)S(1)}, f32[256,384]{1,0:T(8,128)S(1)}) custom-call(bf16[256,256]{1,0:T(8,128)(2,1)S(1)} %get-tuple-element.11.order, bf16[16,24,384]{2,1,0:T(8,128)(2,1)S(1)} %all_to_all.10.got, f32[384]{0:T(512)S(1)} %copy-done.2, f32[384]{0:T(512)S(1)} %copy-done.3, bf16[3,3,192,384]{3,2,1,0:T(8,128)(2,1)S(1)} %bitcast.9, ...), custom_call_target="tpu_custom_call" | custom-call | bytes 5737472 | tf_op jit(solution)/shard_map/slopes_of_class/pallas_call | solution.py:139
  22.6 0.0 collective-permute-done.2.refs_1_
  22.6 2.5 %adjoint_of_class.1 = bf16[256,384]{1,0:T(8,128)(2,1)S(1)} custom-call(bf16[256,256]{1,0:T(8,128)(2,1)S(1)} %get-tuple-element.11.order, f32[256,384]{1,0:T(8,128)S(1)} %get-tuple-element.14.first_slope, f32[256,384]{1,0:T(8,128)S(1)} %get-tuple-element.15.second_slope, bf16[16,8,384]{2,1,0:T(8,128)(2,1)S(1)} %slice.4.refs_0_, ...), custom_call_target="tpu_custom_call" | custom-call | bytes 6422528 | tf_op jit(solution)/shard_map/adjoint_of_class/pallas_call | solution.py:139
  25.2 10.9 %all_to_all.11 = bf16[32,8,384]{2,1,0:T(8,128)(2,1)S(1)} all-to-all(bf16[32,8,384]{2,1,0:T(8,128)(2,1)S(1)} %bitcast.17), channel_id=1, replica_groups={{0,8,12,4,16,24,28,20,1,9,13,5,17,25,29,21,2,10,14,6,18,26,30,22,3,11,1..., dimensions={0} | all-to-all | bytes 393216 | tf_op jit(solution)/shard_map/all_to_all | solution.py:67
  36.1 0.2 attribution_rows.1
  36.3 0.6 %copy.8 = bf16[8,16,384]{2,1,0:T(8,128)(2,1)} copy(bf16[8,16,384]{2,1,0:T(8,128)(2,1)S(1)} %attribution_rows.1) | data formatting | bytes 196608
  (1 shorter events, 0.0 us)
Async XLA Ops:
  0.0 0.9 %copy-start.4 = (bf16[16,16,384]{2,1,0:T(8,128)(2,1)S(1)}, bf16[16,16,384]{2,1,0:T(8,128)(2,1)}, u32[]{:S(2)}) copy-start(bf16[16,16,384]{2,1,0:T(8,128)(2,1)} %param.7) | copy-start | bytes 589828
  0.0 1.0 %copy-start.5 = (bf16[16,16,384]{2,1,0:T(8,128)(2,1)S(1)}, bf16[16,16,384]{2,1,0:T(8,128)(2,1)}, u32[]{:S(2)}) copy-start(bf16[16,16,384]{2,1,0:T(8,128)(2,1)} %param.8) | copy-start | bytes 589828
  0.0 1.1 %copy-start.6 = (bf16[16,16,384]{2,1,0:T(8,128)(2,1)S(1)}, bf16[16,16,384]{2,1,0:T(8,128)(2,1)}, u32[]{:S(2)}) copy-start(bf16[16,16,384]{2,1,0:T(8,128)(2,1)} %param.9) | copy-start | bytes 589828
  0.0 20.4 %collective-permute-start = (bf16[9,192,384]{2,1,0:T(8,128)(2,1)}, bf16[9,192,384]{2,1,0:T(8,128)(2,1)S(1)}, u32[]{:S(2)}, u32[]{:S(2)}) collective-permute-start(bf16[9,192,384]{2,1,0:T(8,128)(2,1)} %param.10), channel_id=1, source_target_pairs={{0,16},{16,0},{1,17},{17,1},{2,18},{18,2},{3,19},{19,3},{4,20},{20... | collective-permute-start | bytes 3981320 | tf_op jit(solution)/shard_map/ppermute | solution.py:362
  0.5 19.9 %collective-permute-start.1 = (bf16[9,192,384]{2,1,0:T(8,128)(2,1)}, bf16[9,192,384]{2,1,0:T(8,128)(2,1)S(1)}, u32[]{:S(2)}, u32[]{:S(2)}) collective-permute-start(bf16[9,192,384]{2,1,0:T(8,128)(2,1)} %param.12), channel_id=1, source_target_pairs={{0,16},{16,0},{1,17},{17,1},{2,18},{18,2},{3,19},{19,3},{4,20},{20... | collective-permute-start | bytes 3981320 | tf_op jit(solution)/shard_map/ppermute | solution.py:362
  1.1 19.3 %copy-start = (bf16[9,192,384]{2,1,0:T(8,128)(2,1)S(1)}, bf16[9,192,384]{2,1,0:T(8,128)(2,1)}, u32[]{:S(2)}) copy-start(bf16[9,192,384]{2,1,0:T(8,128)(2,1)} %param.10) | copy-start | bytes 3981316
  1.1 19.3 %copy-start.1 = (bf16[9,192,384]{2,1,0:T(8,128)(2,1)S(1)}, bf16[9,192,384]{2,1,0:T(8,128)(2,1)}, u32[]{:S(2)}) copy-start(bf16[9,192,384]{2,1,0:T(8,128)(2,1)} %param.12) | copy-start | bytes 3981316
  1.1 19.3 %copy-start.2 = (f32[384]{0:T(512)S(1)}, f32[384]{0:T(512)}, u32[]{:S(2)}) copy-start(f32[384]{0:T(512)} %first_bias.1) | copy-start | bytes 4612
  1.1 19.3 %copy-start.3 = (f32[384]{0:T(512)S(1)}, f32[384]{0:T(512)}, u32[]{:S(2)}) copy-start(f32[384]{0:T(512)} %second_bias.1) | copy-start | bytes 4612
  20.3 2.3 %collective-permute-start.2 = (bf16[16,8,384]{2,1,0:T(8,128)(2,1)S(1)}, bf16[16,8,384]{2,1,0:T(8,128)(2,1)S(1)}, u32[]{:S(2)}, u32[]{:S(2)}) collective-permute-start(bf16[16,8,384]{2,1,0:T(8,128)(2,1)S(1)} %slice.4.refs_0_), channel_id=1, source_target_pairs={{0,16},{16,0},{1,17},{17,1},{2,18},{18,2},{3,19},{19,3},{4,20},{20... | collective-permute-start | bytes 294920 | tf_op jit(solution)/shard_map/ppermute | solution.py:362

commit v10 on v9

--- a/solution.py
+++ b/solution.py
@@ -51,7 +51,7 @@
     slow = group_lon // fast
     bits = slow.bit_length() - 1
     listing = [sum(((i ^ (i >> 1)) >> b & 1) << (bits - 1 - b) for b in range(bits)) for i in range(slow)]
-    return slow, fast, listing
+    return slow, fast, listing[-1:] + listing[:-1]
 
 
 def listed(points):

time: 37.2 us -> 36.3 us (0.976)
  blocking collectives: 29.7 us -> 28.9 us
    all_to_all x2, blocking collectives: 29.7 us -> 28.9 us  [swap_listed(): lax.all_to_all(chunks, ('lon', 'lat', 'path'), 0, 0, tiled=True, axis_ind...]
where the time goes in v10:
time: 36.3 us; the launch traced here: 36.1 us
  blocking collectives  28.9 us (80%)
  Pallas kernels  5.44 us (15%)
  local copies, waits for them, and re-layouts  1.01 us (3%)
  starting transfers between devices  0.67 us (2%)
    all_to_all x2, blocking collectives, swap_listed(): lax.all_to_all(chunks, ('lon', 'lat', 'path'), 0, 0, tiled=True, axis_ind...  28.9 us
    pallas_call x5, Pallas kernels, call(): pl.pallas_call(kernel, out_shape=[pltpu.VMEM(shape, dtype) for shape, dty...  5.44 us
    unnamed x15, local copies, waits for them, and re-layouts  1 us
  transfers between devices with their start and end apart: 3, of which 0 were waited for; matrix products, arithmetic and copies ran while one was open for 0% of the time, Pallas kernels for 7%

profile of v10, /device:TPU:0, one launch (start us, length us, event | category | flops | bytes accessed | tf_op | source)
XLA Modules:
  0.0 36.1 jit_solution(10906440652923987364)
XLA Ops:
  0.0 0.0 copy-start.4
  0.0 0.0 copy-start.5
  0.0 0.0 copy-start.6
  0.0 0.5 %collective-permute-start = (bf16[9,192,384]{2,1,0:T(8,128)(2,1)}, bf16[9,192,384]{2,1,0:T(8,128)(2,1)S(1)}, u32[]{:S(2)}, u32[]{:S(2)}) collective-permute-start(bf16[9,192,384]{2,1,0:T(8,128)(2,1)} %param.10), channel_id=1, source_target_pairs={{0,16},{16,0},{1,17},{17,1},{2,18},{18,2},{3,19},{19,3},{4,20},{20... | collective-permute-start | bytes 3981320 | tf_op jit(solution)/shard_map/ppermute | solution.py:362
  0.5 0.1 collective-permute-start.1
  0.6 0.2 row_orders.1
  0.8 0.1 copy-done.4
  0.9 0.1 copy-done.5
  1.0 0.1 copy-done.6
  1.1 0.0 copy-start
  1.1 0.0 copy-start.1
  1.1 0.0 copy-start.2
  1.1 0.0 copy-start.3
  1.1 0.3 pack_classes.1
  1.5 17.9 %all_to_all.10.got = bf16[16,24,384]{2,1,0:T(8,128)(2,1)S(1)} all-to-all(bf16[16,24,384]{2,1,0:T(8,128)(2,1)S(1)} %get-tuple-element.13), channel_id=1, replica_groups={{4,0,8,12,5,1,9,13,6,2,10,14,7,3,11,15},{20,16,24,28,21,17,25,29,22,18,..., dimensions={0} | all-to-all | bytes 589824 | tf_op jit(solution)/shard_map/all_to_all | solution.py:67
  19.4 0.1 collective-permute-start.2
  19.5 0.0 collective-permute-done
  19.5 0.0 collective-permute-done.1
  19.5 0.0 copy-done
  19.5 0.0 copy-done.1
  19.5 0.0 copy-done.2
  19.5 0.0 copy-done.3
  19.6 2.2 %slopes_of_class.1 = (f32[256,384]{1,0:T(8,128)S(1)}, f32[256,384]{1,0:T(8,128)S(1)}) custom-call(bf16[256,256]{1,0:T(8,128)(2,1)S(1)} %get-tuple-element.11.order, bf16[16,24,384]{2,1,0:T(8,128)(2,1)S(1)} %all_to_all.10.got, f32[384]{0:T(512)S(1)} %copy-done.2, f32[384]{0:T(512)S(1)} %copy-done.3, bf16[3,3,192,384]{3,2,1,0:T(8,128)(2,1)S(1)} %bitcast.9, ...), custom_call_target="tpu_custom_call" | custom-call | bytes 5737472 | tf_op jit(solution)/shard_map/slopes_of_class/pallas_call | solution.py:139
  21.7 0.0 collective-permute-done.2.refs_1_
  21.8 2.5 %adjoint_of_class.1 = bf16[256,384]{1,0:T(8,128)(2,1)S(1)} custom-call(bf16[256,256]{1,0:T(8,128)(2,1)S(1)} %get-tuple-element.11.order, f32[256,384]{1,0:T(8,128)S(1)} %get-tuple-element.14.first_slope, f32[256,384]{1,0:T(8,128)S(1)} %get-tuple-element.15.second_slope, bf16[16,8,384]{2,1,0:T(8,128)(2,1)S(1)} %slice.4.refs_0_, ...), custom_call_target="tpu_custom_call" | custom-call | bytes 6422528 | tf_op jit(solution)/shard_map/adjoint_of_class/pallas_call | solution.py:139
  24.3 10.9 %all_to_all.11 = bf16[32,8,384]{2,1,0:T(8,128)(2,1)S(1)} all-to-all(bf16[32,8,384]{2,1,0:T(8,128)(2,1)S(1)} %bitcast.17), channel_id=1, replica_groups={{4,0,8,12,20,16,24,28,5,1,9,13,21,17,25,29,6,2,10,14,22,18,26,30,7,3,11..., dimensions={0} | all-to-all | bytes 393216 | tf_op jit(solution)/shard_map/all_to_all | solution.py:67
  35.2 0.2 attribution_rows.1
  35.4 0.6 %copy.8 = bf16[8,16,384]{2,1,0:T(8,128)(2,1)} copy(bf16[8,16,384]{2,1,0:T(8,128)(2,1)S(1)} %attribution_rows.1) | data formatting | bytes 196608
  (1 shorter events, 0.0 us)
Async XLA Ops:
  0.0 0.9 %copy-start.4 = (bf16[16,16,384]{2,1,0:T(8,128)(2,1)S(1)}, bf16[16,16,384]{2,1,0:T(8,128)(2,1)}, u32[]{:S(2)}) copy-start(bf16[16,16,384]{2,1,0:T(8,128)(2,1)} %param.7) | copy-start | bytes 589828
  0.0 1.0 %copy-start.5 = (bf16[16,16,384]{2,1,0:T(8,128)(2,1)S(1)}, bf16[16,16,384]{2,1,0:T(8,128)(2,1)}, u32[]{:S(2)}) copy-start(bf16[16,16,384]{2,1,0:T(8,128)(2,1)} %param.8) | copy-start | bytes 589828
  0.0 1.1 %copy-start.6 = (bf16[16,16,384]{2,1,0:T(8,128)(2,1)S(1)}, bf16[16,16,384]{2,1,0:T(8,128)(2,1)}, u32[]{:S(2)}) copy-start(bf16[16,16,384]{2,1,0:T(8,128)(2,1)} %param.9) | copy-start | bytes 589828
  0.0 19.5 %collective-permute-start = (bf16[9,192,384]{2,1,0:T(8,128)(2,1)}, bf16[9,192,384]{2,1,0:T(8,128)(2,1)S(1)}, u32[]{:S(2)}, u32[]{:S(2)}) collective-permute-start(bf16[9,192,384]{2,1,0:T(8,128)(2,1)} %param.10), channel_id=1, source_target_pairs={{0,16},{16,0},{1,17},{17,1},{2,18},{18,2},{3,19},{19,3},{4,20},{20... | collective-permute-start | bytes 3981320 | tf_op jit(solution)/shard_map/ppermute | solution.py:362
  0.5 19.0 %collective-permute-start.1 = (bf16[9,192,384]{2,1,0:T(8,128)(2,1)}, bf16[9,192,384]{2,1,0:T(8,128)(2,1)S(1)}, u32[]{:S(2)}, u32[]{:S(2)}) collective-permute-start(bf16[9,192,384]{2,1,0:T(8,128)(2,1)} %param.12), channel_id=1, source_target_pairs={{0,16},{16,0},{1,17},{17,1},{2,18},{18,2},{3,19},{19,3},{4,20},{20... | collective-permute-start | bytes 3981320 | tf_op jit(solution)/shard_map/ppermute | solution.py:362
  1.1 18.4 %copy-start = (bf16[9,192,384]{2,1,0:T(8,128)(2,1)S(1)}, bf16[9,192,384]{2,1,0:T(8,128)(2,1)}, u32[]{:S(2)}) copy-start(bf16[9,192,384]{2,1,0:T(8,128)(2,1)} %param.10) | copy-start | bytes 3981316
  1.1 18.4 %copy-start.1 = (bf16[9,192,384]{2,1,0:T(8,128)(2,1)S(1)}, bf16[9,192,384]{2,1,0:T(8,128)(2,1)}, u32[]{:S(2)}) copy-start(bf16[9,192,384]{2,1,0:T(8,128)(2,1)} %param.12) | copy-start | bytes 3981316
  1.1 18.4 %copy-start.2 = (f32[384]{0:T(512)S(1)}, f32[384]{0:T(512)}, u32[]{:S(2)}) copy-start(f32[384]{0:T(512)} %first_bias.1) | copy-start | bytes 4612
  1.1 18.4 %copy-start.3 = (f32[384]{0:T(512)S(1)}, f32[384]{0:T(512)}, u32[]{:S(2)}) copy-start(f32[384]{0:T(512)} %second_bias.1) | copy-start | bytes 4612
  19.4 2.3 %collective-permute-start.2 = (bf16[16,8,384]{2,1,0:T(8,128)(2,1)S(1)}, bf16[16,8,384]{2,1,0:T(8,128)(2,1)S(1)}, u32[]{:S(2)}, u32[]{:S(2)}) collective-permute-start(bf16[16,8,384]{2,1,0:T(8,128)(2,1)S(1)} %slice.4.refs_0_), channel_id=1, source_target_pairs={{0,16},{16,0},{1,17},{17,1},{2,18},{18,2},{3,19},{19,3},{4,20},{20... | collective-permute-start | bytes 294920 | tf_op jit(solution)/shard_map/ppermute | solution.py:362

commit v11 on v10

--- a/solution.py
+++ b/solution.py
@@ -303,18 +303,31 @@
 
         def run(place, cotangent, first, second):
             spread, _, transposed_part = class_tools(sizes, depth, edged)
+            def near_part(at, end):
+                sides = [near_taps[j * rows : j * rows + cells, :] for j in range(3)]
+                blocks = [
+                    jnp.concatenate([part[2 - i, 2 - j] for part in first], axis=0)[at:end]
+                    for j in range(3)
+                    for i in range(3)
+                ]
+                dims = (((1,), (1,)), ((), ()))
+                joint, weights = jnp.concatenate(sides, axis=1), jnp.concatenate(blocks, axis=1)
+                return lax.dot_general(joint, weights, dims, preferred_element_type=F32)
+
+            near_taps[:rows, :] = jnp.zeros((rows, 3 * depth), BF16)
+            near_taps[rows + cells :, :] = jnp.zeros((rows, 3 * depth), BF16)
             upstream = jnp.concatenate([share[...].astype(F32) for share in cotangent], axis=1)
             upstream = jnp.dot(order[...], upstream.reshape(cells, depth).astype(BF16), preferred_element_type=F32)
             spread(second_slope[...] * upstream, FAR // NEAR, 0, far_taps)
             for at, end in channel_parts(depth):
                 hidden_adj = upstream[:, at:end] + transposed_part(far_taps, second, FAR // NEAR, at, end)
                 grad[:, at:end] = hidden_adj
-                spread(first_slope[:, at:end] * hidden_adj, 1, at, near_taps)
+                spread(first_slope[:, at:end] * hidden_adj, 1, at, near_taps.at[rows : rows + cells])
             slow, fast, listing = lon_parts()
             dims = (group_lat, col_part, slow, fast, points, row_part // points)
             home = ordering(dims, (3, 0, 4, 2, 5, 1), (2, listing))
             for at, end in channel_parts(depth):
-                grad[:, at:end] += transposed_part(near_taps, first, 1, at, end)
+                grad[:, at:end] += near_part(at, end)
             sent[...] = jnp.dot(home, grad[...].astype(BF16), preferred_element_type=F32).astype(BF16)
 
         by_place(points, run, refs[:points], refs[points : 2 * points], refs[2 * points : 3 * points])
@@ -323,7 +336,7 @@
         kernel,
         [((cells, depth), BF16)],
         [pltpu.VMEM((cols, rows + 2 * EDGE, depth), F32)]
-        + [pltpu.VMEM((cells, 3 * depth), BF16)] * 2
+        + [pltpu.VMEM((cells + 2 * rows, 3 * depth), BF16), pltpu.VMEM((cells, 3 * depth), BF16)]
         + [pltpu.VMEM((cells, depth), F32)],
         "adjoint_of_class",
         16,

time: 36.3 us -> 36.2 us (level)
  no operation moved by 1% of the time
where the time goes in v11:
time: 36.2 us; the launch traced here: 36.1 us
  blocking collectives  28.9 us (80%)
  Pallas kernels  5.4 us (15%)
  local copies, waits for them, and re-layouts  1.01 us (3%)
  starting transfers between devices  0.67 us (2%)
    all_to_all x2, blocking collectives, swap_listed(): lax.all_to_all(chunks, ('lon', 'lat', 'path'), 0, 0, tiled=True, axis_ind...  28.9 us
    pallas_call x5, Pallas kernels, call(): pl.pallas_call(kernel, out_shape=[pltpu.VMEM(shape, dtype) for shape, dty...  5.4 us
    unnamed x15, local copies, waits for them, and re-layouts  1 us
  transfers between devices with their start and end apart: 3, of which 0 were waited for; matrix products, arithmetic and copies ran while one was open for 0% of the time, Pallas kernels for 7%

profile of v11, /device:TPU:0, one launch (start us, length us, event | category | flops | bytes accessed | tf_op | source)
XLA Modules:
  0.0 36.1 jit_solution(8352452040893622446)
XLA Ops:
  0.0 0.0 copy-start.4
  0.0 0.0 copy-start.5
  0.0 0.0 copy-start.6
  0.0 0.5 %collective-permute-start = (bf16[9,192,384]{2,1,0:T(8,128)(2,1)}, bf16[9,192,384]{2,1,0:T(8,128)(2,1)S(1)}, u32[]{:S(2)}, u32[]{:S(2)}) collective-permute-start(bf16[9,192,384]{2,1,0:T(8,128)(2,1)} %param.10), channel_id=1, source_target_pairs={{0,16},{16,0},{1,17},{17,1},{2,18},{18,2},{3,19},{19,3},{4,20},{20... | collective-permute-start | bytes 3981320 | tf_op jit(solution)/shard_map/ppermute | solution.py:375
  0.5 0.1 collective-permute-start.1
  0.6 0.2 row_orders.1
  0.8 0.1 copy-done.4
  0.9 0.1 copy-done.5
  1.0 0.1 copy-done.6
  1.1 0.0 copy-start
  1.1 0.0 copy-start.1
  1.1 0.0 copy-start.2
  1.1 0.0 copy-start.3
  1.1 0.3 pack_classes.1
  1.5 17.9 %all_to_all.10.got = bf16[16,24,384]{2,1,0:T(8,128)(2,1)S(1)} all-to-all(bf16[16,24,384]{2,1,0:T(8,128)(2,1)S(1)} %get-tuple-element.13), channel_id=1, replica_groups={{4,0,8,12,5,1,9,13,6,2,10,14,7,3,11,15},{20,16,24,28,21,17,25,29,22,18,..., dimensions={0} | all-to-all | bytes 589824 | tf_op jit(solution)/shard_map/all_to_all | solution.py:67
  19.4 0.1 collective-permute-start.2
  19.5 0.0 collective-permute-done
  19.5 0.0 collective-permute-done.1
  19.5 0.0 copy-done
  19.5 0.0 copy-done.1
  19.5 0.0 copy-done.2
  19.5 0.0 copy-done.3
  19.6 2.2 %slopes_of_class.1 = (f32[256,384]{1,0:T(8,128)S(1)}, f32[256,384]{1,0:T(8,128)S(1)}) custom-call(bf16[256,256]{1,0:T(8,128)(2,1)S(1)} %get-tuple-element.11.order, bf16[16,24,384]{2,1,0:T(8,128)(2,1)S(1)} %all_to_all.10.got, f32[384]{0:T(512)S(1)} %copy-done.2, f32[384]{0:T(512)S(1)} %copy-done.3, bf16[3,3,192,384]{3,2,1,0:T(8,128)(2,1)S(1)} %bitcast.9, ...), custom_call_target="tpu_custom_call" | custom-call | bytes 5737472 | tf_op jit(solution)/shard_map/slopes_of_class/pallas_call | solution.py:139
  21.7 0.0 collective-permute-done.2.refs_1_
  21.8 2.5 %adjoint_of_class.1 = bf16[256,384]{1,0:T(8,128)(2,1)S(1)} custom-call(bf16[256,256]{1,0:T(8,128)(2,1)S(1)} %get-tuple-element.11.order, f32[256,384]{1,0:T(8,128)S(1)} %get-tuple-element.14.first_slope, f32[256,384]{1,0:T(8,128)S(1)} %get-tuple-element.15.second_slope, bf16[16,8,384]{2,1,0:T(8,128)(2,1)S(1)} %slice.4.refs_0_, ...), custom_call_target="tpu_custom_call" | custom-call | bytes 6422528 | tf_op jit(solution)/shard_map/adjoint_of_class/pallas_call | solution.py:139
  24.3 10.9 %all_to_all.11 = bf16[32,8,384]{2,1,0:T(8,128)(2,1)S(1)} all-to-all(bf16[32,8,384]{2,1,0:T(8,128)(2,1)S(1)} %bitcast.17), channel_id=1, replica_groups={{4,0,8,12,20,16,24,28,5,1,9,13,21,17,25,29,6,2,10,14,22,18,26,30,7,3,11..., dimensions={0} | all-to-all | bytes 393216 | tf_op jit(solution)/shard_map/all_to_all | solution.py:67
  35.2 0.2 attribution_rows.1
  35.4 0.6 %copy.8 = bf16[8,16,384]{2,1,0:T(8,128)(2,1)} copy(bf16[8,16,384]{2,1,0:T(8,128)(2,1)S(1)} %attribution_rows.1) | data formatting | bytes 196608
  (1 shorter events, 0.0 us)
Async XLA Ops:
  0.0 0.9 %copy-start.4 = (bf16[16,16,384]{2,1,0:T(8,128)(2,1)S(1)}, bf16[16,16,384]{2,1,0:T(8,128)(2,1)}, u32[]{:S(2)}) copy-start(bf16[16,16,384]{2,1,0:T(8,128)(2,1)} %param.7) | copy-start | bytes 589828
  0.0 1.0 %copy-start.5 = (bf16[16,16,384]{2,1,0:T(8,128)(2,1)S(1)}, bf16[16,16,384]{2,1,0:T(8,128)(2,1)}, u32[]{:S(2)}) copy-start(bf16[16,16,384]{2,1,0:T(8,128)(2,1)} %param.8) | copy-start | bytes 589828
  0.0 1.1 %copy-start.6 = (bf16[16,16,384]{2,1,0:T(8,128)(2,1)S(1)}, bf16[16,16,384]{2,1,0:T(8,128)(2,1)}, u32[]{:S(2)}) copy-start(bf16[16,16,384]{2,1,0:T(8,128)(2,1)} %param.9) | copy-start | bytes 589828
  0.0 19.5 %collective-permute-start = (bf16[9,192,384]{2,1,0:T(8,128)(2,1)}, bf16[9,192,384]{2,1,0:T(8,128)(2,1)S(1)}, u32[]{:S(2)}, u32[]{:S(2)}) collective-permute-start(bf16[9,192,384]{2,1,0:T(8,128)(2,1)} %param.10), channel_id=1, source_target_pairs={{0,16},{16,0},{1,17},{17,1},{2,18},{18,2},{3,19},{19,3},{4,20},{20... | collective-permute-start | bytes 3981320 | tf_op jit(solution)/shard_map/ppermute | solution.py:375
  0.5 19.0 %collective-permute-start.1 = (bf16[9,192,384]{2,1,0:T(8,128)(2,1)}, bf16[9,192,384]{2,1,0:T(8,128)(2,1)S(1)}, u32[]{:S(2)}, u32[]{:S(2)}) collective-permute-start(bf16[9,192,384]{2,1,0:T(8,128)(2,1)} %param.12), channel_id=1, source_target_pairs={{0,16},{16,0},{1,17},{17,1},{2,18},{18,2},{3,19},{19,3},{4,20},{20... | collective-permute-start | bytes 3981320 | tf_op jit(solution)/shard_map/ppermute | solution.py:375
  1.1 18.4 %copy-start = (bf16[9,192,384]{2,1,0:T(8,128)(2,1)S(1)}, bf16[9,192,384]{2,1,0:T(8,128)(2,1)}, u32[]{:S(2)}) copy-start(bf16[9,192,384]{2,1,0:T(8,128)(2,1)} %param.10) | copy-start | bytes 3981316
  1.1 18.4 %copy-start.1 = (bf16[9,192,384]{2,1,0:T(8,128)(2,1)S(1)}, bf16[9,192,384]{2,1,0:T(8,128)(2,1)}, u32[]{:S(2)}) copy-start(bf16[9,192,384]{2,1,0:T(8,128)(2,1)} %param.12) | copy-start | bytes 3981316
  1.1 18.4 %copy-start.2 = (f32[384]{0:T(512)S(1)}, f32[384]{0:T(512)}, u32[]{:S(2)}) copy-start(f32[384]{0:T(512)} %first_bias.1) | copy-start | bytes 4612
  1.1 18.4 %copy-start.3 = (f32[384]{0:T(512)S(1)}, f32[384]{0:T(512)}, u32[]{:S(2)}) copy-start(f32[384]{0:T(512)} %second_bias.1) | copy-start | bytes 4612
  19.4 2.3 %collective-permute-start.2 = (bf16[16,8,384]{2,1,0:T(8,128)(2,1)S(1)}, bf16[16,8,384]{2,1,0:T(8,128)(2,1)S(1)}, u32[]{:S(2)}, u32[]{:S(2)}) collective-permute-start(bf16[16,8,384]{2,1,0:T(8,128)(2,1)S(1)} %slice.4.refs_0_), channel_id=1, source_target_pairs={{0,16},{16,0},{1,17},{17,1},{2,18},{18,2},{3,19},{19,3},{4,20},{20... | collective-permute-start | bytes 294920 | tf_op jit(solution)/shard_map/ppermute | solution.py:375

commit v12 on v11

--- a/solution.py
+++ b/solution.py
@@ -353,17 +353,34 @@
     points, depth = lax.axis_size("path"), home.shape[-1]
     cells, group_lat = rows * cols, group_sizes()[1]
 
-    def kernel(home, diff_rows, out):
+    def kernel(home, diff_rows, out, held, sems):
         bits, ahead = (NEAR * NEAR).bit_length() - 1, (group_lat * lon_parts()[1]).bit_length() - 1
         of_class = tuple(i + (i >= ahead) for i in range(bits))
         dims = (2,) * ahead + (points,) + (2,) * (bits - ahead) + (rows // NEAR, cols // NEAR)
         row_bits, col_bits = of_class[: bits // 2], of_class[bits // 2 :]
         order = ordering(dims, (ahead, bits + 1) + row_bits + (bits + 2,) + col_bits)
         order = sum(order[k * cells : (k + 1) * cells] for k in range(points))
-        moved = jnp.dot(order, home[...], preferred_element_type=F32)
-        out[...] = (diff_rows[...] * moved).reshape(rows, cols, depth).astype(BF16)
-
-    return call(kernel, [((rows, cols, depth), BF16)], [], "attribution_rows", 4, home, diff_rows)[0]
+        copies = []
+        for i in range(2):
+            span = slice(i * cells // 2, (i + 1) * cells // 2)
+            moved = jnp.dot(order[span], home[...], preferred_element_type=F32)
+            place = pl.ds(i * rows // 2, rows // 2)
+            held[place] = (diff_rows[span, :] * moved).reshape(rows // 2, cols, depth).astype(BF16)
+            copies.append(pltpu.make_async_copy(held.at[place], out.at[place], sems.at[i]))
+            copies[-1].start()
+        for copy in copies:
+            copy.wait()
+
+    args = [pltpu.with_memory_space_constraint(x, pltpu.VMEM) for x in (home, diff_rows)]
+    return pl.pallas_call(
+        kernel,
+        out_shape=pltpu.HBM((rows, cols, depth), BF16),
+        in_specs=[VMEM] * 2,
+        out_specs=pl.BlockSpec(memory_space=pltpu.HBM),
+        scratch_shapes=[pltpu.VMEM((rows, cols, depth), BF16), pltpu.SemaphoreType.DMA((2,))],
+        compiler_params=pltpu.CompilerParams(vmem_limit_bytes=4 << 20),
+        name="attribution_rows",
+    )(*args)
 
 
 def one_group(observed, baseline, cotangent, first_weight, first_bias, second_weight, second_bias):

time: 36.2 us -> 36.2 us (level)
  local copies, waits for them, and re-layouts: 1.01 us -> 0.36 us
  Pallas kernels: 5.4 us -> 6.05 us
    pallas_call x0 -> x1, Pallas kernels: none -> 0.88 us  [attribution_rows(): pl.pallas_call(kernel, out_shape=pltpu.HBM((rows, cols, depth), BF16), in...]
    unnamed x15 -> x14, local copies, waits for them, and re-layouts: 1 us -> 0.35 us
    pallas_call x5 -> x4, Pallas kernels: 5.4 us -> 5.18 us  [call(): pl.pallas_call(kernel, out_shape=[pltpu.VMEM(shape, dtype) for shape, dty...]
where the time goes in v12:
time: 36.2 us; the launch traced here: 36.1 us
  blocking collectives  28.9 us (80%)
  Pallas kernels  6.05 us (17%)
  starting transfers between devices  0.67 us (2%)
    all_to_all x2, blocking collectives, swap_listed(): lax.all_to_all(chunks, ('lon', 'lat', 'path'), 0, 0, tiled=True, axis_ind...  28.9 us
    pallas_call x4, Pallas kernels, call(): pl.pallas_call(kernel, out_shape=[pltpu.VMEM(shape, dtype) for shape, dty...  5.18 us
    pallas_call x1, Pallas kernels, attribution_rows(): pl.pallas_call(kernel, out_shape=pltpu.HBM((rows, cols, depth), BF16), in...  0.88 us
  transfers between devices with their start and end apart: 3, of which 0 were waited for; matrix products, arithmetic and copies ran while one was open for 0% of the time, Pallas kernels for 7%

profile of v12, /device:TPU:0, one launch (start us, length us, event | category | flops | bytes accessed | tf_op | source)
XLA Modules:
  0.0 36.1 jit_solution(9355461549225953164)
XLA Ops:
  0.0 0.0 copy-start.4
  0.0 0.0 copy-start.5
  0.0 0.0 copy-start.6
  0.0 0.5 %collective-permute-start = (bf16[9,192,384]{2,1,0:T(8,128)(2,1)}, bf16[9,192,384]{2,1,0:T(8,128)(2,1)S(1)}, u32[]{:S(2)}, u32[]{:S(2)}) collective-permute-start(bf16[9,192,384]{2,1,0:T(8,128)(2,1)} %param.10), channel_id=1, source_target_pairs={{0,16},{16,0},{1,17},{17,1},{2,18},{18,2},{3,19},{19,3},{4,20},{20... | collective-permute-start | bytes 3981320 | tf_op jit(solution)/shard_map/ppermute | solution.py:392
  0.5 0.1 collective-permute-start.1
  0.6 0.2 row_orders.1
  0.8 0.1 copy-done.4
  0.9 0.1 copy-done.5
  1.0 0.1 copy-done.6
  1.1 0.0 copy-start
  1.1 0.0 copy-start.1
  1.1 0.0 copy-start.2
  1.1 0.0 copy-start.3
  1.1 0.3 pack_classes.1
  1.5 17.9 %all_to_all.10.got = bf16[16,24,384]{2,1,0:T(8,128)(2,1)S(1)} all-to-all(bf16[16,24,384]{2,1,0:T(8,128)(2,1)S(1)} %get-tuple-element.13), channel_id=1, replica_groups={{4,0,8,12,5,1,9,13,6,2,10,14,7,3,11,15},{20,16,24,28,21,17,25,29,22,18,..., dimensions={0} | all-to-all | bytes 589824 | tf_op jit(solution)/shard_map/all_to_all | solution.py:67
  19.4 0.1 collective-permute-start.2
  19.5 0.0 collective-permute-done
  19.5 0.0 collective-permute-done.1
  19.5 0.0 copy-done
  19.5 0.0 copy-done.1
  19.5 0.0 copy-done.2
  19.5 0.0 copy-done.3
  19.6 2.2 %slopes_of_class.1 = (f32[256,384]{1,0:T(8,128)S(1)}, f32[256,384]{1,0:T(8,128)S(1)}) custom-call(bf16[256,256]{1,0:T(8,128)(2,1)S(1)} %get-tuple-element.11.order, bf16[16,24,384]{2,1,0:T(8,128)(2,1)S(1)} %all_to_all.10.got, f32[384]{0:T(512)S(1)} %copy-done.2, f32[384]{0:T(512)S(1)} %copy-done.3, bf16[3,3,192,384]{3,2,1,0:T(8,128)(2,1)S(1)} %bitcast.9, ...), custom_call_target="tpu_custom_call" | custom-call | bytes 5737472 | tf_op jit(solution)/shard_map/slopes_of_class/pallas_call | solution.py:139
  21.7 0.0 collective-permute-done.2.refs_1_
  21.8 2.5 %adjoint_of_class.1 = bf16[256,384]{1,0:T(8,128)(2,1)S(1)} custom-call(bf16[256,256]{1,0:T(8,128)(2,1)S(1)} %get-tuple-element.11.order, f32[256,384]{1,0:T(8,128)S(1)} %get-tuple-element.14.first_slope, f32[256,384]{1,0:T(8,128)S(1)} %get-tuple-element.15.second_slope, bf16[16,8,384]{2,1,0:T(8,128)(2,1)S(1)} %slice.4.refs_0_, ...), custom_call_target="tpu_custom_call" | custom-call | bytes 6422528 | tf_op jit(solution)/shard_map/adjoint_of_class/pallas_call | solution.py:139
  24.3 10.9 %all_to_all.11 = bf16[32,8,384]{2,1,0:T(8,128)(2,1)S(1)} all-to-all(bf16[32,8,384]{2,1,0:T(8,128)(2,1)S(1)} %bitcast.17), channel_id=1, replica_groups={{4,0,8,12,20,16,24,28,5,1,9,13,21,17,25,29,6,2,10,14,22,18,26,30,7,3,11..., dimensions={0} | all-to-all | bytes 393216 | tf_op jit(solution)/shard_map/all_to_all | solution.py:67
  35.2 0.9 %attribution_rows.1 = bf16[8,16,384]{2,1,0:T(8,128)(2,1)} custom-call(bf16[256,384]{1,0:T(8,128)(2,1)S(1)} %bitcast.18, f32[128,384]{1,0:T(8,128)S(1)} %get-tuple-element.16.diff_rows), custom_call_target="tpu_custom_call" | custom-call | tf_op jit(solution)/shard_map/attribution_rows/pallas_call | solution.py:375
  (1 shorter events, 0.0 us)
Async XLA Ops:
  0.0 0.9 %copy-start.4 = (bf16[16,16,384]{2,1,0:T(8,128)(2,1)S(1)}, bf16[16,16,384]{2,1,0:T(8,128)(2,1)}, u32[]{:S(2)}) copy-start(bf16[16,16,384]{2,1,0:T(8,128)(2,1)} %param.7) | copy-start | bytes 589828
  0.0 1.0 %copy-start.5 = (bf16[16,16,384]{2,1,0:T(8,128)(2,1)S(1)}, bf16[16,16,384]{2,1,0:T(8,128)(2,1)}, u32[]{:S(2)}) copy-start(bf16[16,16,384]{2,1,0:T(8,128)(2,1)} %param.8) | copy-start | bytes 589828
  0.0 1.1 %copy-start.6 = (bf16[16,16,384]{2,1,0:T(8,128)(2,1)S(1)}, bf16[16,16,384]{2,1,0:T(8,128)(2,1)}, u32[]{:S(2)}) copy-start(bf16[16,16,384]{2,1,0:T(8,128)(2,1)} %param.9) | copy-start | bytes 589828
  0.0 19.5 %collective-permute-start = (bf16[9,192,384]{2,1,0:T(8,128)(2,1)}, bf16[9,192,384]{2,1,0:T(8,128)(2,1)S(1)}, u32[]{:S(2)}, u32[]{:S(2)}) collective-permute-start(bf16[9,192,384]{2,1,0:T(8,128)(2,1)} %param.10), channel_id=1, source_target_pairs={{0,16},{16,0},{1,17},{17,1},{2,18},{18,2},{3,19},{19,3},{4,20},{20... | collective-permute-start | bytes 3981320 | tf_op jit(solution)/shard_map/ppermute | solution.py:392
  0.5 19.0 %collective-permute-start.1 = (bf16[9,192,384]{2,1,0:T(8,128)(2,1)}, bf16[9,192,384]{2,1,0:T(8,128)(2,1)S(1)}, u32[]{:S(2)}, u32[]{:S(2)}) collective-permute-start(bf16[9,192,384]{2,1,0:T(8,128)(2,1)} %param.12), channel_id=1, source_target_pairs={{0,16},{16,0},{1,17},{17,1},{2,18},{18,2},{3,19},{19,3},{4,20},{20... | collective-permute-start | bytes 3981320 | tf_op jit(solution)/shard_map/ppermute | solution.py:392
  1.1 18.4 %copy-start = (bf16[9,192,384]{2,1,0:T(8,128)(2,1)S(1)}, bf16[9,192,384]{2,1,0:T(8,128)(2,1)}, u32[]{:S(2)}) copy-start(bf16[9,192,384]{2,1,0:T(8,128)(2,1)} %param.10) | copy-start | bytes 3981316
  1.1 18.4 %copy-start.1 = (bf16[9,192,384]{2,1,0:T(8,128)(2,1)S(1)}, bf16[9,192,384]{2,1,0:T(8,128)(2,1)}, u32[]{:S(2)}) copy-start(bf16[9,192,384]{2,1,0:T(8,128)(2,1)} %param.12) | copy-start | bytes 3981316
  1.1 18.4 %copy-start.2 = (f32[384]{0:T(512)S(1)}, f32[384]{0:T(512)}, u32[]{:S(2)}) copy-start(f32[384]{0:T(512)} %first_bias.1) | copy-start | bytes 4612
  1.1 18.4 %copy-start.3 = (f32[384]{0:T(512)S(1)}, f32[384]{0:T(512)}, u32[]{:S(2)}) copy-start(f32[384]{0:T(512)} %second_bias.1) | copy-start | bytes 4612
  19.4 2.3 %collective-permute-start.2 = (bf16[16,8,384]{2,1,0:T(8,128)(2,1)S(1)}, bf16[16,8,384]{2,1,0:T(8,128)(2,1)S(1)}, u32[]{:S(2)}, u32[]{:S(2)}) collective-permute-start(bf16[16,8,384]{2,1,0:T(8,128)(2,1)S(1)} %slice.4.refs_0_), channel_id=1, source_target_pairs={{0,16},{16,0},{1,17},{17,1},{2,18},{18,2},{3,19},{19,3},{4,20},{20... | collective-permute-start | bytes 294920 | tf_op jit(solution)/shard_map/ppermute | solution.py:392
